TPU v7x, 32 devices: a whole 2x2x4 slice. The times are simulated.
32 devices in a mesh: slab: 2 (over x), space: 8 (over z, y), elec: 2 (over core).
Axes of the slice: x: 2, y: 2, z: 4, core: 2. Of those that a mesh axis runs over, the one named last changes fastest.
Arguments:
- potentials: bfloat16 [1024, 32, 1024], P('elec', ('slab', 'space')), parts along dimension 1, may hold values from -6 to 6
- elec_order: int32 [1024], replicated, may hold values from 0 to 1023, each once
- quadripoles: int32 [1024, 4], replicated, may hold values from 0 to 1023, all different within a row
- weighted_misfit: bfloat16 [2048], P('slab'), parts along dimension 0, may hold values from -6 to 6
- salinity: float32 [32, 1024], P(('slab', 'space')), parts along dimension 0, may hold values from 1 to 35
- water_content: float32 [32, 1024], P(('slab', 'space')), parts along dimension 0, may hold values from 0.15 to 0.45
- cementation: float32 [32, 1024], P(('slab', 'space')), parts along dimension 0, may hold values from 1.3 to 2.5
- anisotropy: float32 [3, 32, 1024], P(None, ('slab', 'space')), parts along dimension 1, may hold values from 0.1 to 1.9
Outputs:
- grad_salt: float32 [32, 1024], P(('slab', 'space')), parts along dimension 0
- grad_water: float32 [32, 1024], P(('slab', 'space')), parts along dimension 0
There are 2 independent parts, one for each index of `slab`. A program takes and returns all parts, laid end to end along the dimension named above; an argument that names none is the same for every part. Nothing has to cross between parts.
Inputs may be any that keep to these rules, and one draw needn't show every extreme that they name: `elec_order`: a permutation of the electrodes. `quadripoles`: the four electrodes of a measurement differ; every electrode takes part in some measurement.
All inputs are finite; a program needn't handle non-finite values.
Results may differ from a plain program's by a relative error of at most 0.0045.
Values may be sent and summed in bfloat16 or wider, within the bound.
No kernel may reach another device: no remote copies, remote signals or barrier semaphores. Data moves between devices by JAX's collectives and lax.ppermute only.
A program may use at most 64 MiB of HBM per device.

v0:
```python
import jax
import jax.numpy as jnp
from jax import lax
from jax.sharding import PartitionSpec as P

NX = 32
NY = 32


def partner(value, axis, apart):
    mask = 2**apart
    pairs = [(source, source ^ mask) for source in range(lax.axis_size(axis))]
    return lax.ppermute(value, axis, pairs)


def with_halo(array, sides, width):
    for axis, dim in sides:
        size, length = (lax.axis_size(axis), array.shape[dim])
        up = [(i, (i + 1) % size) for i in range(size - 1)]
        down = [(j, i) for i, j in up]
        last = lax.slice_in_dim(array, length - width, length, axis=dim)
        leading = lax.slice_in_dim(array, 0, width, axis=dim)
        before = lax.ppermute(last, axis, up)
        after = lax.ppermute(leading, axis, down)
        array = jnp.concatenate([before, array, after], axis=dim)
    return array


def assemble_rows(quadripoles, weighted_misfit, row_electrodes, elec_order):
    first = quadripoles[:, 0][None, :] == row_electrodes[:, None]
    second = quadripoles[:, 1][None, :] == row_electrodes[:, None]
    left_side = first.astype(jnp.bfloat16) - second.astype(jnp.bfloat16)
    third = quadripoles[:, 2][:, None] == elec_order[None, :]
    fourth = quadripoles[:, 3][:, None] == elec_order[None, :]
    signed = third.astype(jnp.float32) - fourth.astype(jnp.float32)
    right_side = (weighted_misfit.astype(jnp.float32)[:, None] * signed).astype(jnp.bfloat16)
    return jnp.dot(left_side, right_side, preferred_element_type=jnp.float32).astype(jnp.bfloat16)


def half_difference(upper, lower):
    return (0.5 * (upper.astype(jnp.float32) - lower.astype(jnp.float32))).astype(jnp.bfloat16)


def layer_gradients(extended):
    rows_n = extended.shape[0]
    layers = extended.shape[1] - 2
    field = extended.reshape(rows_n, layers + 2, NY, NX)
    along_z = half_difference(field[:, 2:], field[:, :-2])
    middle = field[:, 1:-1]
    pad_y = jnp.pad(middle, ((0, 0), (0, 0), (1, 1), (0, 0)))
    along_y = half_difference(pad_y[:, :, 2:], pad_y[:, :, :-2])
    pad_x = jnp.pad(middle, ((0, 0), (0, 0), (0, 0), (1, 1)))
    along_x = half_difference(pad_x[:, :, :, 2:], pad_x[:, :, :, :-2])
    return [along_z.reshape(rows_n, -1), along_y.reshape(rows_n, -1), along_x.reshape(rows_n, -1)]


def archie_chain(sensitivity, salt_v, water_volume, cement_v):
    return (sensitivity / salt_v, cement_v * sensitivity / water_volume)


def local(
    potentials,
    elec_order,
    quadripoles,
    weighted_misfit,
    salinity,
    water_content,
    cementation,
    anisotropy,
):
    group_index = lax.axis_index("elec")
    group_rows = potentials.shape[0]
    layers = potentials.shape[1]
    foreign_group = partner(potentials, "elec", 0)
    paired = jnp.concatenate([potentials, foreign_group], axis=0)
    widened = with_halo(paired, (("space", 1),), 1)
    own_extended = widened[:group_rows]
    other_extended = widened[group_rows:]
    other_index = 1 - group_index
    row_electrodes = lax.dynamic_slice_in_dim(elec_order, group_index * group_rows, group_rows, 0)
    own_weights = assemble_rows(quadripoles, weighted_misfit, row_electrodes, elec_order)
    weights_self = lax.dynamic_slice_in_dim(own_weights, group_index * group_rows, group_rows, 1)
    weights_cross = lax.dynamic_slice_in_dim(own_weights, other_index * group_rows, group_rows, 1)
    own_grads = layer_gradients(own_extended)
    other_grads = layer_gradients(other_extended)
    salt_flat = salinity.reshape(-1)
    water_flat = water_content.reshape(-1)
    cement_flat = cementation.reshape(-1)
    bulk = 0.15 * salt_flat * water_flat**cement_flat
    aniso_flat = anisotropy.reshape(3, -1)
    partial_sens = jnp.zeros_like(bulk)
    for component in range(3):
        mixed = jnp.dot(weights_self, own_grads[component], preferred_element_type=jnp.float32)
        mixed = mixed + jnp.dot(
            weights_cross, other_grads[component], preferred_element_type=jnp.float32
        )
        inner = jnp.sum(own_grads[component].astype(jnp.float32) * mixed, axis=0)
        partial_sens = partial_sens + bulk * aniso_flat[component] * inner
    sensitivity = lax.psum(partial_sens, "elec")
    salt_out, water_out = archie_chain(sensitivity, salt_flat, water_flat, cement_flat)
    return (salt_out.reshape(layers, -1), water_out.reshape(layers, -1))


def solution(mesh):
    placed = (
        P("elec", ("slab", "space"), None),
        P(),
        P(),
        P("slab"),
        P(("slab", "space"), None),
        P(("slab", "space"), None),
        P(("slab", "space"), None),
        P(None, ("slab", "space"), None),
    )
    return jax.shard_map(
        local,
        mesh=mesh,
        in_specs=placed,
        out_specs=(P(("slab", "space"), None), P(("slab", "space"), None)),
        check_vma=False,
    )
```

profile of v0, /device:TPU:0, one launch (start us, length us, event | category | flops | bytes accessed | tf_op | source)
XLA Modules:
  0.0 163.6 jit_solution(15241908384131785620)
XLA Ops:
  0.6 4.7 %copy.11 = bf16[512,2,1024]{0,2,1:T(8,128)(2,1)S(1)} copy(bf16[512,2,1024]{2,1,0:T(2,128)(2,1)} %param.8) | data formatting | bytes 4194304 | tf_op args[0]
  5.4 0.0 copy-start.16
  5.4 0.0 copy-start.17
  5.4 0.0 copy-start.15
  5.4 0.0 copy-start.14
  5.4 0.5 collective-permute-start
  5.9 3.8 %collective-permute-done = bf16[512,2,1024]{0,2,1:T(8,128)(2,1)S(1)} collective-permute-done((bf16[512,2,1024]{0,2,1:T(8,128)(2,1)S(1)}, bf16[512,2,1024]{0,2,1:T(8,128)(2,1)S(1)}, u32[]{:S(2)}, u32[]{:S(2)}) %collective-permute-start) | collective-permute-done | bytes 2097184 | tf_op jit(solution)/shard_map/ppermute | solution.py:13
  9.7 2.5 %fusion.1 = (bf16[1024,1,1024]{0,2,1:T(8,128)(2,1)}, bf16[1024,1,1024]{0,2,1:T(8,128)(2,1)}) fusion(bf16[512,2,1024]{0,2,1:T(8,128)(2,1)S(1)} %copy.11, bf16[512,2,1024]{0,2,1:T(8,128)(2,1)S(1)} %collective-permute-done), kind=kLoop, calls=%fused_computation.18 | loop fusion | flops 8388608 | bytes 8388608 | tf_op jit(solution)/shard_map/concatenate | solution.py:75
  12.2 0.1 copy-done.7
  12.4 6.1 %collective-permute-start.1 = (bf16[1024,1,1024]{0,2,1:T(8,128)(2,1)}, bf16[1024,1,1024]{0,2,1:T(8,128)(2,1)}, u32[]{:S(2)}, u32[]{:S(2)}) collective-permute-start(bf16[1024,1,1024]{0,2,1:T(8,128)(2,1)} %get-tuple-element.4), channel_id=1, source_target_pairs={{0,2},{2,4},{4,6},{6,8},{8,10},{10,12},{12,14},{1,3},{3,5},{5,7},{... | collective-permute-start | bytes 6291464 | tf_op jit(solution)/shard_map/ppermute | solution.py:23
  18.5 1.3 collective-permute-start.2
  19.8 0.0 copy-done.16
  19.8 0.0 copy-done.17
  19.8 0.1 dynamic_slice.9
  19.9 0.0 copy-done.15
  19.9 0.0 copy-done.14
  20.0 0.0 copy-start.8
  20.0 1.9 %fusion.6 = bf16[512,1024]{1,0:T(8,128)(2,1)S(1)} fusion(s32[1024]{0:T(1024)S(1)} %copy-done.17, f32[1024]{0:T(1024)S(1)} %convert_element_type.96, s32[1024]{0:T(1024)S(1)} %bitcast.85, s32[1024]{0:T(1024)S(1)} %bitcast.86, s32[1024]{0:T(1024)S(1)} %bitcast.84, s32[1024]{0:T(1024)S(1)} %bitcast.83, s32[512]{0:T(512)S(1)} %dynamic_slice.9), kind=kOutput, calls=%fused_computation.26 | convolution fusion | flops 1084227584 | bytes 1075200 | tf_op jit(solution)/shard_map/dot_general | solution.py:37
  21.8 85.7 %collective-permute-done.1 = bf16[1024,1,1024]{0,2,1:T(8,128)(2,1)} collective-permute-done((bf16[1024,1,1024]{0,2,1:T(8,128)(2,1)}, bf16[1024,1,1024]{0,2,1:T(8,128)(2,1)}, u32[]{:S(2)}, u32[]{:S(2)}) %collective-permute-start.1) | collective-permute-done | bytes 2097184 | tf_op jit(solution)/shard_map/ppermute | solution.py:23
  107.6 0.0 collective-permute-done.2
  107.6 0.0 copy-done.8
  107.6 3.3 %pad_maximum_fusion = bf16[1024,4,1024]{0,2,1:T(8,128)(2,1)S(1)} fusion(bf16[1024,1,1024]{0,2,1:T(8,128)(2,1)} %collective-permute-done.2, bf16[512,2,1024]{0,2,1:T(8,128)(2,1)S(1)} %copy-done.8, bf16[512,2,1024]{0,2,1:T(8,128)(2,1)S(1)} %copy.11, bf16[1024,1,1024]{0,2,1:T(8,128)(2,1)} %collective-permute-done.1), kind=kLoop, calls=%fused_computation | loop fusion | flops 33554432 | bytes 16777216 | tf_op jit(solution)/shard_map/concatenate | solution.py:25
  110.9 2.5 %fusion.34 = (bf16[512,4,1024]{0,2,1:T(8,128)(2,1)}, bf16[512,4,1024]{0,2,1:T(8,128)(2,1)S(1)}) fusion(bf16[1024,4,1024]{0,2,1:T(8,128)(2,1)S(1)} %pad_maximum_fusion), kind=kLoop, calls=%fused_computation.63 | loop fusion | bytes 16777216 | tf_op jit(solution)/shard_map/slice | solution.py:78
  113.4 0.9 multiply_convert_fusion.6
  114.3 1.5 slice.111
  115.8 2.4 %copy.12 = bf16[512,2048]{1,0:T(8,128)(2,1)} copy(bf16[512,2048]{0,1:T(8,128)(2,1)S(1)} %bitcast.72) | data formatting | bytes 4194304 | tf_op jit(solution)/shard_map/reshape | solution.py:54
  118.2 3.3 %fusion.19 = f32[512,2048]{1,0:T(8,128)} fusion(bf16[512,2048]{0,1:T(8,128)(2,1)S(1)} %bitcast.73, bf16[512,1024]{1,0:T(8,128)(2,1)S(1)} %fusion.6, s32[]{:T(128)S(6)} %select_n.7), kind=kOutput, calls=%fused_computation.38 | convolution fusion | flops 1073741824 | bytes 6815748 | tf_op jit(solution)/shard_map/dot_general | solution.py:93
  121.5 0.0 copy-done.1
  121.5 2.9 %multiply_convert_fusion.3 = (bf16[512,2,32,32]{0,3,2,1:T(8,128)(2,1)S(1)}, bf16[512,2,32,32]{0,3,2,1:T(8,128)(2,1)S(1)}) fusion(bf16[512,2,32,32]{0,3,2,1:T(8,128)(2,1)S(1)} %copy-done.1), kind=kLoop, calls=%fused_computation.8 | loop fusion | flops 10485760 | bytes 6291456 | tf_op jit(solution)/shard_map/convert_element_type | solution.py:41
  124.4 0.0 copy-start.2
  124.4 1.3 copy-done.2
  125.7 3.3 %fusion.17 = f32[512,2048]{1,0:T(8,128)} fusion(bf16[512,2048]{0,1:T(8,128)(2,1)S(1)} %bitcast.70, bf16[512,1024]{1,0:T(8,128)(2,1)S(1)} %fusion.6, s32[]{:T(128)S(6)} %select_n.7), kind=kOutput, calls=%fused_computation.36 | convolution fusion | flops 1073741824 | bytes 6815748 | tf_op jit(solution)/shard_map/dot_general | solution.py:93
  129.0 4.0 %copy.13 = bf16[512,2048]{1,0:T(8,128)(2,1)} copy(bf16[512,2048]{0,1:T(8,128)(2,1)} %bitcast.71) | data formatting | bytes 4194304 | tf_op jit(solution)/shard_map/reshape | solution.py:54
  132.9 4.7 %multiply_convert_fusion.4 = bf16[512,2,32,32]{0,3,2,1:T(8,128)(2,1)} fusion(bf16[512,4,32,32]{0,3,2,1:T(8,128)(2,1)} %bitcast.64), kind=kLoop, calls=%fused_computation.10 | loop fusion | flops 5242880 | bytes 6291456 | tf_op jit(solution)/shard_map/convert_element_type | solution.py:41
  137.6 1.5 slice.112
  139.1 3.3 %fusion.15 = f32[512,2048]{1,0:T(8,128)} fusion(bf16[512,2048]{0,1:T(8,128)(2,1)S(1)} %bitcast.68, bf16[512,1024]{1,0:T(8,128)(2,1)S(1)} %fusion.6, s32[]{:T(128)S(6)} %select_n.7), kind=kOutput, calls=%fused_computation.34 | convolution fusion | flops 1073741824 | bytes 6815748 | tf_op jit(solution)/shard_map/dot_general | solution.py:93
  142.4 2.5 %copy.14 = bf16[512,2048]{1,0:T(8,128)(2,1)} copy(bf16[512,2048]{0,1:T(8,128)(2,1)S(1)} %bitcast.69) | data formatting | bytes 4194304 | tf_op jit(solution)/shard_map/reshape | solution.py:54
  144.9 6.7 %multiply_convert_fusion.2 = (bf16[512,2,32,32]{0,3,2,1:T(8,128)(2,1)S(1)}, bf16[512,2,32,32]{0,3,2,1:T(8,128)(2,1)S(1)}) fusion(bf16[512,2,32,32]{0,3,2,1:T(8,128)(2,1)} %slice.112), kind=kLoop, calls=%fused_computation.7 | loop fusion | flops 10485760 | bytes 6291456 | tf_op jit(solution)/shard_map/convert_element_type | solution.py:41
  151.6 3.6 %multiply_reduce_fusion.2 = f32[2048]{0:T(1024)S(1)} fusion(f32[512,2048]{1,0:T(8,128)} %fusion.19, bf16[512,2048]{1,0:T(8,128)(2,1)S(1)} %copy-done.4, bf16[512,2048]{0,1:T(8,128)(2,1)S(1)} %bitcast.75, bf16[512,1024]{1,0:T(8,128)(2,1)S(1)} %fusion.6, s32[]{:T(128)S(6)} %select_n.8), kind=kOutput, calls=%fused_computation.9 | convolution fusion | flops 1077934080 | bytes 8921092 | tf_op jit(solution)/shard_map/dot_general | solution.py:94
  155.3 0.0 copy-done.5
  155.3 0.4 copy-done.9
  155.7 1.3 multiply_reduce_fusion.1
  157.0 0.3 copy-done.6
  157.3 1.2 copy-done.10
  158.5 1.3 multiply_reduce_fusion
  159.9 2.5 %psum.7 = f32[2048]{0:T(1024)S(1)} all-reduce(f32[2048]{0:T(1024)S(1)} %fusion.22), channel_id=1, replica_groups=mesh['slab'=2,'space'=8,'elec'=2] {'elec'}, use_global_device_ids=true, to_apply=%region_3.4 | all-reduce | flops 2048 | bytes 16384 | tf_op jit(solution)/shard_map/psum | solution.py:99
  162.4 0.6 reshape.66
  163.0 0.6 reshape.67
  (23 shorter events, 0.1 us)
Async XLA Ops:
  5.4 14.4 %copy-start.16 = (bf16[1024]{0:T(1024)(128)(2,1)S(1)}, bf16[1024]{0:T(1024)(128)(2,1)}, u32[]{:S(2)}) copy-start(bf16[1024]{0:T(1024)(128)(2,1)} %param.11) | copy-start | bytes 6148
  5.4 14.4 %copy-start.17 = (s32[1024]{0:T(1024)S(1)}, s32[1024]{0:T(1024)}, u32[]{:S(2)}) copy-start(s32[1024]{0:T(1024)} %param.9) | copy-start | bytes 12292
  5.4 14.5 %copy-start.15 = (s32[1024,4]{0,1:T(4,128)S(1)}, s32[1024,4]{0,1:T(4,128)}, u32[]{:S(2)}) copy-start(s32[1024,4]{0,1:T(4,128)} %param.10) | copy-start | bytes 49156
  5.4 14.5 %copy-start.14 = (f32[3,2,1024]{2,1,0:T(2,128)S(1)}, f32[3,2,1024]{2,1,0:T(2,128)}, u32[]{:S(2)}) copy-start(f32[3,2,1024]{2,1,0:T(2,128)} %param.15) | copy-start | bytes 73732
  5.4 4.3 %collective-permute-start = (bf16[512,2,1024]{0,2,1:T(8,128)(2,1)S(1)}, bf16[512,2,1024]{0,2,1:T(8,128)(2,1)S(1)}, u32[]{:S(2)}, u32[]{:S(2)}) collective-permute-start(bf16[512,2,1024]{0,2,1:T(8,128)(2,1)S(1)} %copy.11), channel_id=1, source_target_pairs={{0,1},{1,0},{2,3},{3,2},{4,5},{5,4},{6,7},{7,6},{8,9},{9,8},{10,11... | collective-permute-start | bytes 6291464 | tf_op jit(solution)/shard_map/ppermute | solution.py:13
  9.7 2.6 %copy-start.7 = (bf16[512,2,1024]{0,2,1:T(8,128)(2,1)}, bf16[512,2,1024]{0,2,1:T(8,128)(2,1)S(1)}, u32[]{:S(2)}) copy-start(bf16[512,2,1024]{0,2,1:T(8,128)(2,1)S(1)} %collective-permute-done) | copy-start | bytes 6291460
  12.4 95.2 %collective-permute-start.1 = (bf16[1024,1,1024]{0,2,1:T(8,128)(2,1)}, bf16[1024,1,1024]{0,2,1:T(8,128)(2,1)}, u32[]{:S(2)}, u32[]{:S(2)}) collective-permute-start(bf16[1024,1,1024]{0,2,1:T(8,128)(2,1)} %get-tuple-element.4), channel_id=1, source_target_pairs={{0,2},{2,4},{4,6},{6,8},{8,10},{10,12},{12,14},{1,3},{3,5},{5,7},{... | collective-permute-start | bytes 6291464 | tf_op jit(solution)/shard_map/ppermute | solution.py:23
  18.5 89.1 %collective-permute-start.2 = (bf16[1024,1,1024]{0,2,1:T(8,128)(2,1)}, bf16[1024,1,1024]{0,2,1:T(8,128)(2,1)}, u32[]{:S(2)}, u32[]{:S(2)}) collective-permute-start(bf16[1024,1,1024]{0,2,1:T(8,128)(2,1)} %get-tuple-element.5), channel_id=1, source_target_pairs={{2,0},{4,2},{6,4},{8,6},{10,8},{12,10},{14,12},{3,1},{5,3},{7,5},{... | collective-permute-start | bytes 6291464 | tf_op jit(solution)/shard_map/ppermute | solution.py:24
  20.0 87.6 %copy-start.8 = (bf16[512,2,1024]{0,2,1:T(8,128)(2,1)S(1)}, bf16[512,2,1024]{0,2,1:T(8,128)(2,1)}, u32[]{:S(2)}) copy-start(bf16[512,2,1024]{0,2,1:T(8,128)(2,1)} %copy-done.7) | copy-start | bytes 6291460
  118.2 3.3 %copy-start.1 = (bf16[512,2,32,32]{0,3,2,1:T(8,128)(2,1)S(1)}, bf16[512,2,32,32]{0,3,2,1:T(8,128)(2,1)}, u32[]{:S(2)}) copy-start(bf16[512,2,32,32]{0,3,2,1:T(8,128)(2,1)} %slice.111) | copy-start | bytes 6291460
  124.4 1.3 copy-start.2
  132.9 4.7 %copy-start = (bf16[512,4,1024]{0,2,1:T(8,128)(2,1)S(1)}, bf16[512,4,1024]{0,2,1:T(8,128)(2,1)}, u32[]{:S(2)}) copy-start(bf16[512,4,1024]{0,2,1:T(8,128)(2,1)} %get-tuple-element.2) | copy-start | bytes 12582916
  144.8 6.7 %copy-start.3 = (bf16[512,2,32,32]{0,3,2,1:T(8,128)(2,1)S(1)}, bf16[512,2,32,32]{0,3,2,1:T(8,128)(2,1)}, u32[]{:S(2)}) copy-start(bf16[512,2,32,32]{0,3,2,1:T(8,128)(2,1)} %multiply_convert_fusion.4) | copy-start | bytes 6291460
  144.8 6.7 %copy-start.4 = (bf16[512,2048]{1,0:T(8,128)(2,1)S(1)}, bf16[512,2048]{1,0:T(8,128)(2,1)}, u32[]{:S(2)}) copy-start(bf16[512,2048]{1,0:T(8,128)(2,1)} %copy.12) | copy-start | bytes 6291460
  151.6 3.7 %copy-start.5 = (bf16[512,2048]{1,0:T(8,128)(2,1)S(1)}, bf16[512,2048]{1,0:T(8,128)(2,1)}, u32[]{:S(2)}) copy-start(bf16[512,2048]{1,0:T(8,128)(2,1)} %copy.13) | copy-start | bytes 6291460
  151.6 4.1 %copy-start.9 = (f32[512,2048]{1,0:T(8,128)S(1)}, f32[512,2048]{1,0:T(8,128)}, u32[]{:S(2)}) copy-start(f32[512,2048]{1,0:T(8,128)} %fusion.17) | copy-start | bytes 12582916
  155.7 1.6 copy-start.6
  155.7 2.8 %copy-start.10 = (f32[512,2048]{1,0:T(8,128)S(1)}, f32[512,2048]{1,0:T(8,128)}, u32[]{:S(2)}) copy-start(f32[512,2048]{1,0:T(8,128)} %fusion.15) | copy-start | bytes 12582916
  158.5 1.3 copy-start.11
  158.5 1.3 copy-start.12
  158.5 1.3 copy-start.13
where the time goes:
time: 165 us; the launch traced here: 164 us
  waiting for transfers between devices  89.5 us (54%)
  local copies, waits for them, and re-layouts  23.8 us (14%)
  other arithmetic  21 us (13%)
  matrix products  17.9 us (11%)
  starting transfers between devices  7.94 us (5%)
  blocking collectives  2.5 us (2%)
    ppermute x1, waiting for transfers between devices, with_halo(): before = lax.ppermute(last, axis, up)  85.7 us
    convert_element_type x4, other arithmetic, half_difference(): (0.5 * (upper.astype(jnp.float32) - lower.astype(jnp.float32))).astype(jn...  15.2 us
    dot_general x3, matrix products, local(): jnp.dot(weights_self, own_grads[component], preferred_element_type=jnp.fl...  9.8 us
    unnamed x38, local copies, waits for them, and re-layouts  8.15 us
    dot_general x3, matrix products, local(): jnp.dot(weights_cross, other_grads[component], preferred_element_type=jnp...  6.25 us
    ppermute x1, starting transfers between devices, with_halo(): before = lax.ppermute(last, axis, up)  6.14 us
    reshape x1, local copies, waits for them, and re-layouts, layer_gradients(): along_y.reshape(rows_n, -1)  3.95 us
    ppermute x1, waiting for transfers between devices, partner(): return lax.ppermute(value, axis, pairs)  3.79 us
  transfers between devices with their start and end apart: 3, of which 2 were waited for; matrix products, arithmetic and copies ran while one was open for 1% of the time, Pallas kernels for 0%

commit v1 on v0

v1 whole, which is shorter than its diff:
```python
import jax
import jax.numpy as jnp
from jax import lax
from jax.sharding import PartitionSpec as P

NX = 32
NY = 32


def assemble(quadripoles, weighted_misfit, order):
    left_side = (quadripoles[:, 0][None, :] == order[:, None]).astype(jnp.bfloat16) - (
        quadripoles[:, 1][None, :] == order[:, None]
    ).astype(jnp.bfloat16)
    third = quadripoles[:, 2][:, None] == order[None, :]
    fourth = quadripoles[:, 3][:, None] == order[None, :]
    signed = third.astype(jnp.float32) - fourth.astype(jnp.float32)
    right_side = (weighted_misfit.astype(jnp.float32)[:, None] * signed).astype(jnp.bfloat16)
    return jnp.dot(left_side, right_side, preferred_element_type=jnp.float32).astype(jnp.bfloat16)


def half_difference(upper, lower):
    return (0.5 * (upper.astype(jnp.float32) - lower.astype(jnp.float32))).astype(jnp.bfloat16)


def form(weights, grads):
    mixed = jnp.dot(weights, grads, preferred_element_type=jnp.float32)
    return jnp.sum(grads.astype(jnp.float32) * mixed, axis=0)


def local(potentials, elec_order, quadripoles, weighted_misfit, salinity, water_content, cementation, anisotropy):
    blocks = lax.axis_size("space")
    s = lax.axis_index("space")
    c = lax.axis_index("elec")
    rows, layers, cells = potentials.shape
    half = cells // 2
    odd = lax.rem(s, 2)
    to_mate = [(i, i ^ 1) for i in range(blocks)]
    back_two = [(i, (i - 2) % blocks if i % 2 == 0 else (i + 2) % blocks) for i in range(blocks)]
    swap = [(0, 1), (1, 0)]

    def cut(array, layer, start, width):
        return lax.dynamic_slice(array, (0, layer, start), (rows, 1, width)).reshape(rows, width)

    near = cut(potentials, odd, c * half, half)
    far = cut(potentials, 1 - odd, c * half, half)
    near_in_0 = lax.ppermute(near, "space", to_mate)
    far_in_0 = lax.ppermute(far, "space", back_two)

    halo = 128
    width = half + halo
    theirs = lax.dynamic_slice(potentials, (0, 0, (1 - c) * (half - halo)), (rows, layers, width))
    other = lax.ppermute(theirs, "elec", swap)
    own = lax.dynamic_slice(potentials, (0, 0, c * (half - halo)), (rows, layers, width))
    near_2 = cut(other, odd, c * halo, half)
    far_2 = cut(other, 1 - odd, c * halo, half)
    near_in_1 = lax.ppermute(near_2, "space", to_mate)
    far_in_1 = lax.ppermute(far_2, "space", back_two)

    order = jnp.roll(elec_order, -c * rows)
    weights = assemble(quadripoles, weighted_misfit, order)

    field = jnp.concatenate([own, other], axis=0).reshape(2 * rows, layers, width // NX, NX)
    pad_x = jnp.pad(lax.dynamic_slice_in_dim(field, c * (halo // NX), half // NX, 2), ((0, 0), (0, 0), (0, 0), (1, 1)))
    along_x = half_difference(pad_x[..., 2:], pad_x[..., :-2]).reshape(2 * rows, -1)
    pad_y = jnp.pad(field, ((0, 0), (0, 0), (1, 1), (0, 0)))
    pad_y = lax.dynamic_slice_in_dim(pad_y, c * (halo // NX), half // NX + 2, 2)
    along_y = half_difference(pad_y[:, :, 2:], pad_y[:, :, :-2]).reshape(2 * rows, -1)
    form_y = form(weights, along_y).reshape(layers, half)
    form_x = form(weights, along_x).reshape(layers, half)

    bulk = 0.15 * salinity * water_content**cementation
    mine = lax.dynamic_slice_in_dim(anisotropy, c * half, half, 2)
    flat = mine[1] * form_y + mine[2] * form_x
    flat_other = lax.ppermute(flat, "elec", swap)

    near_in = jnp.concatenate([near_in_0, near_in_1], axis=0)
    far_in = jnp.concatenate([far_in_0, far_in_1], axis=0)
    far_all = jnp.concatenate([far, far_2], axis=0)
    inside = jnp.where(odd == 1, s >= 2, s + 2 < blocks)
    grad_a = half_difference(far_all, near_in)
    grad_b = half_difference(far_in, jnp.where(inside, near_in, jnp.zeros_like(near_in)))
    form_a = form(weights, grad_a)
    form_b = form(weights, grad_b)

    def joint(pairs, cross):
        return [(2 * i + k, 2 * j + (k ^ cross)) for i, j in pairs for k in range(2)]

    ahead_two = [(j, i) for i, j in back_two]
    both = ("space", "elec")
    a_same = lax.ppermute(form_a, both, joint(to_mate, 0))
    a_cross = lax.ppermute(form_a, both, joint(to_mate, 1))
    b_same = lax.ppermute(form_b, both, joint(ahead_two, 0))
    b_cross = lax.ppermute(form_b, both, joint(ahead_two, 1))

    def whole(same, cross):
        return jnp.where(c == 0, jnp.concatenate([same, cross], -1), jnp.concatenate([cross, same], -1))

    from_mate = whole(a_same, a_cross)
    from_far = whole(b_same, b_cross)
    form_z = jnp.where(odd == 1, jnp.stack([from_mate, from_far]), jnp.stack([from_far, from_mate]))
    sensitivity = bulk * (anisotropy[0] * form_z + whole(flat, flat_other))
    return sensitivity / salinity, cementation * sensitivity / water_content


def solution(mesh):
    split = P(("slab", "space"), None)
    placed = (P("elec", ("slab", "space"), None), P(), P(), P("slab"), split, split, split, P(None, ("slab", "space"), None))
    return jax.shard_map(local, mesh=mesh, in_specs=placed, out_specs=(split, split), check_vma=False)
```

time: 165 us -> 77.8 us (0.47)
  waiting for transfers between devices: 89.5 us -> 7.41 us
  other arithmetic: 21 us -> 9.63 us
  starting transfers between devices: 7.94 us -> 15 us
  local copies, waits for them, and re-layouts: 23.8 us -> 26.6 us
  blocking collectives: 2.5 us -> 0 us
    ppermute x3 -> x10, waiting for transfers between devices: 89.5 us -> 7.41 us  [the longest x1 4 us: local(): near_in_0 = lax.ppermute(near, 'space', to_mate)]
    convert_element_type x4 -> x2, other arithmetic: 15.2 us -> 5.13 us  [half_difference(): (0.5 * (upper.astype(jnp.float32) - lower.astype(jnp.float32))).astype(jn...]
    dynamic_slice x1 -> x3, local copies, waits for them, and re-layouts: 0.08 us -> 7.42 us  [the longest x1 3.65 us: cut(): lax.dynamic_slice(array, (0, layer, start), (rows, 1, width))]
    ppermute x3 -> x10, starting transfers between devices: 7.94 us -> 15 us  [the longest x1 3.65 us: local(): far_in_0 = lax.ppermute(far, 'space', back_two)]
    slice x4 -> x1, local copies, waits for them, and re-layouts: 5.51 us -> 0.01 us  [assemble(): quadripoles[:, 0][None, :] == order[:, None]]
    concatenate x0 -> x2, local copies, waits for them, and re-layouts: none -> 4.07 us  [the longest x1 2.99 us: local(): jnp.concatenate([own, other], axis=0)]
    unnamed x38 -> x33, local copies, waits for them, and re-layouts: 8.15 us -> 4.72 us
    concatenate x2, other arithmetic: 5.79 us -> 3.18 us  [the longest x1 3.1 us: local(): jnp.concatenate([own, other], axis=0)]
  transfers between devices with their start and end apart: 3 -> 10, of which waited for: 2 -> 4; matrix products, arithmetic and copies ran while one was open for 1% -> 61% of each run, Pallas kernels for 0% -> 0%
where the time goes in v1:
time: 77.8 us; the launch traced here: 77.3 us
  local copies, waits for them, and re-layouts  26.6 us (34%)
  matrix products  17.7 us (23%)
  starting transfers between devices  15 us (19%)
  other arithmetic  9.63 us (12%)
  waiting for transfers between devices  7.41 us (10%)
  between operations  0.96 us (1%)
    dot_general x4, matrix products, form(): mixed = jnp.dot(weights, grads, preferred_element_type=jnp.float32)  13.6 us
    convert_element_type x2, other arithmetic, half_difference(): (0.5 * (upper.astype(jnp.float32) - lower.astype(jnp.float32))).astype(jn...  5.13 us
    unnamed x33, local copies, waits for them, and re-layouts  4.72 us
    dot_general x1, matrix products, assemble(): jnp.dot(left_side, right_side, preferred_element_type=jnp.float32)  4.16 us
    reshape x1, local copies, waits for them, and re-layouts, local(): half_difference(pad_x[..., 2:], pad_x[..., :-2]).reshape(2 * rows, -1)  4.1 us
    ppermute x1, waiting for transfers between devices, local(): near_in_0 = lax.ppermute(near, 'space', to_mate)  4 us
    reshape x1, local copies, waits for them, and re-layouts, local(): half_difference(pad_y[:, :, 2:], pad_y[:, :, :-2]).reshape(2 * rows, -1)  3.96 us
    ppermute x1, starting transfers between devices, local(): far_in_0 = lax.ppermute(far, 'space', back_two)  3.65 us
  transfers between devices with their start and end apart: 10, of which 4 were waited for; matrix products, arithmetic and copies ran while one was open for 61% of the time, Pallas kernels for 0%

profile of v1, /device:TPU:0, one launch (start us, length us, event | category | flops | bytes accessed | tf_op | source)
XLA Modules:
  0.0 77.3 jit_solution(1900195675081396259)
XLA Ops:
  0.6 3.6 %constant_dynamic-slice_fusion.1 = (bf16[512,2,640]{2,1,0:T(2,128)(2,1)S(1)}, bf16[512,2,640]{2,1,0:T(2,128)(2,1)S(1)}) fusion(bf16[512,2,1024]{2,1,0:T(2,128)(2,1)} %param.8, s32[]{:T(128)S(6)} %select_n.110, s32[]{:T(128)S(6)} %select_n.98), kind=kLoop, calls=%fused_computation.60 | loop fusion | bytes 5242888 | tf_op jit(solution)/shard_map/dynamic_slice | solution.py:53
  4.2 0.0 copy-start
  4.2 1.3 %copy.18 = bf16[512,2,640]{2,0,1:T(8,128)(2,1)} copy(bf16[512,2,640]{2,1,0:T(2,128)(2,1)S(1)} %get-tuple-element.7) | data formatting | bytes 2621440
  5.5 0.5 collective-permute-start
  5.9 0.3 copy-done
  6.3 3.7 %constant_dynamic-slice_fusion.4 = (bf16[512,1,512]{2,1,0:T(2,128)(2,1)S(1)}, bf16[512,1,512]{2,1,0:T(2,128)(2,1)S(1)}) fusion(bf16[512,2,1024]{2,1,0:T(2,128)(2,1)S(1)} %copy-done, s32[]{:T(128)S(6)} %select_n.96, s32[]{:T(128)S(6)} %select_n.97, s32[]{:T(128)S(6)} %select_n.100), kind=kLoop, calls=%fused_computation.63 | loop fusion | bytes 2097164 | tf_op jit(solution)/shard_map/dynamic_slice | solution.py:42
  9.9 0.0 copy-start.11
  9.9 0.9 %copy.23 = bf16[512,1,512]{2,0,1:T(8,128)(2,1)} copy(bf16[512,1,512]{2,1,0:T(2,128)(2,1)S(1)} %get-tuple-element.5) | data formatting | bytes 1048576
  10.8 3.0 %collective-permute-start.1 = (bf16[512,512]{1,0:T(8,128)(2,1)}, bf16[512,512]{1,0:T(8,128)(2,1)}, u32[]{:S(2)}, u32[]{:S(2)}) collective-permute-start(bf16[512,512]{1,0:T(8,128)(2,1)} %bitcast.40), channel_id=1, source_target_pairs={{0,2},{2,0},{4,6},{6,4},{8,10},{10,8},{12,14},{14,12},{1,3},{3,1},... | collective-permute-start | bytes 1572872 | tf_op jit(solution)/shard_map/ppermute | solution.py:46
  13.8 0.1 copy.24
  13.9 3.7 %collective-permute-start.5 = (bf16[512,512]{1,0:T(8,128)(2,1)S(1)}, bf16[512,512]{1,0:T(8,128)(2,1)}, u32[]{:S(2)}, u32[]{:S(2)}) collective-permute-start(bf16[512,512]{1,0:T(8,128)(2,1)S(1)} %bitcast.48), channel_id=1, source_target_pairs={{0,12},{2,6},{4,0},{6,10},{8,4},{10,14},{12,8},{14,2},{1,13},{3,7}... | collective-permute-start | bytes 1572872 | tf_op jit(solution)/shard_map/ppermute | solution.py:47
  17.6 0.2 copy.20
  17.8 0.1 fusion.27
  17.9 4.2 %fusion.10 = bf16[1024,1024]{1,0:T(8,128)(2,1)} fusion(s32[1024]{0:T(1024)S(1)} %fusion.27, f32[1024]{0:T(1024)S(1)} %convert_element_type.79, s32[1024]{0:T(1024)S(1)} %bitcast.52, s32[1024]{0:T(1024)S(1)} %bitcast.53, s32[1024]{0:T(1024)S(1)} %bitcast.51, s32[1024]{0:T(1024)S(1)} %bitcast.50), kind=kOutput, calls=%fused_computation.25 | convolution fusion | flops 2161115136 | bytes 2121728 | tf_op jit(solution)/shard_map/dot_general | solution.py:18
  22.1 4.0 %collective-permute-done.1 = bf16[512,512]{1,0:T(8,128)(2,1)} collective-permute-done((bf16[512,512]{1,0:T(8,128)(2,1)}, bf16[512,512]{1,0:T(8,128)(2,1)}, u32[]{:S(2)}, u32[]{:S(2)}) %collective-permute-start.1) | collective-permute-done | bytes 524320 | tf_op jit(solution)/shard_map/ppermute | solution.py:46
  26.1 1.9 %constant_dynamic-update-slice_fusion.1 = bf16[1024,512]{1,0:T(8,128)(2,1)} fusion(bf16[512,512]{1,0:T(8,128)(2,1)} %collective-permute-done.1), kind=kLoop, calls=%fused_computation.52 | loop fusion | bytes 1048576
  27.9 0.0 collective-permute-done
  27.9 2.3 %dynamic-slice_bitcast_fusion.1 = (bf16[512,512]{1,0:T(8,128)(2,1)}, bf16[512,512]{1,0:T(8,128)(2,1)}) fusion(bf16[512,2,640]{2,0,1:T(8,128)(2,1)} %collective-permute-done, s32[]{:T(128)S(6)} %select_n.96, s32[]{:T(128)S(6)} %select_n.99, s32[]{:T(128)S(6)} %select_n.100), kind=kLoop, calls=%fused_computation.40 | loop fusion | bytes 2097164 | tf_op jit(solution)/shard_map/reshape | solution.py:42
  30.2 1.7 %collective-permute-start.2 = (bf16[512,512]{1,0:T(8,128)(2,1)}, bf16[512,512]{1,0:T(8,128)(2,1)}, u32[]{:S(2)}, u32[]{:S(2)}) collective-permute-start(bf16[512,512]{1,0:T(8,128)(2,1)} %get-tuple-element.9), channel_id=1, source_target_pairs={{0,2},{2,0},{4,6},{6,4},{8,10},{10,8},{12,14},{14,12},{1,3},{3,1},... | collective-permute-start | bytes 1572872 | tf_op jit(solution)/shard_map/ppermute | solution.py:56
  31.9 3.6 %collective-permute-start.6 = (bf16[512,512]{1,0:T(8,128)(2,1)}, bf16[512,512]{1,0:T(8,128)(2,1)}, u32[]{:S(2)}, u32[]{:S(2)}) collective-permute-start(bf16[512,512]{1,0:T(8,128)(2,1)} %get-tuple-element.8), channel_id=1, source_target_pairs={{0,12},{2,6},{4,0},{6,10},{8,4},{10,14},{12,8},{14,2},{1,13},{3,7}... | collective-permute-start | bytes 1572872 | tf_op jit(solution)/shard_map/ppermute | solution.py:57
  35.5 3.1 %pad_maximum_fusion = bf16[1024,2,640]{2,0,1:T(8,128)(2,1)} fusion(bf16[512,2,640]{2,0,1:T(8,128)(2,1)} %collective-permute-done, bf16[512,2,640]{2,0,1:T(8,128)(2,1)S(1)} %copy.20), kind=kLoop, calls=%fused_computation.9 | loop fusion | flops 5242880 | bytes 5242880 | tf_op jit(solution)/shard_map/concatenate | solution.py:62
  38.6 3.0 %copy.14 = bf16[1024,2,640]{0,2,1:T(8,128)(2,1)S(1)} copy(bf16[1024,2,640]{2,0,1:T(8,128)(2,1)} %pad_maximum_fusion) | data formatting | bytes 5242880 | tf_op jit(solution)/shard_map/concatenate | solution.py:62
  41.6 2.4 %multiply_convert_fusion.1 = bf16[1024,2,16,32]{0,3,2,1:T(8,128)(2,1)} fusion(s32[]{:T(128)S(6)} %select_n.111, bf16[1024,2,20,32]{0,3,2,1:T(8,128)(2,1)S(1)} %bitcast.42, s32[]{:T(128)S(6)} %add.68), kind=kLoop, calls=%fused_computation.3 | loop fusion | flops 5242880 | bytes 4718600 | tf_op jit(solution)/shard_map/convert_element_type | solution.py:22
  44.0 4.0 %copy.15 = bf16[1024,1024]{1,0:T(8,128)(2,1)} copy(bf16[1024,1024]{0,1:T(8,128)(2,1)} %bitcast.44) | data formatting | bytes 4194304 | tf_op jit(solution)/shard_map/reshape | solution.py:67
  48.0 0.2 constant_dynamic-slice_fusion
  48.2 2.7 %multiply_convert_fusion = bf16[1024,2,16,32]{0,3,2,1:T(8,128)(2,1)} fusion(bf16[1024,2,16,32]{0,3,2,1:T(8,128)(2,1)S(1)} %constant_dynamic-slice_fusion), kind=kLoop, calls=%fused_computation.1 | loop fusion | flops 5242880 | bytes 4194304 | tf_op jit(solution)/shard_map/convert_element_type | solution.py:22
  50.9 4.1 %copy.16 = bf16[1024,1024]{1,0:T(8,128)(2,1)} copy(bf16[1024,1024]{0,1:T(8,128)(2,1)} %bitcast.46) | data formatting | bytes 4194304 | tf_op jit(solution)/shard_map/reshape | solution.py:64
  55.1 4.8 %multiply_reduce_fusion.1 = f32[1024]{0:T(1024)S(1)} fusion(bf16[1024,1024]{1,0:T(8,128)(2,1)} %copy.15, bf16[1024,1024]{1,0:T(8,128)(2,1)} %fusion.10, bf16[1024,1024]{0,1:T(8,128)(2,1)S(1)} %bitcast.45), kind=kOutput, calls=%fused_computation.2 | convolution fusion | flops 2150628352 | bytes 6295552 | tf_op jit(solution)/shard_map/dot_general | solution.py:26
  59.9 0.0 copy-start.7
  59.9 2.4 %multiply_reduce_fusion = f32[1024]{0:T(1024)S(1)} fusion(bf16[1024,1024]{1,0:T(8,128)(2,1)S(1)} %copy-done.3, bf16[1024,1024]{1,0:T(8,128)(2,1)S(1)} %copy-done.12, bf16[1024,1024]{0,1:T(8,128)(2,1)S(1)} %bitcast.47), kind=kOutput, calls=%fused_computation | convolution fusion | flops 2150628352 | bytes 6295552 | tf_op jit(solution)/shard_map/dot_general | solution.py:26
  62.3 0.1 collective-permute-start.9
  62.4 0.0 collective-permute-done.2
  62.4 1.1 %constant_dynamic-update-slice_fusion = bf16[1024,512]{1,0:T(8,128)(2,1)S(1)} fusion(bf16[1024,512]{1,0:T(8,128)(2,1)S(1)} %copy-done.4, bf16[512,512]{1,0:T(8,128)(2,1)} %collective-permute-done.2), kind=kLoop, calls=%fused_computation.51 | loop fusion | bytes 1048576 | tf_op jit(solution)/shard_map/concatenate | solution.py:76
  63.5 0.0 collective-permute-done.6
  63.5 3.8 %multiply_reduce_fusion.2 = f32[512]{0:T(512)S(1)} fusion(bf16[1024,1024]{1,0:T(8,128)(2,1)} %fusion.10, bf16[512,512]{1,0:T(8,128)(2,1)} %collective-permute-done.6, bf16[512,512]{1,0:T(8,128)(2,1)} %collective-permute-done.5, bf16[1024,512]{1,0:T(8,128)(2,1)S(1)} %constant_dynamic-update-slice_fusion, pred[]{:T(512)S(6)} %select_n.104), kind=kOutput, calls=%fused_computation.14 | convolution fusion | flops 1084751360 | bytes 4196353 | tf_op jit(solution)/shard_map/dot_general | solution.py:26
  67.3 0.0 copy-start.5
  67.3 0.0 copy-start.8
  67.4 0.0 copy-start.9
  67.4 0.1 collective-permute-start.7
  67.4 0.1 collective-permute-start.8
  67.5 2.6 %multiply_reduce_fusion.3 = f32[512]{0:T(512)S(1)} fusion(bf16[1024,1024]{1,0:T(8,128)(2,1)S(1)} %copy-done.13, bf16[1024,512]{1,0:T(8,128)(2,1)S(1)} %constant_dynamic-update-slice_fusion, bf16[512,512]{1,0:T(8,128)(2,1)} %get-tuple-element.8, bf16[512,512]{1,0:T(8,128)(2,1)S(1)} %bitcast.49), kind=kOutput, calls=%fused_computation.16 | convolution fusion | flops 1083702784 | bytes 4196352 | tf_op jit(solution)/shard_map/dot_general | solution.py:26
  70.2 2.2 %collective-permute-start.4 = (f32[512]{0:T(512)S(1)}, f32[512]{0:T(512)S(1)}, u32[]{:S(2)}, u32[]{:S(2)}) collective-permute-start(f32[512]{0:T(512)S(1)} %multiply_reduce_fusion.3), channel_id=1, source_target_pairs={{0,3},{1,2},{2,1},{3,0},{4,7},{5,6},{6,5},{7,4},{8,11},{9,10},{10,... | collective-permute-start | bytes 6152 | tf_op jit(solution)/shard_map/ppermute | solution.py:91
  72.4 0.2 collective-permute-start.3
  72.5 0.3 collective-permute-done.7
  72.8 0.9 %collective-permute-done.4 = f32[512]{0:T(512)S(1)} collective-permute-done((f32[512]{0:T(512)S(1)}, f32[512]{0:T(512)S(1)}, u32[]{:S(2)}, u32[]{:S(2)}) %collective-permute-start.4) | collective-permute-done | bytes 2080 | tf_op jit(solution)/shard_map/ppermute | solution.py:91
  73.7 2.3 %collective-permute-done.3 = f32[512]{0:T(512)S(1)} collective-permute-done((f32[512]{0:T(512)S(1)}, f32[512]{0:T(512)S(1)}, u32[]{:S(2)}, u32[]{:S(2)}) %collective-permute-start.3) | collective-permute-done | bytes 2080 | tf_op jit(solution)/shard_map/ppermute | solution.py:90
  76.0 0.7 multiply_divide_fusion
  76.7 0.6 div.6
  (31 shorter events, 0.1 us)
Async XLA Ops:
  4.2 2.1 %copy-start = (bf16[512,2,1024]{2,1,0:T(2,128)(2,1)S(1)}, bf16[512,2,1024]{2,1,0:T(2,128)(2,1)}, u32[]{:S(2)}) copy-start(bf16[512,2,1024]{2,1,0:T(2,128)(2,1)} %param.8) | copy-start | bytes 6291460
  5.5 22.5 %collective-permute-start = (bf16[512,2,640]{2,0,1:T(8,128)(2,1)}, bf16[512,2,640]{2,0,1:T(8,128)(2,1)}, u32[]{:S(2)}, u32[]{:S(2)}) collective-permute-start(bf16[512,2,640]{2,0,1:T(8,128)(2,1)} %copy.18), channel_id=1, source_target_pairs={{0,1},{1,0},{2,3},{3,2},{4,5},{5,4},{6,7},{7,6},{8,9},{9,8},{10,11... | collective-permute-start | bytes 3932168 | tf_op jit(solution)/shard_map/ppermute | solution.py:52
  9.9 7.7 %copy-start.11 = (bf16[1024]{0:T(1024)(128)(2,1)S(1)}, bf16[1024]{0:T(1024)(128)(2,1)}, u32[]{:S(2)}) copy-start(bf16[1024]{0:T(1024)(128)(2,1)} %param.11) | copy-start | bytes 6148
  10.8 15.2 %collective-permute-start.1 = (bf16[512,512]{1,0:T(8,128)(2,1)}, bf16[512,512]{1,0:T(8,128)(2,1)}, u32[]{:S(2)}, u32[]{:S(2)}) collective-permute-start(bf16[512,512]{1,0:T(8,128)(2,1)} %bitcast.40), channel_id=1, source_target_pairs={{0,2},{2,0},{4,6},{6,4},{8,10},{10,8},{12,14},{14,12},{1,3},{3,1},... | collective-permute-start | bytes 1572872 | tf_op jit(solution)/shard_map/ppermute | solution.py:46
  13.8 4.0 %copy-start.10 = (s32[1024]{0:T(1024)S(1)}, s32[1024]{0:T(1024)}, u32[]{:S(2)}) copy-start(s32[1024]{0:T(1024)} %param.9) | copy-start | bytes 12292
  13.8 4.1 %copy-start.6 = (s32[1024,4]{0,1:T(4,128)S(1)}, s32[1024,4]{0,1:T(4,128)}, u32[]{:S(2)}) copy-start(s32[1024,4]{0,1:T(4,128)} %param.10) | copy-start | bytes 49156
  13.9 49.6 %collective-permute-start.5 = (bf16[512,512]{1,0:T(8,128)(2,1)S(1)}, bf16[512,512]{1,0:T(8,128)(2,1)}, u32[]{:S(2)}, u32[]{:S(2)}) collective-permute-start(bf16[512,512]{1,0:T(8,128)(2,1)S(1)} %bitcast.48), channel_id=1, source_target_pairs={{0,12},{2,6},{4,0},{6,10},{8,4},{10,14},{12,8},{14,2},{1,13},{3,7}... | collective-permute-start | bytes 1572872 | tf_op jit(solution)/shard_map/ppermute | solution.py:47
  30.2 32.2 %collective-permute-start.2 = (bf16[512,512]{1,0:T(8,128)(2,1)}, bf16[512,512]{1,0:T(8,128)(2,1)}, u32[]{:S(2)}, u32[]{:S(2)}) collective-permute-start(bf16[512,512]{1,0:T(8,128)(2,1)} %get-tuple-element.9), channel_id=1, source_target_pairs={{0,2},{2,0},{4,6},{6,4},{8,10},{10,8},{12,14},{14,12},{1,3},{3,1},... | collective-permute-start | bytes 1572872 | tf_op jit(solution)/shard_map/ppermute | solution.py:56
  31.9 31.6 %collective-permute-start.6 = (bf16[512,512]{1,0:T(8,128)(2,1)}, bf16[512,512]{1,0:T(8,128)(2,1)}, u32[]{:S(2)}, u32[]{:S(2)}) collective-permute-start(bf16[512,512]{1,0:T(8,128)(2,1)} %get-tuple-element.8), channel_id=1, source_target_pairs={{0,12},{2,6},{4,0},{6,10},{8,4},{10,14},{12,8},{14,2},{1,13},{3,7}... | collective-permute-start | bytes 1572872 | tf_op jit(solution)/shard_map/ppermute | solution.py:57
  50.9 4.1 %copy-start.1 = (bf16[1024,2,16,32]{0,3,2,1:T(8,128)(2,1)S(1)}, bf16[1024,2,16,32]{0,3,2,1:T(8,128)(2,1)}, u32[]{:S(2)}) copy-start(bf16[1024,2,16,32]{0,3,2,1:T(8,128)(2,1)} %multiply_convert_fusion.1) | copy-start | bytes 6291460
  55.0 4.8 %copy-start.2 = (bf16[1024,2,16,32]{0,3,2,1:T(8,128)(2,1)S(1)}, bf16[1024,2,16,32]{0,3,2,1:T(8,128)(2,1)}, u32[]{:S(2)}) copy-start(bf16[1024,2,16,32]{0,3,2,1:T(8,128)(2,1)} %multiply_convert_fusion) | copy-start | bytes 6291460
  55.0 4.8 %copy-start.3 = (bf16[1024,1024]{1,0:T(8,128)(2,1)S(1)}, bf16[1024,1024]{1,0:T(8,128)(2,1)}, u32[]{:S(2)}) copy-start(bf16[1024,1024]{1,0:T(8,128)(2,1)} %copy.16) | copy-start | bytes 6291460
  55.1 4.8 %copy-start.12 = (bf16[1024,1024]{1,0:T(8,128)(2,1)S(1)}, bf16[1024,1024]{1,0:T(8,128)(2,1)}, u32[]{:S(2)}) copy-start(bf16[1024,1024]{1,0:T(8,128)(2,1)} %fusion.10) | copy-start | bytes 6291460
  59.9 2.4 %copy-start.7 = (f32[3,2,1024]{2,1,0:T(2,128)S(1)}, f32[3,2,1024]{2,1,0:T(2,128)}, u32[]{:S(2)}) copy-start(f32[3,2,1024]{2,1,0:T(2,128)} %param.15) | copy-start | bytes 73732
  59.9 2.6 %copy-start.4 = (bf16[1024,512]{1,0:T(8,128)(2,1)S(1)}, bf16[1024,512]{1,0:T(8,128)(2,1)}, u32[]{:S(2)}) copy-start(bf16[1024,512]{1,0:T(8,128)(2,1)} %constant_dynamic-update-slice_fusion.1) | copy-start | bytes 3145732
  62.3 13.6 %collective-permute-start.9 = (f32[2,512]{1,0:T(2,128)S(1)}, f32[2,512]{1,0:T(2,128)S(1)}, u32[]{:S(2)}, u32[]{:S(2)}) collective-permute-start(f32[2,512]{1,0:T(2,128)S(1)} %fusion.29), channel_id=1, source_target_pairs={{0,1},{1,0},{2,3},{3,2},{4,5},{5,4},{6,7},{7,6},{8,9},{9,8},{10,11... | collective-permute-start | bytes 12296 | tf_op jit(solution)/shard_map/ppermute | solution.py:74
  63.5 4.0 %copy-start.13 = (bf16[1024,1024]{1,0:T(8,128)(2,1)S(1)}, bf16[1024,1024]{1,0:T(8,128)(2,1)}, u32[]{:S(2)}) copy-start(bf16[1024,1024]{1,0:T(8,128)(2,1)} %fusion.10) | copy-start | bytes 6291460
  67.3 8.6 %copy-start.5 = (f32[2,1024]{1,0:T(2,128)S(1)}, f32[2,1024]{1,0:T(2,128)}, u32[]{:S(2)}) copy-start(f32[2,1024]{1,0:T(2,128)} %param.12) | copy-start | bytes 24580
  67.3 8.6 %copy-start.8 = (f32[2,1024]{1,0:T(2,128)S(1)}, f32[2,1024]{1,0:T(2,128)}, u32[]{:S(2)}) copy-start(f32[2,1024]{1,0:T(2,128)} %param.13) | copy-start | bytes 24580
  67.4 8.6 %copy-start.9 = (f32[2,1024]{1,0:T(2,128)S(1)}, f32[2,1024]{1,0:T(2,128)}, u32[]{:S(2)}) copy-start(f32[2,1024]{1,0:T(2,128)} %param.14) | copy-start | bytes 24580
  67.4 5.4 %collective-permute-start.7 = (f32[512]{0:T(512)S(1)}, f32[512]{0:T(512)S(1)}, u32[]{:S(2)}, u32[]{:S(2)}) collective-permute-start(f32[512]{0:T(512)S(1)} %multiply_reduce_fusion.2), channel_id=1, source_target_pairs={{12,0},{13,1},{6,2},{7,3},{0,4},{1,5},{10,6},{11,7},{4,8},{5,9},{1... | collective-permute-start | bytes 6152 | tf_op jit(solution)/shard_map/ppermute | solution.py:92
  67.4 5.4 %collective-permute-start.8 = (f32[512]{0:T(512)S(1)}, f32[512]{0:T(512)S(1)}, u32[]{:S(2)}, u32[]{:S(2)}) collective-permute-start(f32[512]{0:T(512)S(1)} %multiply_reduce_fusion.2), channel_id=1, source_target_pairs={{12,1},{13,0},{6,3},{7,2},{0,5},{1,4},{10,7},{11,6},{4,9},{5,8},{1... | collective-permute-start | bytes 6152 | tf_op jit(solution)/shard_map/ppermute | solution.py:93
  70.2 3.5 %collective-permute-start.4 = (f32[512]{0:T(512)S(1)}, f32[512]{0:T(512)S(1)}, u32[]{:S(2)}, u32[]{:S(2)}) collective-permute-start(f32[512]{0:T(512)S(1)} %multiply_reduce_fusion.3), channel_id=1, source_target_pairs={{0,3},{1,2},{2,1},{3,0},{4,7},{5,6},{6,5},{7,4},{8,11},{9,10},{10,... | collective-permute-start | bytes 6152 | tf_op jit(solution)/shard_map/ppermute | solution.py:91
  72.4 3.6 %collective-permute-start.3 = (f32[512]{0:T(512)S(1)}, f32[512]{0:T(512)S(1)}, u32[]{:S(2)}, u32[]{:S(2)}) collective-permute-start(f32[512]{0:T(512)S(1)} %multiply_reduce_fusion.3), channel_id=1, source_target_pairs={{0,2},{1,3},{2,0},{3,1},{4,6},{5,7},{6,4},{7,5},{8,10},{9,11},{10,... | collective-permute-start | bytes 6152 | tf_op jit(solution)/shard_map/ppermute | solution.py:90

commit v2 on v1

v2 whole, which is shorter than its diff:
```python
import functools
import jax
import jax.numpy as jnp
from jax import lax
from jax.experimental import pallas as pl
from jax.experimental.pallas import tpu as pltpu
from jax.sharding import PartitionSpec as P

NX = 32
LANES = 128
VMEM = pl.BlockSpec(memory_space=pltpu.VMEM)
SMEM = pl.BlockSpec(memory_space=pltpu.SMEM)
MIB = 2**20


def call(kernel, outs, specs, name, scratch=(), limit=16, flops=0, moved=0):
    return pl.pallas_call(
        kernel,
        out_shape=outs,
        in_specs=specs,
        out_specs=jax.tree.map(lambda _: VMEM, outs),
        scratch_shapes=scratch,
        compiler_params=pltpu.CompilerParams(vmem_limit_bytes=limit * MIB),
        cost_estimate=pl.CostEstimate(flops=flops, bytes_accessed=moved, transcendentals=0),
        name=name,
    )


def dot(left, right):
    return jnp.dot(left, right, preferred_element_type=jnp.float32)


def own_kernel(place, field, near, far):
    odd, core = place[0], place[1]
    half = near.shape[1]
    step = 64
    for r in range(0, field.shape[0], step):
        rows = pl.ds(r, step)
        for k in range(2):

            @pl.when(core == k)
            def _():
                first = field[rows, 0, k * half : (k + 1) * half]
                second = field[rows, 1, k * half : (k + 1) * half]
                near[rows, :] = jnp.where(odd == 1, second, first)
                far[rows, :] = jnp.where(odd == 1, first, second)


def give_kernel(place, field, give, rim):
    odd, core = place[0], place[1]
    half = field.shape[2] // 2
    step = 64
    for r in range(0, field.shape[0], step):
        rows = pl.ds(r, step)
        for k in range(2):

            @pl.when(core == k)
            def _():
                first = field[rows, 0, :]
                second = field[rows, 1, :]
                near = jnp.where(odd == 1, second, first)
                far = jnp.where(odd == 1, first, second)
                other = slice((1 - k) * half, (2 - k) * half)
                mine = slice(half - LANES, half) if k == 0 else slice(half, half + LANES)
                theirs = slice(half, half + LANES) if k == 0 else slice(half - LANES, half)
                give[rows, :half] = near[:, other]
                give[rows, half : 2 * half] = far[:, other]
                give[rows, 2 * half : 2 * half + LANES] = near[:, mine]
                give[rows, 2 * half + LANES :] = far[:, mine]
                rim[rows, :LANES] = near[:, theirs]
                rim[rows, LANES:] = far[:, theirs]


def cross_kernel(weights, out):
    n = out.shape[0]
    out[...] = (weights[n:, :n].astype(jnp.float32) + weights[:n, n:].astype(jnp.float32).T).astype(out.dtype)


def x_change(block):
    x = lax.rem(lax.broadcasted_iota(jnp.int32, block.shape, 1), NX)
    back = pltpu.roll(block, 2, 1)
    return jnp.where(x == 0, 0.0, block) - jnp.where(x == 1, 0.0, back)


def y_change(blocks, rim, first):
    lane = lax.broadcasted_iota(jnp.int32, rim.shape, 1)
    turned = [pltpu.roll(block, 2 * NX, 1) for block in blocks]
    above = jnp.where(first, rim, 0.0)
    below = jnp.where(first, 0.0, pltpu.roll(rim, 2 * NX, 1))
    out = []
    for b, block in enumerate(blocks):
        if b == 0:
            upper = jnp.where(lane < NX, above, block)
            lower = jnp.where(lane < NX, turned[-1], jnp.where(lane < 2 * NX, below, turned[0]))
        else:
            upper = block
            lower = jnp.where(lane < 2 * NX, turned[b - 1], turned[b])
        out.append(upper - lower)
    return out


def plane_kernel(place, near, far, rim, other, weights, cross, out, delta):
    first = place[1] == 0
    rows, half = near.shape
    count = half // LANES
    step = 128
    for layer, own in enumerate((near, far)):
        for group in range(2):
            for r in range(0, rows, step):
                if group == 0:
                    body = own[r : r + step, :]
                    edge = rim[r : r + step, layer * LANES : (layer + 1) * LANES]
                else:
                    body = other[r : r + step, layer * half : (layer + 1) * half]
                    at = 2 * half + layer * LANES
                    edge = other[r : r + step, at : at + LANES]
                body, edge = body.astype(jnp.float32), edge.astype(jnp.float32)
                blocks = [body[:, b * LANES : (b + 1) * LANES] for b in range(count)]
                along_y = y_change(blocks, edge, first)
                along_x = [x_change(block) for block in blocks]
                at = group * rows + r
                delta[0, at : at + step, :] = jnp.concatenate(along_y, axis=1).astype(jnp.bfloat16)
                delta[1, at : at + step, :] = jnp.concatenate(along_x, axis=1).astype(jnp.bfloat16)
        for part in range(2):
            total = jnp.zeros((8, half), jnp.float32)
            for at in range(0, 2 * rows, 256):
                grads = delta[part, at : at + 256, :]
                if at < rows:
                    mixed = dot(weights[at : at + 256, :rows], delta[part, :rows, :])
                else:
                    mixed = dot(weights[at : at + 256, rows:], delta[part, rows:, :])
                    mixed = mixed + dot(cross[at - rows : at - rows + 256, :], delta[part, :rows, :])
                total = total + jnp.sum((grads.astype(jnp.float32) * mixed).reshape(-1, 8, half), axis=0)
            total = 0.25 * jnp.sum(total, axis=0, keepdims=True)
            if part == 0:
                total = pltpu.roll(jnp.broadcast_to(total, (8, half)), half - NX, 1)
            else:
                total = jnp.broadcast_to(total, (8, half))
                total = jnp.concatenate(
                    [pltpu.roll(total[:, b * LANES : (b + 1) * LANES], LANES - 1, 1) for b in range(count)], axis=1
                )
            out[2 * layer + part : 2 * layer + part + 1, :] = total[:1]


def differences(place, far, near_in, far_in, rows):
    inside = place[2] == 1
    near_v = near_in[rows, :].astype(jnp.float32)
    change_a = far[rows, :].astype(jnp.float32) - near_v
    change_b = far_in[rows, :].astype(jnp.float32) - jnp.where(inside, near_v, 0.0)
    return change_a.astype(jnp.bfloat16), change_b.astype(jnp.bfloat16)


def early_kernel(place, far, near_in, far_in, weights, cross, carry, out, delta):
    rows, half = far.shape
    for r in range(0, rows, 128):
        at = pl.ds(r, 128)
        delta[at, :half], delta[at, half:] = differences(place, far, near_in, far_in, at)
    total = jnp.zeros((8, 2 * half), jnp.float32)
    for r in range(0, rows, 256):
        mixed = dot(weights[r : r + 256, :rows], delta[...])
        carry[r : r + 256, :] = dot(cross[r : r + 256, :], delta[...])
        total = total + jnp.sum((delta[r : r + 256, :].astype(jnp.float32) * mixed).reshape(-1, 8, 2 * half), axis=0)
    out[...] = total


def late_kernel(place, far, near_in, far_in, weights, carry, early, out_a, out_b, delta):
    rows, half = far.shape
    for r in range(0, rows, 128):
        at = pl.ds(r, 128)
        delta[at, :half], delta[at, half:] = differences(place, far, near_in, far_in, at)
    total = early[...]
    for r in range(0, rows, 256):
        mixed = carry[r : r + 256, :] + dot(weights[rows + r : rows + r + 256, rows:], delta[...])
        total = total + jnp.sum((delta[r : r + 256, :].astype(jnp.float32) * mixed).reshape(-1, 8, 2 * half), axis=0)
    total = 0.25 * jnp.sum(total, axis=0, keepdims=True)
    out_a[...] = total[:, :half]
    out_b[...] = total[:, half:]


def assemble(quadripoles, weighted_misfit, order):
    left_side = (quadripoles[:, 0][None, :] == order[:, None]).astype(jnp.bfloat16) - (
        quadripoles[:, 1][None, :] == order[:, None]
    ).astype(jnp.bfloat16)
    third = quadripoles[:, 2][:, None] == order[None, :]
    fourth = quadripoles[:, 3][:, None] == order[None, :]
    signed = third.astype(jnp.float32) - fourth.astype(jnp.float32)
    right_side = (weighted_misfit.astype(jnp.float32)[:, None] * signed).astype(jnp.bfloat16)
    return dot(left_side, right_side).astype(jnp.bfloat16)


def local(potentials, elec_order, quadripoles, weighted_misfit, salinity, water_content, cementation, anisotropy):
    blocks = lax.axis_size("space")
    s = lax.axis_index("space")
    c = lax.axis_index("elec")
    rows, layers, cells = potentials.shape
    half = cells // 2
    odd = lax.rem(s, 2)
    to_mate = [(i, i ^ 1) for i in range(blocks)]
    back_two = [(i, (i - 2) % blocks if i % 2 == 0 else (i + 2) % blocks) for i in range(blocks)]
    swap = [(0, 1), (1, 0)]
    inside = jnp.where(odd == 1, s >= 2, s + 2 < blocks)
    place = jnp.stack([odd, c, inside.astype(jnp.int32)]).astype(jnp.int32)
    shape = jax.ShapeDtypeStruct
    bf16, f32 = jnp.bfloat16, jnp.float32

    near, far = call(
        own_kernel, (shape((rows, half), bf16), shape((rows, half), bf16)), [SMEM, VMEM], "own", moved=rows * cells * 4
    )(place, potentials)
    near_in_0 = lax.ppermute(near, "space", to_mate)
    far_in_0 = lax.ppermute(far, "space", back_two)

    give, rim = call(
        give_kernel,
        (shape((rows, 2 * half + 2 * LANES), bf16), shape((rows, 2 * LANES), bf16)),
        [SMEM, VMEM],
        "give",
        moved=rows * cells * 4,
    )(place, potentials)
    other = lax.ppermute(give, "elec", swap)
    near_2 = other[:, :half]
    far_2 = other[:, half : 2 * half]
    near_in_1 = lax.ppermute(near_2, "space", to_mate)
    far_in_1 = lax.ppermute(far_2, "space", back_two)

    order = jnp.where(c == 0, elec_order, jnp.concatenate([elec_order[rows:], elec_order[:rows]]))
    weights = assemble(quadripoles, weighted_misfit, order)
    cross = call(cross_kernel, shape((rows, rows), bf16), [VMEM], "cross", moved=4 * rows * rows * 2)(weights)

    big = 2 * rows * rows * half * 2
    forms = call(
        plane_kernel,
        shape((2 * layers, half), f32),
        [SMEM] + [VMEM] * 6,
        "plane",
        scratch=[pltpu.VMEM((2, 2 * rows, half), bf16)],
        flops=big * 6,
        moved=rows * cells * 16,
    )(place, near, far, rim, other, weights, cross)

    bulk = 0.15 * salinity * water_content**cementation
    forms = jnp.where(odd == 1, jnp.concatenate([forms[2:], forms[:2]]), forms)
    mine = jnp.where(c == 0, anisotropy[1:, :, :half], anisotropy[1:, :, half:])
    flat = mine[0] * forms[0::2] + mine[1] * forms[1::2]
    flat_other = lax.ppermute(flat, "elec", swap)

    carry, early = call(
        early_kernel,
        (shape((rows, 2 * half), f32), shape((8, 2 * half), f32)),
        [SMEM] + [VMEM] * 5,
        "early",
        scratch=[pltpu.VMEM((rows, 2 * half), bf16)],
        flops=big * 4,
        moved=rows * cells * 16,
    )(place, far, near_in_0, far_in_0, weights, cross)
    form_a, form_b = call(
        late_kernel,
        (shape((1, half), f32), shape((1, half), f32)),
        [SMEM] + [VMEM] * 6,
        "late",
        scratch=[pltpu.VMEM((rows, 2 * half), bf16)],
        flops=big * 2,
        moved=rows * cells * 16,
    )(place, far_2, near_in_1, far_in_1, weights, carry, early)

    def joint(pairs, cross):
        return [(2 * i + k, 2 * j + (k ^ cross)) for i, j in pairs for k in range(2)]

    ahead_two = [(j, i) for i, j in back_two]
    both = ("space", "elec")
    a_same = lax.ppermute(form_a, both, joint(to_mate, 0))
    a_cross = lax.ppermute(form_a, both, joint(to_mate, 1))
    b_same = lax.ppermute(form_b, both, joint(ahead_two, 0))
    b_cross = lax.ppermute(form_b, both, joint(ahead_two, 1))

    def whole(same, cross):
        return jnp.where(c == 0, jnp.concatenate([same, cross], -1), jnp.concatenate([cross, same], -1))

    from_mate = whole(a_same, a_cross)
    from_far = whole(b_same, b_cross)
    form_z = jnp.where(odd == 1, jnp.concatenate([from_mate, from_far]), jnp.concatenate([from_far, from_mate]))
    sensitivity = bulk * (anisotropy[0] * form_z + whole(flat, flat_other))
    return sensitivity / salinity, cementation * sensitivity / water_content


def solution(mesh):
    split = P(("slab", "space"), None)
    placed = (P("elec", ("slab", "space"), None), P(), P(), P("slab"), split, split, split, P(None, ("slab", "space"), None))
    return jax.shard_map(local, mesh=mesh, in_specs=placed, out_specs=(split, split), check_vma=False)
```

time: 77.8 us -> 57.2 us (0.74)
  Pallas kernels: 0 us -> 19.7 us
  local copies, waits for them, and re-layouts: 26.6 us -> 7.33 us
  matrix products: 17.7 us -> 2.8 us
  other arithmetic: 9.63 us -> 1.42 us
  waiting for transfers between devices: 7.41 us -> 10.2 us
    pallas_call x0 -> x6, Pallas kernels: none -> 19.7 us  [the longest x1 5.88 us: local(): call(plane_kernel, shape((2 * layers, half), f32), [SMEM] + [VMEM] * 6, '...]
    dot_general x5 -> x1, matrix products: 17.7 us -> 2.8 us  [dot(): return jnp.dot(left, right, preferred_element_type=jnp.float32)]
    reshape x5 -> x0, local copies, waits for them, and re-layouts: 10.3 us -> none  [the longest x1 4.1 us: local(): half_difference(pad_x[..., 2:], pad_x[..., :-2]).reshape(2 * rows, -1)]
    dynamic_slice x3 -> x0, local copies, waits for them, and re-layouts: 7.42 us -> none  [the longest x1 3.65 us: cut(): lax.dynamic_slice(array, (0, layer, start), (rows, 1, width))]
    convert_element_type x2 -> x0, other arithmetic: 5.13 us -> none  [half_difference(): (0.5 * (upper.astype(jnp.float32) - lower.astype(jnp.float32))).astype(jn...]
    concatenate x2 -> x0, local copies, waits for them, and re-layouts: 4.07 us -> none  [the longest x1 2.99 us: local(): jnp.concatenate([own, other], axis=0)]
    ppermute x1, waiting for transfers between devices: 4 us -> 0.01 us  [local(): near_in_0 = lax.ppermute(near, 'space', to_mate)]
    ppermute x1, waiting for transfers between devices: 0.01 us -> 3.35 us  [local(): b_cross = lax.ppermute(form_b, both, joint(ahead_two, 1))]
  transfers between devices with their start and end apart: 10 -> 10, of which waited for: 4 -> 6; matrix products, arithmetic and copies ran while one was open for 61% -> 5% of each run, Pallas kernels for 0% -> 26%
where the time goes in v2:
time: 57.2 us; the launch traced here: 56.9 us
  Pallas kernels  19.7 us (34%)
  starting transfers between devices  14.6 us (26%)
  waiting for transfers between devices  10.2 us (18%)
  local copies, waits for them, and re-layouts  7.33 us (13%)
  matrix products  2.8 us (5%)
  other arithmetic  1.42 us (2%)
  between operations  0.83 us (1%)
    pallas_call x1, Pallas kernels, local(): call(plane_kernel, shape((2 * layers, half), f32), [SMEM] + [VMEM] * 6, '...  5.88 us
    pallas_call x1, Pallas kernels, local(): call(give_kernel, (shape((rows, 2 * half + 2 * LANES), bf16), shape((rows...  5.84 us
    unnamed x28, local copies, waits for them, and re-layouts  5.09 us
    ppermute x1, starting transfers between devices, local(): far_in_0 = lax.ppermute(far, 'space', back_two)  3.6 us
    ppermute x1, waiting for transfers between devices, local(): b_cross = lax.ppermute(form_b, both, joint(ahead_two, 1))  3.35 us
    pallas_call x1, Pallas kernels, local(): call(own_kernel, (shape((rows, half), bf16), shape((rows, half), bf16)),...  3.23 us
    ppermute x1, starting transfers between devices, local(): far_in_1 = lax.ppermute(far_2, 'space', back_two)  3.04 us
    ppermute x1, starting transfers between devices, local(): near_in_0 = lax.ppermute(near, 'space', to_mate)  3.03 us
  transfers between devices with their start and end apart: 10, of which 6 were waited for; matrix products, arithmetic and copies ran while one was open for 5% of the time, Pallas kernels for 26%

profile of v2, /device:TPU:0, one launch (start us, length us, event | category | flops | bytes accessed | tf_op | source)
XLA Modules:
  0.0 56.9 jit_solution(280984277038113237)
XLA Ops:
  0.6 0.1 pad_add_fusion.place
  0.7 1.6 %copy-done = bf16[512,2,1024]{2,1,0:T(2,128)(2,1)S(1)} copy-done((bf16[512,2,1024]{2,1,0:T(2,128)(2,1)S(1)}, bf16[512,2,1024]{2,1,0:T(2,128)(2,1)}, u32[]{:S(2)}) %copy-start) | copy-done | bytes 2097176
  2.3 3.2 %own.1 = (bf16[512,512]{1,0:T(8,128)(2,1)S(1)}, bf16[512,512]{1,0:T(8,128)(2,1)S(1)}) custom-call(s32[3]{0:T(128)S(1)} %pad_add_fusion.place, bf16[512,2,1024]{2,1,0:T(2,128)(2,1)S(1)} %copy-done), custom_call_target="tpu_custom_call" | custom-call | bytes 2097152 | tf_op jit(solution)/shard_map/own/pallas_call | solution.py:206
  5.6 0.0 copy-start.3
  5.6 0.0 copy-start.5
  5.6 3.0 %collective-permute-start.3 = (bf16[512,512]{1,0:T(8,128)(2,1)S(1)}, bf16[512,512]{1,0:T(8,128)(2,1)}, u32[]{:S(2)}, u32[]{:S(2)}) collective-permute-start(bf16[512,512]{1,0:T(8,128)(2,1)S(1)} %get-tuple-element.12.near), channel_id=1, source_target_pairs={{0,2},{2,0},{4,6},{6,4},{8,10},{10,8},{12,14},{14,12},{1,3},{3,1},... | collective-permute-start | bytes 1572872 | tf_op jit(solution)/shard_map/ppermute | solution.py:209
  8.6 3.6 %collective-permute-start.4 = (bf16[512,512]{1,0:T(8,128)(2,1)S(1)}, bf16[512,512]{1,0:T(8,128)(2,1)}, u32[]{:S(2)}, u32[]{:S(2)}) collective-permute-start(bf16[512,512]{1,0:T(8,128)(2,1)S(1)} %get-tuple-element.11.far), channel_id=1, source_target_pairs={{0,12},{2,6},{4,0},{6,10},{8,4},{10,14},{12,8},{14,2},{1,13},{3,7}... | collective-permute-start | bytes 1572872 | tf_op jit(solution)/shard_map/ppermute | solution.py:210
  12.2 5.8 %give.1 = (bf16[512,1280]{1,0:T(8,128)(2,1)}, bf16[512,256]{1,0:T(8,128)(2,1)S(1)}) custom-call(s32[3]{0:T(128)S(1)} %pad_add_fusion.place, bf16[512,2,1024]{2,1,0:T(2,128)(2,1)S(1)} %copy-done), custom_call_target="tpu_custom_call" | custom-call | bytes 2097152 | tf_op jit(solution)/shard_map/give/pallas_call | solution.py:212
  18.0 0.0 collective-permute-start
  18.0 0.0 copy-done.9
  18.1 0.0 copy-done.13
  18.1 0.0 copy-done.10
  18.1 2.8 %fusion.10.weights = bf16[1024,1024]{1,0:T(8,128)(2,1)S(1)} fusion(s32[1024]{0:T(1024)S(1)} %add_select_fusion, f32[1024]{0:T(1024)S(1)} %convert_element_type.24, s32[1024]{0:T(1024)S(1)} %bitcast.24, s32[1024]{0:T(1024)S(1)} %bitcast.25, s32[1024]{0:T(1024)S(1)} %bitcast.23, s32[1024]{0:T(1024)S(1)} %bitcast.22), kind=kOutput, calls=%fused_computation.12 | convolution fusion | flops 2161115136 | bytes 2121728 | tf_op jit(solution)/shard_map/dot_general | solution.py:30
  20.9 0.0 copy-done.3
  20.9 0.0 copy-start.8
  21.0 0.2 cross.1
  21.2 0.5 copy-done.8
  21.7 0.0 collective-permute-done.3.near_in
  21.7 1.4 %collective-permute-done.4.far_in = bf16[512,512]{1,0:T(8,128)(2,1)} collective-permute-done((bf16[512,512]{1,0:T(8,128)(2,1)S(1)}, bf16[512,512]{1,0:T(8,128)(2,1)}, u32[]{:S(2)}, u32[]{:S(2)}) %collective-permute-start.4) | collective-permute-done | bytes 524320 | tf_op jit(solution)/shard_map/ppermute | solution.py:210
  23.1 0.0 copy-done.5
  23.1 2.6 %early.1 = (f32[512,1024]{1,0:T(8,128)S(1)}, f32[8,1024]{1,0:T(8,128)S(1)}) custom-call(s32[3]{0:T(128)S(1)} %pad_add_fusion.place, bf16[512,512]{1,0:T(8,128)(2,1)S(1)} %get-tuple-element.11.far, bf16[512,512]{1,0:T(8,128)(2,1)} %collective-permute-done.3.near_in, bf16[512,512]{1,0:T(8,128)(2,1)} %collective-permute-done.4.far_in, ...), custom_call_target="tpu_custom_call" | custom-call | flops 2147483648 | bytes 8388608 | tf_op jit(solution)/shard_map/early/pallas_call | solution.py:246
  25.7 0.0 copy-start.1
  25.7 1.4 %copy-done.1 = f32[512,1024]{1,0:T(8,128)} copy-done((f32[512,1024]{1,0:T(8,128)}, f32[512,1024]{1,0:T(8,128)S(1)}, u32[]{:S(2)}) %copy-start.1) | copy-done | bytes 2097176
  27.1 0.0 collective-permute-done.other
  27.1 2.2 %fusion.20 = (bf16[512,512]{1,0:T(8,128)(2,1)}, bf16[512,512]{1,0:T(8,128)(2,1)S(1)}) fusion(bf16[512,1280]{1,0:T(8,128)(2,1)} %collective-permute-done.other), kind=kLoop, calls=%fused_computation.30 | loop fusion | bytes 2097152 | tf_op jit(solution)/shard_map/slice | solution.py:220
  29.2 1.4 %collective-permute-start.1 = (bf16[512,512]{1,0:T(8,128)(2,1)}, bf16[512,512]{1,0:T(8,128)(2,1)S(1)}, u32[]{:S(2)}, u32[]{:S(2)}) collective-permute-start(bf16[512,512]{1,0:T(8,128)(2,1)} %get-tuple-element.20), channel_id=1, source_target_pairs={{0,2},{2,0},{4,6},{6,4},{8,10},{10,8},{12,14},{14,12},{1,3},{3,1},... | collective-permute-start | bytes 1572872 | tf_op jit(solution)/shard_map/ppermute | solution.py:222
  30.6 3.0 %collective-permute-start.2 = (bf16[512,512]{1,0:T(8,128)(2,1)S(1)}, bf16[512,512]{1,0:T(8,128)(2,1)}, u32[]{:S(2)}, u32[]{:S(2)}) collective-permute-start(bf16[512,512]{1,0:T(8,128)(2,1)S(1)} %get-tuple-element.21.far), channel_id=1, source_target_pairs={{0,12},{2,6},{4,0},{6,10},{8,4},{10,14},{12,8},{14,2},{1,13},{3,7}... | collective-permute-start | bytes 1572872 | tf_op jit(solution)/shard_map/ppermute | solution.py:223
  33.6 0.0 copy-done.4
  33.6 0.0 copy-done.6
  33.6 5.9 %plane.1 = f32[4,512]{1,0:T(4,128)S(1)} custom-call(s32[3]{0:T(128)S(1)} %pad_add_fusion.place, bf16[512,512]{1,0:T(8,128)(2,1)S(1)} %copy-done.4, bf16[512,512]{1,0:T(8,128)(2,1)S(1)} %copy-done.6, bf16[512,256]{1,0:T(8,128)(2,1)S(1)} %get-tuple-element.17.rim, bf16[512,1280]{1,0:T(8,128)(2,1)} %collective-permute-done.other, ...), custom_call_target="tpu_custom_call" | custom-call | flops 3221225472 | bytes 8388608 | tf_op jit(solution)/shard_map/plane/pallas_call | solution.py:230
  39.6 2.8 %collective-permute-done.1.near_in = bf16[512,512]{1,0:T(8,128)(2,1)S(1)} collective-permute-done((bf16[512,512]{1,0:T(8,128)(2,1)}, bf16[512,512]{1,0:T(8,128)(2,1)S(1)}, u32[]{:S(2)}, u32[]{:S(2)}) %collective-permute-start.1) | collective-permute-done | bytes 524320 | tf_op jit(solution)/shard_map/ppermute | solution.py:222
  42.4 1.2 %collective-permute-done.2.far_in = bf16[512,512]{1,0:T(8,128)(2,1)} collective-permute-done((bf16[512,512]{1,0:T(8,128)(2,1)S(1)}, bf16[512,512]{1,0:T(8,128)(2,1)}, u32[]{:S(2)}, u32[]{:S(2)}) %collective-permute-start.2) | collective-permute-done | bytes 524320 | tf_op jit(solution)/shard_map/ppermute | solution.py:223
  43.6 1.6 %copy-done.2 = f32[512,1024]{1,0:T(8,128)S(1)} copy-done((f32[512,1024]{1,0:T(8,128)S(1)}, f32[512,1024]{1,0:T(8,128)}, u32[]{:S(2)}) %copy-start.2) | copy-done | bytes 2097176
  45.2 2.0 %late.1 = (f32[1,512]{1,0:T(1,128)S(1)}, f32[1,512]{1,0:T(1,128)S(1)}) custom-call(s32[3]{0:T(128)S(1)} %pad_add_fusion.place, bf16[512,512]{1,0:T(8,128)(2,1)S(1)} %get-tuple-element.21.far, bf16[512,512]{1,0:T(8,128)(2,1)S(1)} %collective-permute-done.1.near_in, bf16[512,512]{1,0:T(8,128)(2,1)} %collective-permute-done.2.far_in, ...), custom_call_target="tpu_custom_call" | custom-call | flops 1073741824 | bytes 8388608 | tf_op jit(solution)/shard_map/late/pallas_call | solution.py:255
  47.2 0.1 collective-permute-start.6
  47.3 2.7 %collective-permute-start.5 = (f32[1,512]{1,0:T(1,128)S(1)}, f32[1,512]{1,0:T(1,128)S(1)}, u32[]{:S(2)}, u32[]{:S(2)}) collective-permute-start(f32[1,512]{1,0:T(1,128)S(1)} %get-tuple-element.15), channel_id=1, source_target_pairs={{0,2},{1,3},{2,0},{3,1},{4,6},{5,7},{6,4},{7,5},{8,10},{9,11},{10,... | collective-permute-start | bytes 6152 | tf_op jit(solution)/shard_map/ppermute | solution.py:270
  50.0 0.1 collective-permute-start.9
  50.1 0.0 collective-permute-start.8
  50.1 0.7 %collective-permute-start.7 = (f32[1,512]{1,0:T(1,128)S(1)}, f32[1,512]{1,0:T(1,128)S(1)}, u32[]{:S(2)}, u32[]{:S(2)}) collective-permute-start(f32[1,512]{1,0:T(1,128)S(1)} %get-tuple-element.16), channel_id=1, source_target_pairs={{12,0},{13,1},{6,2},{7,3},{0,4},{1,5},{10,6},{11,7},{4,8},{5,9},{1... | collective-permute-start | bytes 6152 | tf_op jit(solution)/shard_map/ppermute | solution.py:272
  50.8 0.0 collective-permute-done.6
  50.8 0.7 %collective-permute-done.5 = f32[1,512]{1,0:T(1,128)S(1)} collective-permute-done((f32[1,512]{1,0:T(1,128)S(1)}, f32[1,512]{1,0:T(1,128)S(1)}, u32[]{:S(2)}, u32[]{:S(2)}) %collective-permute-start.5) | collective-permute-done | bytes 2080 | tf_op jit(solution)/shard_map/ppermute | solution.py:270
  51.5 3.4 %collective-permute-done.8 = f32[1,512]{1,0:T(1,128)S(1)} collective-permute-done((f32[1,512]{1,0:T(1,128)S(1)}, f32[1,512]{1,0:T(1,128)S(1)}, u32[]{:S(2)}, u32[]{:S(2)}) %collective-permute-start.8) | collective-permute-done | bytes 2080 | tf_op jit(solution)/shard_map/ppermute | solution.py:273
  54.9 0.6 %collective-permute-done.7 = f32[1,512]{1,0:T(1,128)S(1)} collective-permute-done((f32[1,512]{1,0:T(1,128)S(1)}, f32[1,512]{1,0:T(1,128)S(1)}, u32[]{:S(2)}, u32[]{:S(2)}) %collective-permute-start.7) | collective-permute-done | bytes 2080 | tf_op jit(solution)/shard_map/ppermute | solution.py:272
  55.5 0.0 collective-permute-done.9
  55.5 0.0 copy-done.7
  55.5 0.0 copy-done.11
  55.6 0.7 %multiply_divide_fusion = (f32[2,1024]{1,0:T(2,128)}, f32[2,1024]{1,0:T(2,128)S(1)}) fusion(f32[2,1024]{1,0:T(2,128)S(1)} %copy-done.11, f32[2,1024]{1,0:T(2,128)S(1)} %copy-done.12, f32[2,512]{1,0:T(2,128)S(1)} %fusion.17, f32[2,512]{1,0:T(2,128)S(1)} %collective-permute-done.9, pred[]{:T(512)S(6)} %eq.33, f32[1,1024]{1,0:T(1,128)S(1)} %broadcast_select_fusion.1, ...), kind=kLoop, calls=%fused_computation.19 | loop fusion | flops 26624 | bytes 65538 | tf_op jit(solution)/shard_map/div | solution.py:282
  56.2 0.6 %div.6 = f32[2,1024]{1,0:T(2,128)} divide(f32[2,1024]{1,0:T(2,128)S(1)} %get-tuple-element.19, f32[2,1024]{1,0:T(2,128)S(1)} %copy-done.7) | non-fusion elementwise | flops 2048 | bytes 24576 | tf_op jit(solution)/shard_map/div | solution.py:282
  (23 shorter events, 0.1 us)
Async XLA Ops:
  0.7 1.6 %copy-start = (bf16[512,2,1024]{2,1,0:T(2,128)(2,1)S(1)}, bf16[512,2,1024]{2,1,0:T(2,128)(2,1)}, u32[]{:S(2)}) copy-start(bf16[512,2,1024]{2,1,0:T(2,128)(2,1)} %field.3) | copy-start | bytes 6291460
  2.3 15.7 %copy-start.9 = (s32[1024]{0:T(1024)S(1)}, s32[1024]{0:T(1024)}, u32[]{:S(2)}) copy-start(s32[1024]{0:T(1024)} %param.9) | copy-start | bytes 12292
  2.3 15.8 %copy-start.13 = (bf16[1024]{0:T(1024)(128)(2,1)S(1)}, bf16[1024]{0:T(1024)(128)(2,1)}, u32[]{:S(2)}) copy-start(bf16[1024]{0:T(1024)(128)(2,1)} %param.11) | copy-start | bytes 6148
  2.3 15.8 %copy-start.10 = (s32[1024,4]{0,1:T(4,128)S(1)}, s32[1024,4]{0,1:T(4,128)}, u32[]{:S(2)}) copy-start(s32[1024,4]{0,1:T(4,128)} %param.10) | copy-start | bytes 49156
  5.6 15.4 %copy-start.3 = (bf16[512,512]{1,0:T(8,128)(2,1)}, bf16[512,512]{1,0:T(8,128)(2,1)S(1)}, u32[]{:S(2)}) copy-start(bf16[512,512]{1,0:T(8,128)(2,1)S(1)} %get-tuple-element.12.near) | copy-start | bytes 1572868
  5.6 17.6 %copy-start.5 = (bf16[512,512]{1,0:T(8,128)(2,1)}, bf16[512,512]{1,0:T(8,128)(2,1)S(1)}, u32[]{:S(2)}) copy-start(bf16[512,512]{1,0:T(8,128)(2,1)S(1)} %get-tuple-element.11.far) | copy-start | bytes 1572868
  5.6 16.1 %collective-permute-start.3 = (bf16[512,512]{1,0:T(8,128)(2,1)S(1)}, bf16[512,512]{1,0:T(8,128)(2,1)}, u32[]{:S(2)}, u32[]{:S(2)}) collective-permute-start(bf16[512,512]{1,0:T(8,128)(2,1)S(1)} %get-tuple-element.12.near), channel_id=1, source_target_pairs={{0,2},{2,0},{4,6},{6,4},{8,10},{10,8},{12,14},{14,12},{1,3},{3,1},... | collective-permute-start | bytes 1572872 | tf_op jit(solution)/shard_map/ppermute | solution.py:209
  8.6 14.5 %collective-permute-start.4 = (bf16[512,512]{1,0:T(8,128)(2,1)S(1)}, bf16[512,512]{1,0:T(8,128)(2,1)}, u32[]{:S(2)}, u32[]{:S(2)}) collective-permute-start(bf16[512,512]{1,0:T(8,128)(2,1)S(1)} %get-tuple-element.11.far), channel_id=1, source_target_pairs={{0,12},{2,6},{4,0},{6,10},{8,4},{10,14},{12,8},{14,2},{1,13},{3,7}... | collective-permute-start | bytes 1572872 | tf_op jit(solution)/shard_map/ppermute | solution.py:210
  18.0 9.0 %collective-permute-start = (bf16[512,1280]{1,0:T(8,128)(2,1)}, bf16[512,1280]{1,0:T(8,128)(2,1)}, u32[]{:S(2)}, u32[]{:S(2)}) collective-permute-start(bf16[512,1280]{1,0:T(8,128)(2,1)} %get-tuple-element.10), channel_id=1, source_target_pairs={{0,1},{1,0},{2,3},{3,2},{4,5},{5,4},{6,7},{7,6},{8,9},{9,8},{10,11... | collective-permute-start | bytes 3932168 | tf_op jit(solution)/shard_map/ppermute | solution.py:219
  20.9 0.7 %copy-start.8 = (f32[3,2,1024]{2,1,0:T(2,128)S(1)}, f32[3,2,1024]{2,1,0:T(2,128)}, u32[]{:S(2)}) copy-start(f32[3,2,1024]{2,1,0:T(2,128)} %param.15) | copy-start | bytes 73732
  25.7 1.4 %copy-start.1 = (f32[512,1024]{1,0:T(8,128)}, f32[512,1024]{1,0:T(8,128)S(1)}, u32[]{:S(2)}) copy-start(f32[512,1024]{1,0:T(8,128)S(1)} %get-tuple-element.13.carry) | copy-start | bytes 6291460
  27.1 6.6 %copy-start.4 = (bf16[512,512]{1,0:T(8,128)(2,1)S(1)}, bf16[512,512]{1,0:T(8,128)(2,1)}, u32[]{:S(2)}) copy-start(bf16[512,512]{1,0:T(8,128)(2,1)} %copy-done.3) | copy-start | bytes 1572868
  27.1 6.6 %copy-start.6 = (bf16[512,512]{1,0:T(8,128)(2,1)S(1)}, bf16[512,512]{1,0:T(8,128)(2,1)}, u32[]{:S(2)}) copy-start(bf16[512,512]{1,0:T(8,128)(2,1)} %copy-done.5) | copy-start | bytes 1572868
  29.2 13.2 %collective-permute-start.1 = (bf16[512,512]{1,0:T(8,128)(2,1)}, bf16[512,512]{1,0:T(8,128)(2,1)S(1)}, u32[]{:S(2)}, u32[]{:S(2)}) collective-permute-start(bf16[512,512]{1,0:T(8,128)(2,1)} %get-tuple-element.20), channel_id=1, source_target_pairs={{0,2},{2,0},{4,6},{6,4},{8,10},{10,8},{12,14},{14,12},{1,3},{3,1},... | collective-permute-start | bytes 1572872 | tf_op jit(solution)/shard_map/ppermute | solution.py:222
  30.6 13.0 %collective-permute-start.2 = (bf16[512,512]{1,0:T(8,128)(2,1)S(1)}, bf16[512,512]{1,0:T(8,128)(2,1)}, u32[]{:S(2)}, u32[]{:S(2)}) collective-permute-start(bf16[512,512]{1,0:T(8,128)(2,1)S(1)} %get-tuple-element.21.far), channel_id=1, source_target_pairs={{0,12},{2,6},{4,0},{6,10},{8,4},{10,14},{12,8},{14,2},{1,13},{3,7}... | collective-permute-start | bytes 1572872 | tf_op jit(solution)/shard_map/ppermute | solution.py:223
  43.6 1.6 %copy-start.2 = (f32[512,1024]{1,0:T(8,128)S(1)}, f32[512,1024]{1,0:T(8,128)}, u32[]{:S(2)}) copy-start(f32[512,1024]{1,0:T(8,128)} %copy-done.1) | copy-start | bytes 6291460
  45.2 10.3 %copy-start.7 = (f32[2,1024]{1,0:T(2,128)S(1)}, f32[2,1024]{1,0:T(2,128)}, u32[]{:S(2)}) copy-start(f32[2,1024]{1,0:T(2,128)} %param.12) | copy-start | bytes 24580
  45.2 10.3 %copy-start.11 = (f32[2,1024]{1,0:T(2,128)S(1)}, f32[2,1024]{1,0:T(2,128)}, u32[]{:S(2)}) copy-start(f32[2,1024]{1,0:T(2,128)} %param.13) | copy-start | bytes 24580
  45.2 10.3 %copy-start.12 = (f32[2,1024]{1,0:T(2,128)S(1)}, f32[2,1024]{1,0:T(2,128)}, u32[]{:S(2)}) copy-start(f32[2,1024]{1,0:T(2,128)} %param.14) | copy-start | bytes 24580
  47.2 3.6 %collective-permute-start.6 = (f32[1,512]{1,0:T(1,128)S(1)}, f32[1,512]{1,0:T(1,128)S(1)}, u32[]{:S(2)}, u32[]{:S(2)}) collective-permute-start(f32[1,512]{1,0:T(1,128)S(1)} %get-tuple-element.15), channel_id=1, source_target_pairs={{0,3},{1,2},{2,1},{3,0},{4,7},{5,6},{6,5},{7,4},{8,11},{9,10},{10,... | collective-permute-start | bytes 6152 | tf_op jit(solution)/shard_map/ppermute | solution.py:271
  47.3 4.2 %collective-permute-start.5 = (f32[1,512]{1,0:T(1,128)S(1)}, f32[1,512]{1,0:T(1,128)S(1)}, u32[]{:S(2)}, u32[]{:S(2)}) collective-permute-start(f32[1,512]{1,0:T(1,128)S(1)} %get-tuple-element.15), channel_id=1, source_target_pairs={{0,2},{1,3},{2,0},{3,1},{4,6},{5,7},{6,4},{7,5},{8,10},{9,11},{10,... | collective-permute-start | bytes 6152 | tf_op jit(solution)/shard_map/ppermute | solution.py:270
  50.0 5.6 %collective-permute-start.9 = (f32[2,512]{1,0:T(2,128)S(1)}, f32[2,512]{1,0:T(2,128)S(1)}, u32[]{:S(2)}, u32[]{:S(2)}) collective-permute-start(f32[2,512]{1,0:T(2,128)S(1)} %fusion.17), channel_id=1, source_target_pairs={{0,1},{1,0},{2,3},{3,2},{4,5},{5,4},{6,7},{7,6},{8,9},{9,8},{10,11... | collective-permute-start | bytes 12296 | tf_op jit(solution)/shard_map/ppermute | solution.py:244
  50.1 4.8 %collective-permute-start.8 = (f32[1,512]{1,0:T(1,128)S(1)}, f32[1,512]{1,0:T(1,128)S(1)}, u32[]{:S(2)}, u32[]{:S(2)}) collective-permute-start(f32[1,512]{1,0:T(1,128)S(1)} %get-tuple-element.16), channel_id=1, source_target_pairs={{12,1},{13,0},{6,3},{7,2},{0,5},{1,4},{10,7},{11,6},{4,9},{5,8},{1... | collective-permute-start | bytes 6152 | tf_op jit(solution)/shard_map/ppermute | solution.py:273
  50.1 5.5 %collective-permute-start.7 = (f32[1,512]{1,0:T(1,128)S(1)}, f32[1,512]{1,0:T(1,128)S(1)}, u32[]{:S(2)}, u32[]{:S(2)}) collective-permute-start(f32[1,512]{1,0:T(1,128)S(1)} %get-tuple-element.16), channel_id=1, source_target_pairs={{12,0},{13,1},{6,2},{7,3},{0,4},{1,5},{10,6},{11,7},{4,8},{5,9},{1... | collective-permute-start | bytes 6152 | tf_op jit(solution)/shard_map/ppermute | solution.py:272

commit v3 on v2

v3 whole, which is shorter than its diff:
```python
import functools
import jax
import jax.numpy as jnp
from jax import lax
from jax.experimental import pallas as pl
from jax.experimental.pallas import tpu as pltpu
from jax.sharding import PartitionSpec as P

NX = 32
LANES = 128
VMEM = pl.BlockSpec(memory_space=pltpu.VMEM)
SMEM = pl.BlockSpec(memory_space=pltpu.SMEM)
MIB = 2**20
LATER = True
AFTER = True


def call(kernel, outs, specs, name, scratch=(), limit=8, flops=0, moved=0):
    return pl.pallas_call(
        kernel,
        out_shape=outs,
        in_specs=specs,
        out_specs=jax.tree.map(lambda _: VMEM, outs),
        scratch_shapes=scratch,
        compiler_params=pltpu.CompilerParams(vmem_limit_bytes=limit * MIB),
        cost_estimate=pl.CostEstimate(flops=flops, bytes_accessed=moved, transcendentals=0),
        name=name,
    )


def dot(left, right):
    return jnp.dot(left, right, preferred_element_type=jnp.float32)


def keep_kernel(place, field, near, far):
    odd, core = place[0], place[1]
    half = near.shape[1]
    for k in range(2):

        @pl.when(core == k)
        def _():
            near[...] = field[1 - odd, :, k * half : (k + 1) * half]
            far[...] = field[odd, :, k * half : (k + 1) * half]


def give_kernel(place, field, near, far, edge, rim):
    odd, core = place[0], place[1]
    half = near.shape[1]
    for k in range(2):
        low, high = slice(half - LANES, half), slice(half, half + LANES)
        inner, outer = (low, high) if k == 0 else (high, low)

        @pl.when(core == k)
        def _():
            near[...] = field[1 - odd, :, (1 - k) * half : (2 - k) * half]
            far[...] = field[odd, :, (1 - k) * half : (2 - k) * half]

            @pl.loop(0, field.shape[1], step=64)
            def _(r):
                rows = pl.ds(pl.multiple_of(r, 64), 64)
                edge[rows, :LANES] = field[1 - odd, rows, inner]
                edge[rows, LANES:] = field[odd, rows, inner]
                rim[rows, :LANES] = field[1 - odd, rows, outer]
                rim[rows, LANES:] = field[odd, rows, outer]


def cross_kernel(weights, out):
    n = out.shape[0]
    out[...] = (weights[n:, :n].astype(jnp.float32) + weights[:n, n:].astype(jnp.float32).T).astype(out.dtype)


def x_change(block):
    x = lax.rem(lax.broadcasted_iota(jnp.int32, block.shape, 1), NX)
    back = pltpu.roll(block, 2, 1)
    return jnp.where(x == 0, 0.0, block) - jnp.where(x == 1, 0.0, back)


def y_change(blocks, rim, first):
    lane = lax.broadcasted_iota(jnp.int32, rim.shape, 1)
    turned = [pltpu.roll(block, 2 * NX, 1) for block in blocks]
    above = jnp.where(first, rim, 0.0)
    below = jnp.where(first, 0.0, pltpu.roll(rim, 2 * NX, 1))
    out = []
    for b, block in enumerate(blocks):
        if b == 0:
            upper = jnp.where(lane < NX, above, block)
            lower = jnp.where(lane < NX, turned[-1], jnp.where(lane < 2 * NX, below, turned[0]))
        else:
            upper = block
            lower = jnp.where(lane < 2 * NX, turned[b - 1], turned[b])
        out.append(upper - lower)
    return out


def plane_kernel(place, near, far, rim, near_x, far_x, rim_x, weights, cross, out, delta):
    first = place[1] == 0
    rows, half = near.shape
    count = half // LANES
    step = 128
    for layer, own in enumerate(((near, near_x), (far, far_x))):
        for group in range(2):
            for r in range(0, rows, step):
                body = own[group][r : r + step, :]
                edge = (rim, rim_x)[group][r : r + step, layer * LANES : (layer + 1) * LANES]
                body, edge = body.astype(jnp.float32), edge.astype(jnp.float32)
                blocks = [body[:, b * LANES : (b + 1) * LANES] for b in range(count)]
                along_y = y_change(blocks, edge, first)
                along_x = [x_change(block) for block in blocks]
                at = group * rows + r
                delta[0, at : at + step, :] = jnp.concatenate(along_y, axis=1).astype(jnp.bfloat16)
                delta[1, at : at + step, :] = jnp.concatenate(along_x, axis=1).astype(jnp.bfloat16)
        for part in range(2):
            total = jnp.zeros((8, half), jnp.float32)
            for at in range(0, 2 * rows, 256):
                grads = delta[part, at : at + 256, :]
                if at < rows:
                    mixed = dot(weights[at : at + 256, :rows], delta[part, :rows, :])
                else:
                    mixed = dot(weights[at : at + 256, rows:], delta[part, rows:, :])
                    mixed = mixed + dot(cross[at - rows : at - rows + 256, :], delta[part, :rows, :])
                total = total + jnp.sum((grads.astype(jnp.float32) * mixed).reshape(-1, 8, half), axis=0)
            total = 0.25 * jnp.sum(total, axis=0, keepdims=True)
            if part == 0:
                total = pltpu.roll(jnp.broadcast_to(total, (8, half)), half - NX, 1)
            else:
                total = jnp.broadcast_to(total, (8, half))
                total = jnp.concatenate(
                    [pltpu.roll(total[:, b * LANES : (b + 1) * LANES], LANES - 1, 1) for b in range(count)], axis=1
                )
            out[2 * layer + part : 2 * layer + part + 1, :] = total[:1]


def differences(far, near_in, far_in, rows):
    near_v = near_in[rows, :].astype(jnp.float32)
    change_a = far[rows, :].astype(jnp.float32) - near_v
    change_b = far_in[rows, :].astype(jnp.float32) - near_v
    return change_a.astype(jnp.bfloat16), change_b.astype(jnp.bfloat16)


def early_kernel(far, near_in, far_in, weights, cross, carry, out, delta):
    rows, half = far.shape
    for r in range(0, rows, 128):
        at = pl.ds(r, 128)
        delta[at, :half], delta[at, half:] = differences(far, near_in, far_in, at)
    total = jnp.zeros((8, 2 * half), jnp.float32)
    for r in range(0, rows, 256):
        mixed = dot(weights[r : r + 256, :rows], delta[...])
        carry[r : r + 256, :] = dot(cross[r : r + 256, :], delta[...])
        total = total + jnp.sum((delta[r : r + 256, :].astype(jnp.float32) * mixed).reshape(-1, 8, 2 * half), axis=0)
    out[...] = total


def late_kernel(far, near_in, far_in, weights, carry, early, out_a, out_b, delta):
    rows, half = far.shape
    for r in range(0, rows, 128):
        at = pl.ds(r, 128)
        delta[at, :half], delta[at, half:] = differences(far, near_in, far_in, at)
    total = early[...]
    for r in range(0, rows, 256):
        mixed = carry[r : r + 256, :] + dot(weights[rows + r : rows + r + 256, rows:], delta[...])
        total = total + jnp.sum((delta[r : r + 256, :].astype(jnp.float32) * mixed).reshape(-1, 8, 2 * half), axis=0)
    total = 0.25 * jnp.sum(total, axis=0, keepdims=True)
    out_a[...] = total[:, :half]
    out_b[...] = total[:, half:]


def assemble(quadripoles, weighted_misfit, order):
    left_side = (quadripoles[:, 0][None, :] == order[:, None]).astype(jnp.bfloat16) - (
        quadripoles[:, 1][None, :] == order[:, None]
    ).astype(jnp.bfloat16)
    third = quadripoles[:, 2][:, None] == order[None, :]
    fourth = quadripoles[:, 3][:, None] == order[None, :]
    signed = third.astype(jnp.float32) - fourth.astype(jnp.float32)
    right_side = (weighted_misfit.astype(jnp.float32)[:, None] * signed).astype(jnp.bfloat16)
    return dot(left_side, right_side).astype(jnp.bfloat16)


def local(potentials, elec_order, quadripoles, weighted_misfit, salinity, water_content, cementation, anisotropy):
    blocks = lax.axis_size("space")
    s = lax.axis_index("space")
    c = lax.axis_index("elec")
    rows, layers, cells = potentials.shape
    half = cells // 2
    odd = lax.rem(s, 2)
    to_mate = [(i, i ^ 1) for i in range(blocks)]
    ahead = [(i, i - 2) for i in range(2, blocks, 2)] + [(i, i + 2) for i in range(1, blocks - 2, 2)]
    swap = [(0, 1), (1, 0)]
    place = jnp.stack([odd, c]).astype(jnp.int32)
    shape = jax.ShapeDtypeStruct
    bf16, f32 = jnp.bfloat16, jnp.float32
    both = ("space", "elec")

    def joint(pairs, cross):
        return [(2 * i + k, 2 * j + (k ^ cross)) for i, j in pairs for k in range(2)]

    field = jnp.transpose(potentials, (1, 0, 2))
    piece = shape((rows, half), bf16)
    strip = shape((rows, 2 * LANES), bf16)
    near, far = call(keep_kernel, (piece,) * 2, [SMEM, VMEM], "keep", moved=rows * cells * 4, limit=2)(place, field)
    near_in_0 = lax.ppermute(near, both, joint(to_mate, 0))
    far_in_0 = lax.ppermute(far, both, joint(ahead, 0))
    field, near, far = lax.optimization_barrier((field, near, far))
    near_give, far_give, edge, rim = call(
        give_kernel, (piece,) * 2 + (strip,) * 2, [SMEM, VMEM], "give", moved=rows * cells * 4, limit=2
    )(place, field)
    near_x = lax.ppermute(near_give, "elec", swap)
    far_x = lax.ppermute(far_give, "elec", swap)
    rim_x = lax.ppermute(edge, "elec", swap)

    order = jnp.where(c == 0, elec_order, jnp.concatenate([elec_order[rows:], elec_order[:rows]]))
    if AFTER:
        quadripoles, near_give = lax.optimization_barrier((quadripoles, near_give))
    weights = assemble(quadripoles, weighted_misfit, order)
    cross = call(cross_kernel, shape((rows, rows), bf16), [VMEM], "cross", moved=4 * rows * rows * 2)(weights)
    if LATER:
        near_give, far_give, weights = lax.optimization_barrier((near_give, far_give, weights))
    near_in_1 = lax.ppermute(near_give, both, joint(to_mate, 1))
    far_in_1 = lax.ppermute(far_give, both, joint(ahead, 1))

    big = 2 * rows * rows * half * 2
    forms = call(
        plane_kernel,
        shape((2 * layers, half), f32),
        [SMEM] + [VMEM] * 8,
        "plane",
        scratch=[pltpu.VMEM((2, 2 * rows, half), bf16)],
        limit=16,
        flops=big * 6,
        moved=rows * cells * 16,
    )(place, near, far, rim, near_x, far_x, rim_x, weights, cross)

    bulk = 0.15 * salinity * water_content**cementation
    salt_scale = bulk / salinity
    water_scale = bulk * cementation / water_content
    row = lax.broadcasted_iota(jnp.int32, (layers, cells), 0)
    is_near = row == 1 - odd
    is_mine = lax.broadcasted_iota(jnp.int32, (1, cells), 1) // half == c

    def spread(near_mine, near_other, far_mine, far_other):
        def line(mine, other):
            return jnp.where(is_mine, jnp.concatenate([mine, mine], 1), jnp.concatenate([other, other], 1))

        return jnp.where(is_near, line(near_mine, near_other), line(far_mine, far_other))

    forms_x = lax.ppermute(forms, "elec", swap)
    flat = anisotropy[1] * spread(forms[0:1], forms_x[0:1], forms[2:3], forms_x[2:3])
    flat = flat + anisotropy[2] * spread(forms[1:2], forms_x[1:2], forms[3:4], forms_x[3:4])
    salt_base, water_base = salt_scale * flat, water_scale * flat
    salt_scale, water_scale = salt_scale * anisotropy[0], water_scale * anisotropy[0]

    carry, early = call(
        early_kernel,
        (shape((rows, 2 * half), f32), shape((8, 2 * half), f32)),
        [VMEM] * 5,
        "early",
        scratch=[pltpu.VMEM((rows, 2 * half), bf16)],
        flops=big * 4,
        moved=rows * cells * 16,
    )(far, near_in_0, far_in_0, weights, cross)
    early, salt_base, water_base, salt_scale, water_scale = lax.optimization_barrier(
        (early, salt_base, water_base, salt_scale, water_scale)
    )
    form_a, form_b = call(
        late_kernel,
        (shape((1, half), f32), shape((1, half), f32)),
        [VMEM] * 6,
        "late",
        scratch=[pltpu.VMEM((rows, 2 * half), bf16)],
        flops=big * 2,
        moved=rows * cells * 16,
    )(far_x, near_in_1, far_in_1, weights, carry, early)

    b_cross = lax.ppermute(form_b, both, joint(to_mate, 1))
    b_same = lax.ppermute(form_b, both, joint(to_mate, 0))
    a_x = lax.ppermute(form_a, "elec", swap)
    form_z = spread(form_a, a_x, b_same, b_cross)
    return salt_scale * form_z + salt_base, water_scale * form_z + water_base


def solution(mesh):
    split = P(("slab", "space"), None)
    placed = (P("elec", ("slab", "space"), None), P(), P(), P("slab"), split, split, split, P(None, ("slab", "space"), None))
    return jax.shard_map(local, mesh=mesh, in_specs=placed, out_specs=(split, split), check_vma=False)
```

time: 57.2 us -> 39.9 us (0.70)
  Pallas kernels: 19.7 us -> 13 us
  local copies, waits for them, and re-layouts: 7.33 us -> 2.73 us
  waiting for transfers between devices: 10.2 us -> 7.3 us
  starting transfers between devices: 14.6 us -> 11.9 us
    pallas_call x4, Pallas kernels: 16.9 us -> 10.1 us  [the longest x1 5.97 us: local(): call(plane_kernel, shape((2 * layers, half), f32), [SMEM] + [VMEM] * 8, '...]
    ppermute x10 -> x11, waiting for transfers between devices: 10.2 us -> 7.3 us  [the longest x1 3.42 us: local(): far_in_1 = lax.ppermute(far_give, both, joint(ahead, 1))]
    ppermute x10 -> x11, starting transfers between devices: 14.6 us -> 11.9 us  [the longest x1 3.65 us: local(): near_in_1 = lax.ppermute(near_give, both, joint(to_mate, 1))]
    unnamed x28 -> x15, local copies, waits for them, and re-layouts: 5.09 us -> 2.69 us
    slice x4 -> x2, local copies, waits for them, and re-layouts: 2.22 us -> 0.02 us  [the longest x1 0.01 us: local(): forms_x[0:1]]
    div x2 -> x0, other arithmetic: 1.29 us -> none  [local(): return (sensitivity / salinity, cementation * sensitivity / water_content)]
    add x1, other arithmetic: 0.01 us -> 0.68 us  [local(): return (salt_scale * form_z + salt_base, water_scale * form_z + water_base)]
  transfers between devices with their start and end apart: 10 -> 11, of which waited for: 6 -> 4; matrix products, arithmetic and copies ran while one was open for 5% -> 8% of each run, Pallas kernels for 26% -> 27%
where the time goes in v3:
time: 39.9 us; the launch traced here: 39.6 us
  Pallas kernels  13 us (33%)
  starting transfers between devices  11.9 us (30%)
  waiting for transfers between devices  7.3 us (18%)
  matrix products  2.81 us (7%)
  local copies, waits for them, and re-layouts  2.73 us (7%)
  other arithmetic  0.97 us (2%)
  between operations  0.86 us (2%)
    pallas_call x1, Pallas kernels, local(): call(plane_kernel, shape((2 * layers, half), f32), [SMEM] + [VMEM] * 8, '...  5.97 us
    ppermute x1, starting transfers between devices, local(): near_in_1 = lax.ppermute(near_give, both, joint(to_mate, 1))  3.65 us
    ppermute x1, waiting for transfers between devices, local(): far_in_1 = lax.ppermute(far_give, both, joint(ahead, 1))  3.42 us
    ppermute x1, starting transfers between devices, local(): near_in_0 = lax.ppermute(near, both, joint(to_mate, 0))  2.97 us
    dot_general x1, matrix products, dot(): return jnp.dot(left, right, preferred_element_type=jnp.float32)  2.81 us
    pallas_call x1, Pallas kernels, local(): call(early_kernel, (shape((rows, 2 * half), f32), shape((8, 2 * half), f3...  2.73 us
    unnamed x15, local copies, waits for them, and re-layouts  2.69 us
    ppermute x1, waiting for transfers between devices, local(): near_in_1 = lax.ppermute(near_give, both, joint(to_mate, 1))  2.25 us
  transfers between devices with their start and end apart: 11, of which 4 were waited for; matrix products, arithmetic and copies ran while one was open for 8% of the time, Pallas kernels for 27%

profile of v3, /device:TPU:0, one launch (start us, length us, event | category | flops | bytes accessed | tf_op | source)
XLA Modules:
  0.0 39.6 jit_solution(2933045974030721172)
XLA Ops:
  0.6 2.2 %copy.12 = bf16[512,2,1024]{2,0,1:T(8,128)(2,1)S(1)} copy(bf16[512,2,1024]{2,1,0:T(2,128)(2,1)} %param.8) | data formatting | bytes 4194304 | tf_op args[0]
  2.8 0.1 pad_add_fusion.place
  2.9 0.0 copy-start.6
  2.9 0.0 copy-start.1
  2.9 0.0 copy-start.2
  2.9 1.6 %keep.1 = (bf16[512,512]{1,0:T(8,128)(2,1)}, bf16[512,512]{1,0:T(8,128)(2,1)}) custom-call(s32[2]{0:T(128)S(1)} %pad_add_fusion.place, bf16[2,512,1024]{2,1,0:T(8,128)(2,1)S(1)} %bitcast.34), custom_call_target="tpu_custom_call" | custom-call | bytes 2097152 | tf_op jit(solution)/shard_map/keep/pallas_call | solution.py:199
  4.5 3.0 %collective-permute-start = (bf16[512,512]{1,0:T(8,128)(2,1)}, bf16[512,512]{1,0:T(8,128)(2,1)}, u32[]{:S(2)}, u32[]{:S(2)}) collective-permute-start(bf16[512,512]{1,0:T(8,128)(2,1)} %get-tuple-element.35.near), channel_id=1, source_target_pairs={{0,2},{1,3},{2,0},{3,1},{4,6},{5,7},{6,4},{7,5},{8,10},{9,11},{10,... | collective-permute-start | bytes 1572872 | tf_op jit(solution)/shard_map/ppermute | solution.py:200
  7.5 1.3 %collective-permute-start.1 = (bf16[512,512]{1,0:T(8,128)(2,1)}, bf16[512,512]{1,0:T(8,128)(2,1)}, u32[]{:S(2)}, u32[]{:S(2)}) collective-permute-start(bf16[512,512]{1,0:T(8,128)(2,1)} %get-tuple-element.27.far), channel_id=1, source_target_pairs={{4,0},{5,1},{8,4},{9,5},{12,8},{13,9},{2,6},{3,7},{6,10},{7,11},{1... | collective-permute-start | bytes 1572872 | tf_op jit(solution)/shard_map/ppermute | solution.py:201
  8.8 1.7 %give.1 = (bf16[512,512]{1,0:T(8,128)(2,1)}, bf16[512,512]{1,0:T(8,128)(2,1)S(1)}, bf16[512,256]{1,0:T(8,128)(2,1)}, bf16[512,256]{1,0:T(8,128)(2,1)S(1)}) custom-call(s32[2]{0:T(128)S(1)} %pad_add_fusion.place, bf16[2,512,1024]{2,1,0:T(8,128)(2,1)S(1)} %bitcast.35), custom_call_target="tpu_custom_call" | custom-call | bytes 2097152 | tf_op jit(solution)/shard_map/give/pallas_call | solution.py:203
  10.4 0.0 collective-permute-start.4
  10.5 0.5 %collective-permute-start.2 = (bf16[512,512]{1,0:T(8,128)(2,1)}, bf16[512,512]{1,0:T(8,128)(2,1)}, u32[]{:S(2)}, u32[]{:S(2)}) collective-permute-start(bf16[512,512]{1,0:T(8,128)(2,1)} %get-tuple-element.39), channel_id=1, source_target_pairs={{0,1},{1,0},{2,3},{3,2},{4,5},{5,4},{6,7},{7,6},{8,9},{9,8},{10,11... | collective-permute-start | bytes 1572872 | tf_op jit(solution)/shard_map/ppermute | solution.py:206
  11.0 0.0 collective-permute-start.3
  11.0 0.0 copy-done.6
  11.0 0.0 copy-done.1
  11.0 0.0 copy-done.2
  11.0 2.8 %fusion.10.weights = bf16[1024,1024]{1,0:T(8,128)(2,1)S(1)} fusion(s32[1024]{0:T(1024)S(1)} %add_select_fusion.1, f32[1024]{0:T(1024)S(1)} %convert_element_type.23, s32[1024]{0:T(1024)S(1)} %bitcast.46, s32[1024]{0:T(1024)S(1)} %bitcast.47, s32[1024]{0:T(1024)S(1)} %bitcast.48, s32[1024]{0:T(1024)S(1)} %bitcast.45), kind=kOutput, calls=%fused_computation.13 | convolution fusion | flops 2161115136 | bytes 2121728 | tf_op jit(solution)/shard_map/dot_general | solution.py:32
  13.9 0.0 copy-start
  13.9 0.0 copy-start.3
  13.9 0.0 copy-start.4
  13.9 0.0 copy-start.5
  13.9 0.2 cross.1
  14.1 0.5 %copy-done = f32[3,2,1024]{2,1,0:T(2,128)S(1)} copy-done((f32[3,2,1024]{2,1,0:T(2,128)S(1)}, f32[3,2,1024]{2,1,0:T(2,128)}, u32[]{:S(2)}) %copy-start) | copy-done | bytes 24600
  14.6 0.0 copy-done.3
  14.6 0.0 copy-done.4
  14.6 0.0 copy-done.5
  14.6 0.1 bitcast_multiply_fusion
  14.7 0.0 collective-permute-done.4.rim_x
  14.7 3.7 %collective-permute-start.6 = (bf16[512,512]{1,0:T(8,128)(2,1)}, bf16[512,512]{1,0:T(8,128)(2,1)S(1)}, u32[]{:S(2)}, u32[]{:S(2)}) collective-permute-start(bf16[512,512]{1,0:T(8,128)(2,1)} %get-tuple-element.39), channel_id=1, source_target_pairs={{0,3},{1,2},{2,1},{3,0},{4,7},{5,6},{6,5},{7,4},{8,11},{9,10},{10,... | collective-permute-start | bytes 1572872 | tf_op jit(solution)/shard_map/ppermute | solution.py:217
  18.3 0.0 collective-permute-done.2.near_x
  18.3 1.3 %collective-permute-start.7 = (bf16[512,512]{1,0:T(8,128)(2,1)S(1)}, bf16[512,512]{1,0:T(8,128)(2,1)S(1)}, u32[]{:S(2)}, u32[]{:S(2)}) collective-permute-start(bf16[512,512]{1,0:T(8,128)(2,1)S(1)} %get-tuple-element.40), channel_id=1, source_target_pairs={{4,1},{5,0},{8,5},{9,4},{12,9},{13,8},{2,7},{3,6},{6,11},{7,10},{1... | collective-permute-start | bytes 1572872 | tf_op jit(solution)/shard_map/ppermute | solution.py:218
  19.6 0.0 collective-permute-done.3.far_x.far
  19.6 6.0 %plane.1 = f32[4,512]{1,0:T(4,128)S(1)} custom-call(s32[2]{0:T(128)S(1)} %pad_add_fusion.place, bf16[512,512]{1,0:T(8,128)(2,1)} %get-tuple-element.35.near, bf16[512,512]{1,0:T(8,128)(2,1)} %get-tuple-element.27.far, bf16[512,256]{1,0:T(8,128)(2,1)S(1)} %get-tuple-element.36.rim, bf16[512,512]{1,0:T(8,128)(2,1)} %collective-permute-done.2.near_x, ...), custom_call_target="tpu_custom_call" | custom-call | flops 3221225472 | bytes 8388608 | tf_op jit(solution)/shard_map/plane/pallas_call | solution.py:221
  25.6 0.0 collective-permute-start.5
  25.7 0.0 collective-permute-done.near_in
  25.7 0.0 collective-permute-done.1.far_in
  25.7 2.7 %early.1 = (f32[512,1024]{1,0:T(8,128)S(1)}, f32[8,1024]{1,0:T(8,128)S(1)}) custom-call(bf16[512,512]{1,0:T(8,128)(2,1)} %get-tuple-element.27.far, bf16[512,512]{1,0:T(8,128)(2,1)} %collective-permute-done.near_in, bf16[512,512]{1,0:T(8,128)(2,1)} %collective-permute-done.1.far_in, bf16[1024,1024]{1,0:T(8,128)(2,1)S(1)} %fusion.10.weights, ...), custom_call_target="tpu_custom_call" | custom-call | flops 2147483648 | bytes 8388608 | tf_op jit(solution)/shard_map/early/pallas_call | solution.py:251
  28.4 0.0 collective-permute-done.5
  28.5 0.1 fusion.22
  28.6 2.3 %collective-permute-done.6.near_in = bf16[512,512]{1,0:T(8,128)(2,1)S(1)} collective-permute-done((bf16[512,512]{1,0:T(8,128)(2,1)}, bf16[512,512]{1,0:T(8,128)(2,1)S(1)}, u32[]{:S(2)}, u32[]{:S(2)}) %collective-permute-start.6) | collective-permute-done | bytes 524320 | tf_op jit(solution)/shard_map/ppermute | solution.py:217
  30.8 3.4 %collective-permute-done.7.far_in = bf16[512,512]{1,0:T(8,128)(2,1)S(1)} collective-permute-done((bf16[512,512]{1,0:T(8,128)(2,1)S(1)}, bf16[512,512]{1,0:T(8,128)(2,1)S(1)}, u32[]{:S(2)}, u32[]{:S(2)}) %collective-permute-start.7) | collective-permute-done | bytes 524320 | tf_op jit(solution)/shard_map/ppermute | solution.py:218
  34.2 0.8 %late.1 = (f32[1,512]{1,0:T(1,128)S(1)}, f32[1,512]{1,0:T(1,128)S(1)}) custom-call(bf16[512,512]{1,0:T(8,128)(2,1)S(1)} %collective-permute-done.3.far_x.far, bf16[512,512]{1,0:T(8,128)(2,1)S(1)} %collective-permute-done.6.near_in, bf16[512,512]{1,0:T(8,128)(2,1)S(1)} %collective-permute-done.7.far_in, bf16[1024,1024]{1,0:T(8,128)(2,1)S(1)} %fusion.10.weights, ...), custom_call_target="tpu_custom_call" | custom-call | flops 1073741824 | bytes 8388608 | tf_op jit(solution)/shard_map/late/pallas_call | solution.py:263
  35.1 0.2 collective-permute-start.8
  35.3 0.0 collective-permute-start.10
  35.3 2.0 %collective-permute-start.9 = (f32[1,512]{1,0:T(1,128)S(1)}, f32[1,512]{1,0:T(1,128)S(1)}, u32[]{:S(2)}, u32[]{:S(2)}) collective-permute-start(f32[1,512]{1,0:T(1,128)S(1)} %get-tuple-element.44), channel_id=1, source_target_pairs={{0,2},{1,3},{2,0},{3,1},{4,6},{5,7},{6,4},{7,5},{8,10},{9,11},{10,... | collective-permute-start | bytes 6152 | tf_op jit(solution)/shard_map/ppermute | solution.py:274
  37.3 0.0 collective-permute-done.8
  37.3 1.0 %collective-permute-done.10 = f32[1,512]{1,0:T(1,128)S(1)} collective-permute-done((f32[1,512]{1,0:T(1,128)S(1)}, f32[1,512]{1,0:T(1,128)S(1)}, u32[]{:S(2)}, u32[]{:S(2)}) %collective-permute-start.10) | collective-permute-done | bytes 2080 | tf_op jit(solution)/shard_map/ppermute | solution.py:273
  38.3 0.6 %collective-permute-done.9 = f32[1,512]{1,0:T(1,128)S(1)} collective-permute-done((f32[1,512]{1,0:T(1,128)S(1)}, f32[1,512]{1,0:T(1,128)S(1)}, u32[]{:S(2)}, u32[]{:S(2)}) %collective-permute-start.9) | collective-permute-done | bytes 2080 | tf_op jit(solution)/shard_map/ppermute | solution.py:274
  38.9 0.7 %fusion.14 = (f32[2,1024]{1,0:T(2,128)}, f32[2,1024]{1,0:T(2,128)}) fusion(f32[2,1024]{1,0:T(2,128)S(1)} %get-tuple-element.47, f32[2,1024]{1,0:T(2,128)S(1)} %get-tuple-element.46, pred[2]{0:T(512)(128)(4,1)S(1)} %iota_compare_fusion, f32[1024]{0:T(1024)S(1)} %maximum_select_fusion.5, f32[1024]{0:T(1024)S(1)} %maximum_select_fusion.4, ...), kind=kLoop, calls=%fused_computation.17 | loop fusion | flops 10240 | bytes 57346 | tf_op jit(solution)/shard_map/add | solution.py:277
  (12 shorter events, 0.1 us)
Async XLA Ops:
  2.9 8.0 %copy-start.6 = (bf16[1024]{0:T(1024)(128)(2,1)S(1)}, bf16[1024]{0:T(1024)(128)(2,1)}, u32[]{:S(2)}) copy-start(bf16[1024]{0:T(1024)(128)(2,1)} %param.11) | copy-start | bytes 6148
  2.9 8.0 %copy-start.1 = (s32[1024]{0:T(1024)S(1)}, s32[1024]{0:T(1024)}, u32[]{:S(2)}) copy-start(s32[1024]{0:T(1024)} %param.9) | copy-start | bytes 12292
  2.9 8.1 %copy-start.2 = (s32[1024,4]{0,1:T(4,128)S(1)}, s32[1024,4]{0,1:T(4,128)}, u32[]{:S(2)}) copy-start(s32[1024,4]{0,1:T(4,128)} %param.10) | copy-start | bytes 49156
  4.5 21.1 %collective-permute-start = (bf16[512,512]{1,0:T(8,128)(2,1)}, bf16[512,512]{1,0:T(8,128)(2,1)}, u32[]{:S(2)}, u32[]{:S(2)}) collective-permute-start(bf16[512,512]{1,0:T(8,128)(2,1)} %get-tuple-element.35.near), channel_id=1, source_target_pairs={{0,2},{1,3},{2,0},{3,1},{4,6},{5,7},{6,4},{7,5},{8,10},{9,11},{10,... | collective-permute-start | bytes 1572872 | tf_op jit(solution)/shard_map/ppermute | solution.py:200
  7.5 18.2 %collective-permute-start.1 = (bf16[512,512]{1,0:T(8,128)(2,1)}, bf16[512,512]{1,0:T(8,128)(2,1)}, u32[]{:S(2)}, u32[]{:S(2)}) collective-permute-start(bf16[512,512]{1,0:T(8,128)(2,1)} %get-tuple-element.27.far), channel_id=1, source_target_pairs={{4,0},{5,1},{8,4},{9,5},{12,8},{13,9},{2,6},{3,7},{6,10},{7,11},{1... | collective-permute-start | bytes 1572872 | tf_op jit(solution)/shard_map/ppermute | solution.py:201
  10.4 4.2 %collective-permute-start.4 = (bf16[512,256]{1,0:T(8,128)(2,1)}, bf16[512,256]{1,0:T(8,128)(2,1)}, u32[]{:S(2)}, u32[]{:S(2)}) collective-permute-start(bf16[512,256]{1,0:T(8,128)(2,1)} %get-tuple-element.37), channel_id=1, source_target_pairs={{0,1},{1,0},{2,3},{3,2},{4,5},{5,4},{6,7},{7,6},{8,9},{9,8},{10,11... | collective-permute-start | bytes 786440 | tf_op jit(solution)/shard_map/ppermute | solution.py:208
  10.5 7.9 %collective-permute-start.2 = (bf16[512,512]{1,0:T(8,128)(2,1)}, bf16[512,512]{1,0:T(8,128)(2,1)}, u32[]{:S(2)}, u32[]{:S(2)}) collective-permute-start(bf16[512,512]{1,0:T(8,128)(2,1)} %get-tuple-element.39), channel_id=1, source_target_pairs={{0,1},{1,0},{2,3},{3,2},{4,5},{5,4},{6,7},{7,6},{8,9},{9,8},{10,11... | collective-permute-start | bytes 1572872 | tf_op jit(solution)/shard_map/ppermute | solution.py:206
  11.0 8.7 %collective-permute-start.3 = (bf16[512,512]{1,0:T(8,128)(2,1)S(1)}, bf16[512,512]{1,0:T(8,128)(2,1)S(1)}, u32[]{:S(2)}, u32[]{:S(2)}) collective-permute-start(bf16[512,512]{1,0:T(8,128)(2,1)S(1)} %get-tuple-element.40), channel_id=1, source_target_pairs={{0,1},{1,0},{2,3},{3,2},{4,5},{5,4},{6,7},{7,6},{8,9},{9,8},{10,11... | collective-permute-start | bytes 1572872 | tf_op jit(solution)/shard_map/ppermute | solution.py:207
  13.9 0.7 %copy-start = (f32[3,2,1024]{2,1,0:T(2,128)S(1)}, f32[3,2,1024]{2,1,0:T(2,128)}, u32[]{:S(2)}) copy-start(f32[3,2,1024]{2,1,0:T(2,128)} %param.15) | copy-start | bytes 73732
  13.9 0.7 %copy-start.3 = (f32[2,1024]{1,0:T(2,128)S(1)}, f32[2,1024]{1,0:T(2,128)}, u32[]{:S(2)}) copy-start(f32[2,1024]{1,0:T(2,128)} %param.13) | copy-start | bytes 24580
  13.9 0.7 %copy-start.4 = (f32[2,1024]{1,0:T(2,128)S(1)}, f32[2,1024]{1,0:T(2,128)}, u32[]{:S(2)}) copy-start(f32[2,1024]{1,0:T(2,128)} %param.14) | copy-start | bytes 24580
  13.9 0.7 %copy-start.5 = (f32[2,1024]{1,0:T(2,128)S(1)}, f32[2,1024]{1,0:T(2,128)}, u32[]{:S(2)}) copy-start(f32[2,1024]{1,0:T(2,128)} %param.12) | copy-start | bytes 24580
  14.7 16.1 %collective-permute-start.6 = (bf16[512,512]{1,0:T(8,128)(2,1)}, bf16[512,512]{1,0:T(8,128)(2,1)S(1)}, u32[]{:S(2)}, u32[]{:S(2)}) collective-permute-start(bf16[512,512]{1,0:T(8,128)(2,1)} %get-tuple-element.39), channel_id=1, source_target_pairs={{0,3},{1,2},{2,1},{3,0},{4,7},{5,6},{6,5},{7,4},{8,11},{9,10},{10,... | collective-permute-start | bytes 1572872 | tf_op jit(solution)/shard_map/ppermute | solution.py:217
  18.3 15.9 %collective-permute-start.7 = (bf16[512,512]{1,0:T(8,128)(2,1)S(1)}, bf16[512,512]{1,0:T(8,128)(2,1)S(1)}, u32[]{:S(2)}, u32[]{:S(2)}) collective-permute-start(bf16[512,512]{1,0:T(8,128)(2,1)S(1)} %get-tuple-element.40), channel_id=1, source_target_pairs={{4,1},{5,0},{8,5},{9,4},{12,9},{13,8},{2,7},{3,6},{6,11},{7,10},{1... | collective-permute-start | bytes 1572872 | tf_op jit(solution)/shard_map/ppermute | solution.py:218
  25.6 2.8 %collective-permute-start.5 = (f32[4,512]{1,0:T(4,128)S(1)}, f32[4,512]{1,0:T(4,128)S(1)}, u32[]{:S(2)}, u32[]{:S(2)}) collective-permute-start(f32[4,512]{1,0:T(4,128)S(1)} %plane.1), channel_id=1, source_target_pairs={{0,1},{1,0},{2,3},{3,2},{4,5},{5,4},{6,7},{7,6},{8,9},{9,8},{10,11... | collective-permute-start | bytes 24584 | tf_op jit(solution)/shard_map/ppermute | solution.py:245
  35.1 2.2 %collective-permute-start.8 = (f32[1,512]{1,0:T(1,128)S(1)}, f32[1,512]{1,0:T(1,128)S(1)}, u32[]{:S(2)}, u32[]{:S(2)}) collective-permute-start(f32[1,512]{1,0:T(1,128)S(1)} %get-tuple-element.43), channel_id=1, source_target_pairs={{0,1},{1,0},{2,3},{3,2},{4,5},{5,4},{6,7},{7,6},{8,9},{9,8},{10,11... | collective-permute-start | bytes 6152 | tf_op jit(solution)/shard_map/ppermute | solution.py:275
  35.3 3.0 %collective-permute-start.10 = (f32[1,512]{1,0:T(1,128)S(1)}, f32[1,512]{1,0:T(1,128)S(1)}, u32[]{:S(2)}, u32[]{:S(2)}) collective-permute-start(f32[1,512]{1,0:T(1,128)S(1)} %get-tuple-element.44), channel_id=1, source_target_pairs={{0,3},{1,2},{2,1},{3,0},{4,7},{5,6},{6,5},{7,4},{8,11},{9,10},{10,... | collective-permute-start | bytes 6152 | tf_op jit(solution)/shard_map/ppermute | solution.py:273
  35.3 3.7 %collective-permute-start.9 = (f32[1,512]{1,0:T(1,128)S(1)}, f32[1,512]{1,0:T(1,128)S(1)}, u32[]{:S(2)}, u32[]{:S(2)}) collective-permute-start(f32[1,512]{1,0:T(1,128)S(1)} %get-tuple-element.44), channel_id=1, source_target_pairs={{0,2},{1,3},{2,0},{3,1},{4,6},{5,7},{6,4},{7,5},{8,10},{9,11},{10,... | collective-permute-start | bytes 6152 | tf_op jit(solution)/shard_map/ppermute | solution.py:274

commit v4 on v3

--- a/solution.py
+++ b/solution.py
@@ -12,6 +12,7 @@
 SMEM = pl.BlockSpec(memory_space=pltpu.SMEM)
 MIB = 2**20
 LATER = True
+HOLD = True
 AFTER = True
 
 
@@ -43,7 +44,7 @@
             far[...] = field[odd, :, k * half : (k + 1) * half]
 
 
-def give_kernel(place, field, near, far, edge, rim):
+def give_kernel(place, field, near, far, parcel, rim):
     odd, core = place[0], place[1]
     half = near.shape[1]
     for k in range(2):
@@ -54,14 +55,12 @@
         def _():
             near[...] = field[1 - odd, :, (1 - k) * half : (2 - k) * half]
             far[...] = field[odd, :, (1 - k) * half : (2 - k) * half]
-
-            @pl.loop(0, field.shape[1], step=64)
-            def _(r):
-                rows = pl.ds(pl.multiple_of(r, 64), 64)
-                edge[rows, :LANES] = field[1 - odd, rows, inner]
-                edge[rows, LANES:] = field[odd, rows, inner]
-                rim[rows, :LANES] = field[1 - odd, rows, outer]
-                rim[rows, LANES:] = field[odd, rows, outer]
+            parcel[:, :half] = field[1 - odd, :, (1 - k) * half : (2 - k) * half]
+            parcel[:, half : 2 * half] = field[odd, :, (1 - k) * half : (2 - k) * half]
+            parcel[:, 2 * half : 2 * half + LANES] = field[1 - odd, :, inner]
+            parcel[:, 2 * half + LANES :] = field[odd, :, inner]
+            rim[:, :LANES] = field[1 - odd, :, outer]
+            rim[:, LANES:] = field[odd, :, outer]
 
 
 def cross_kernel(weights, out):
@@ -92,16 +91,21 @@
     return out
 
 
-def plane_kernel(place, near, far, rim, near_x, far_x, rim_x, weights, cross, out, delta):
+def plane_kernel(place, near, far, rim, parcel, weights, cross, out, delta):
     first = place[1] == 0
     rows, half = near.shape
     count = half // LANES
     step = 128
-    for layer, own in enumerate(((near, near_x), (far, far_x))):
+    for layer, own in enumerate((near, far)):
         for group in range(2):
             for r in range(0, rows, step):
-                body = own[group][r : r + step, :]
-                edge = (rim, rim_x)[group][r : r + step, layer * LANES : (layer + 1) * LANES]
+                at = pl.ds(r, step)
+                if group == 0:
+                    body = own[at, :]
+                    edge = rim[at, layer * LANES : (layer + 1) * LANES]
+                else:
+                    body = parcel[at, layer * half : (layer + 1) * half]
+                    edge = parcel[at, 2 * half + layer * LANES : 2 * half + (layer + 1) * LANES]
                 body, edge = body.astype(jnp.float32), edge.astype(jnp.float32)
                 blocks = [body[:, b * LANES : (b + 1) * LANES] for b in range(count)]
                 along_y = y_change(blocks, edge, first)
@@ -137,7 +141,7 @@
     return change_a.astype(jnp.bfloat16), change_b.astype(jnp.bfloat16)
 
 
-def early_kernel(far, near_in, far_in, weights, cross, carry, out, delta):
+def early_kernel(far, near_in, far_in, weights, cross, carry_a, carry_b, out_a, out_b, delta):
     rows, half = far.shape
     for r in range(0, rows, 128):
         at = pl.ds(r, 128)
@@ -145,23 +149,24 @@
     total = jnp.zeros((8, 2 * half), jnp.float32)
     for r in range(0, rows, 256):
         mixed = dot(weights[r : r + 256, :rows], delta[...])
-        carry[r : r + 256, :] = dot(cross[r : r + 256, :], delta[...])
+        carry = dot(cross[r : r + 256, :], delta[...])
+        carry_a[r : r + 256, :] = carry[:, :half]
+        carry_b[r : r + 256, :] = carry[:, half:]
         total = total + jnp.sum((delta[r : r + 256, :].astype(jnp.float32) * mixed).reshape(-1, 8, 2 * half), axis=0)
-    out[...] = total
-
-
-def late_kernel(far, near_in, far_in, weights, carry, early, out_a, out_b, delta):
-    rows, half = far.shape
-    for r in range(0, rows, 128):
-        at = pl.ds(r, 128)
-        delta[at, :half], delta[at, half:] = differences(far, near_in, far_in, at)
+    out_a[...] = total[:, :half]
+    out_b[...] = total[:, half:]
+
+
+def close_kernel(upper, lower, weights, carry, early, out, start=0):
+    rows, half = lower.shape
+    upper = upper.at[:, start : start + half]
+    changes = [(upper[r : r + 128, :].astype(jnp.float32) - lower[r : r + 128, :].astype(jnp.float32)) for r in range(0, rows, 128)]
+    delta = jnp.concatenate(changes, axis=0).astype(jnp.bfloat16)
     total = early[...]
     for r in range(0, rows, 256):
-        mixed = carry[r : r + 256, :] + dot(weights[rows + r : rows + r + 256, rows:], delta[...])
-        total = total + jnp.sum((delta[r : r + 256, :].astype(jnp.float32) * mixed).reshape(-1, 8, 2 * half), axis=0)
-    total = 0.25 * jnp.sum(total, axis=0, keepdims=True)
-    out_a[...] = total[:, :half]
-    out_b[...] = total[:, half:]
+        mixed = carry[r : r + 256, :] + dot(weights[rows + r : rows + r + 256, rows:], delta)
+        total = total + jnp.sum((delta[r : r + 256, :].astype(jnp.float32) * mixed).reshape(-1, 8, half), axis=0)
+    out[...] = 0.25 * jnp.sum(total, axis=0, keepdims=True)
 
 
 def assemble(quadripoles, weighted_misfit, order):
@@ -185,6 +190,8 @@
     to_mate = [(i, i ^ 1) for i in range(blocks)]
     ahead = [(i, i - 2) for i in range(2, blocks, 2)] + [(i, i + 2) for i in range(1, blocks - 2, 2)]
     swap = [(0, 1), (1, 0)]
+    low_core, near_level = c == 0, 1 - odd
+    potentials, odd, c, low_core, near_level = lax.optimization_barrier((potentials, odd, c, low_core, near_level))
     place = jnp.stack([odd, c]).astype(jnp.int32)
     shape = jax.ShapeDtypeStruct
     bf16, f32 = jnp.bfloat16, jnp.float32
@@ -200,20 +207,23 @@
     near_in_0 = lax.ppermute(near, both, joint(to_mate, 0))
     far_in_0 = lax.ppermute(far, both, joint(ahead, 0))
     field, near, far = lax.optimization_barrier((field, near, far))
-    near_give, far_give, edge, rim = call(
-        give_kernel, (piece,) * 2 + (strip,) * 2, [SMEM, VMEM], "give", moved=rows * cells * 4, limit=2
+    near_give, far_give, parcel, rim = call(
+        give_kernel,
+        (piece, piece, shape((rows, 2 * half + 2 * LANES), bf16), strip),
+        [SMEM, VMEM],
+        "give",
+        moved=rows * cells * 8,
+        limit=2,
     )(place, field)
-    near_x = lax.ppermute(near_give, "elec", swap)
-    far_x = lax.ppermute(far_give, "elec", swap)
-    rim_x = lax.ppermute(edge, "elec", swap)
-
-    order = jnp.where(c == 0, elec_order, jnp.concatenate([elec_order[rows:], elec_order[:rows]]))
+    parcel = lax.ppermute(parcel, "elec", swap)
+
+    order = jnp.where(low_core, elec_order, jnp.concatenate([elec_order[rows:], elec_order[:rows]]))
     if AFTER:
         quadripoles, near_give = lax.optimization_barrier((quadripoles, near_give))
     weights = assemble(quadripoles, weighted_misfit, order)
     cross = call(cross_kernel, shape((rows, rows), bf16), [VMEM], "cross", moved=4 * rows * rows * 2)(weights)
-    if LATER:
-        near_give, far_give, weights = lax.optimization_barrier((near_give, far_give, weights))
+    near_give, weights = lax.optimization_barrier((near_give, weights))
+    far_give, cross = lax.optimization_barrier((far_give, cross))
     near_in_1 = lax.ppermute(near_give, both, joint(to_mate, 1))
     far_in_1 = lax.ppermute(far_give, both, joint(ahead, 1))
 
@@ -221,19 +231,19 @@
     forms = call(
         plane_kernel,
         shape((2 * layers, half), f32),
-        [SMEM] + [VMEM] * 8,
+        [SMEM] + [VMEM] * 6,
         "plane",
         scratch=[pltpu.VMEM((2, 2 * rows, half), bf16)],
         limit=16,
         flops=big * 6,
         moved=rows * cells * 16,
-    )(place, near, far, rim, near_x, far_x, rim_x, weights, cross)
+    )(place, near, far, rim, parcel, weights, cross)
 
     bulk = 0.15 * salinity * water_content**cementation
     salt_scale = bulk / salinity
     water_scale = bulk * cementation / water_content
     row = lax.broadcasted_iota(jnp.int32, (layers, cells), 0)
-    is_near = row == 1 - odd
+    is_near = row == near_level
     is_mine = lax.broadcasted_iota(jnp.int32, (1, cells), 1) // half == c
 
     def spread(near_mine, near_other, far_mine, far_other):
@@ -248,31 +258,32 @@
     salt_base, water_base = salt_scale * flat, water_scale * flat
     salt_scale, water_scale = salt_scale * anisotropy[0], water_scale * anisotropy[0]
 
-    carry, early = call(
+    weights_e, forms = lax.optimization_barrier((weights, forms))
+    carry_a, carry_b, early_a, early_b = call(
         early_kernel,
-        (shape((rows, 2 * half), f32), shape((8, 2 * half), f32)),
+        (shape((rows, half), f32),) * 2 + (shape((8, half), f32),) * 2,
         [VMEM] * 5,
         "early",
         scratch=[pltpu.VMEM((rows, 2 * half), bf16)],
         flops=big * 4,
         moved=rows * cells * 16,
-    )(far, near_in_0, far_in_0, weights, cross)
-    early, salt_base, water_base, salt_scale, water_scale = lax.optimization_barrier(
-        (early, salt_base, water_base, salt_scale, water_scale)
+    )(far, near_in_0, far_in_0, weights_e, cross)
+    early_a, salt_base, water_base, salt_scale, water_scale = lax.optimization_barrier(
+        (early_a, salt_base, water_base, salt_scale, water_scale)
     )
-    form_a, form_b = call(
-        late_kernel,
-        (shape((1, half), f32), shape((1, half), f32)),
-        [VMEM] * 6,
-        "late",
-        scratch=[pltpu.VMEM((rows, 2 * half), bf16)],
-        flops=big * 2,
-        moved=rows * cells * 16,
-    )(far_x, near_in_1, far_in_1, weights, carry, early)
-
+
+    def close(name, start, *given):
+        return call(
+            functools.partial(close_kernel, start=start), shape((1, half), f32), [VMEM] * 5, name, flops=big, moved=rows * cells * 8, limit=6
+        )(*given)
+
+    form_a = close("close_a", half, parcel, near_in_1, weights, carry_a, early_a)
+    a_x = lax.ppermute(form_a, "elec", swap)
+    if HOLD:
+        far_in_1, form_a = lax.optimization_barrier((far_in_1, form_a))
+    form_b = close("close_b", 0, far_in_1, near_in_1, weights, carry_b, early_b)
     b_cross = lax.ppermute(form_b, both, joint(to_mate, 1))
     b_same = lax.ppermute(form_b, both, joint(to_mate, 0))
-    a_x = lax.ppermute(form_a, "elec", swap)
     form_z = spread(form_a, a_x, b_same, b_cross)
     return salt_scale * form_z + salt_base, water_scale * form_z + water_base
 

time: 39.9 us -> 37.3 us (0.935)
  Pallas kernels: 13 us -> 9.24 us
  starting transfers between devices: 11.9 us -> 13.6 us
  local copies, waits for them, and re-layouts: 2.73 us -> 2.28 us
    pallas_call x4 -> x5, Pallas kernels: 11.2 us -> 8.39 us  [the longest x1 5.23 us: local(): call(plane_kernel, shape((2 * layers, half), f32), [SMEM] + [VMEM] * 6, '...]
    unnamed x15 -> x14, local copies, waits for them, and re-layouts: 2.69 us -> 0.04 us
    ppermute x1, waiting for transfers between devices: 2.25 us -> 4.71 us  [local(): near_in_1 = lax.ppermute(near_give, both, joint(to_mate, 1))]
    ppermute x1, waiting for transfers between devices: 3.42 us -> 1.06 us  [local(): far_in_1 = lax.ppermute(far_give, both, joint(ahead, 1))]
    optimization_barrier x0 -> x1, local copies, waits for them, and re-layouts: none -> 2.2 us  [local(): lax.optimization_barrier((potentials, odd, c, low_core, near_level))]
    ppermute x1, starting transfers between devices: 0.01 us -> 1.43 us  [local(): b_cross = lax.ppermute(form_b, both, joint(to_mate, 1))]
    ppermute x1, starting transfers between devices: 3.65 us -> 4.7 us  [local(): near_in_1 = lax.ppermute(near_give, both, joint(to_mate, 1))]
    pallas_call x1, Pallas kernels: 1.61 us -> 0.62 us  [local(): call(keep_kernel, (piece,) * 2, [SMEM, VMEM], 'keep', moved=rows * cells...]
  transfers between devices with their start and end apart: 11 -> 9, of which waited for: 4 -> 4; matrix products, arithmetic and copies ran while one was open for 8% -> 8% of each run, Pallas kernels for 27% -> 22%
where the time goes in v4:
time: 37.3 us; the launch traced here: 37.1 us
  starting transfers between devices  13.6 us (36%)
  Pallas kernels  9.24 us (25%)
  waiting for transfers between devices  7.36 us (20%)
  matrix products  2.8 us (8%)
  local copies, waits for them, and re-layouts  2.28 us (6%)
  other arithmetic  0.98 us (3%)
  between operations  0.91 us (2%)
    pallas_call x1, Pallas kernels, local(): call(plane_kernel, shape((2 * layers, half), f32), [SMEM] + [VMEM] * 6, '...  5.23 us
    ppermute x1, waiting for transfers between devices, local(): near_in_1 = lax.ppermute(near_give, both, joint(to_mate, 1))  4.71 us
    ppermute x1, starting transfers between devices, local(): near_in_1 = lax.ppermute(near_give, both, joint(to_mate, 1))  4.7 us
    ppermute x1, starting transfers between devices, local(): near_in_0 = lax.ppermute(near, both, joint(to_mate, 0))  3.03 us
    dot_general x1, matrix products, dot(): return jnp.dot(left, right, preferred_element_type=jnp.float32)  2.8 us
    optimization_barrier x1, local copies, waits for them, and re-layouts, local(): lax.optimization_barrier((potentials, odd, c, low_core, near_level))  2.2 us
    ppermute x1, starting transfers between devices, local(): b_cross = lax.ppermute(form_b, both, joint(to_mate, 1))  1.43 us
    pallas_call x1, Pallas kernels, local(): call(early_kernel, (shape((rows, half), f32),) * 2 + (shape((8, half), f3...  1.37 us
  transfers between devices with their start and end apart: 9, of which 4 were waited for; matrix products, arithmetic and copies ran while one was open for 8% of the time, Pallas kernels for 22%

profile of v4, /device:TPU:0, one launch (start us, length us, event | category | flops | bytes accessed | tf_op | source)
XLA Modules:
  0.0 37.1 jit_solution(10964346003644344576)
XLA Ops:
  0.6 2.2 %copy.12 = bf16[512,2,1024]{2,0,1:T(8,128)(2,1)S(1)} copy(bf16[512,2,1024]{2,1,0:T(2,128)(2,1)} %param.8) | data formatting | bytes 4194304 | tf_op jit(solution)/shard_map/optimization_barrier | solution.py:194
  2.8 0.1 pad_add_fusion.place
  2.9 0.0 copy-start.1
  2.9 0.0 copy-start.6
  2.9 0.0 copy-start.2
  2.9 0.6 %keep.1 = (bf16[512,512]{1,0:T(8,128)(2,1)S(1)}, bf16[512,512]{1,0:T(8,128)(2,1)S(1)}) custom-call(s32[2]{0:T(128)S(1)} %pad_add_fusion.place, bf16[2,512,1024]{2,1,0:T(8,128)(2,1)S(1)} %bitcast.34), custom_call_target="tpu_custom_call" | custom-call | bytes 2097152 | tf_op jit(solution)/shard_map/keep/pallas_call | solution.py:206
  3.6 3.0 %collective-permute-start = (bf16[512,512]{1,0:T(8,128)(2,1)S(1)}, bf16[512,512]{1,0:T(8,128)(2,1)S(1)}, u32[]{:S(2)}, u32[]{:S(2)}) collective-permute-start(bf16[512,512]{1,0:T(8,128)(2,1)S(1)} %get-tuple-element.46.near), channel_id=1, source_target_pairs={{0,2},{1,3},{2,0},{3,1},{4,6},{5,7},{6,4},{7,5},{8,10},{9,11},{10,... | collective-permute-start | bytes 1572872 | tf_op jit(solution)/shard_map/ppermute | solution.py:207
  6.6 1.3 %collective-permute-start.1 = (bf16[512,512]{1,0:T(8,128)(2,1)S(1)}, bf16[512,512]{1,0:T(8,128)(2,1)S(1)}, u32[]{:S(2)}, u32[]{:S(2)}) collective-permute-start(bf16[512,512]{1,0:T(8,128)(2,1)S(1)} %get-tuple-element.39.far), channel_id=1, source_target_pairs={{4,0},{5,1},{8,4},{9,5},{12,8},{13,9},{2,6},{3,7},{6,10},{7,11},{1... | collective-permute-start | bytes 1572872 | tf_op jit(solution)/shard_map/ppermute | solution.py:208
  7.9 0.8 %give.1 = (bf16[512,512]{1,0:T(8,128)(2,1)S(1)}, bf16[512,512]{1,0:T(8,128)(2,1)S(1)}, bf16[512,1280]{1,0:T(8,128)(2,1)S(1)}, bf16[512,256]{1,0:T(8,128)(2,1)S(1)}) custom-call(s32[2]{0:T(128)S(1)} %pad_add_fusion.place, bf16[2,512,1024]{2,1,0:T(8,128)(2,1)S(1)} %bitcast.35), custom_call_target="tpu_custom_call" | custom-call | bytes 4194304 | tf_op jit(solution)/shard_map/give/pallas_call | solution.py:210
  8.7 0.1 collective-permute-start.2
  8.8 0.0 copy-done.1
  8.8 0.0 copy-done.6
  8.8 0.0 copy-done.2
  8.8 2.8 %fusion.10.weights = bf16[1024,1024]{1,0:T(8,128)(2,1)S(1)} fusion(s32[1024]{0:T(1024)S(1)} %add_select_fusion.1, f32[1024]{0:T(1024)S(1)} %convert_element_type.23, s32[1024]{0:T(1024)S(1)} %bitcast.46, s32[1024]{0:T(1024)S(1)} %bitcast.47, s32[1024]{0:T(1024)S(1)} %bitcast.48, s32[1024]{0:T(1024)S(1)} %bitcast.45), kind=kOutput, calls=%fused_computation.13 | convolution fusion | flops 2161115136 | bytes 2121728 | tf_op jit(solution)/shard_map/dot_general | solution.py:33
  11.7 0.0 copy-start
  11.7 0.0 copy-start.3
  11.7 0.0 copy-start.4
  11.7 0.0 copy-start.5
  11.7 0.2 cross.1
  11.9 1.3 %collective-permute-start.4 = (bf16[512,512]{1,0:T(8,128)(2,1)S(1)}, bf16[512,512]{1,0:T(8,128)(2,1)S(1)}, u32[]{:S(2)}, u32[]{:S(2)}) collective-permute-start(bf16[512,512]{1,0:T(8,128)(2,1)S(1)} %get-tuple-element.55), channel_id=1, source_target_pairs={{4,1},{5,0},{8,5},{9,4},{12,9},{13,8},{2,7},{3,6},{6,11},{7,10},{1... | collective-permute-start | bytes 1572872 | tf_op jit(solution)/shard_map/ppermute | solution.py:228
  13.2 4.7 %collective-permute-start.5 = (bf16[512,512]{1,0:T(8,128)(2,1)S(1)}, bf16[512,512]{1,0:T(8,128)(2,1)S(1)}, u32[]{:S(2)}, u32[]{:S(2)}) collective-permute-start(bf16[512,512]{1,0:T(8,128)(2,1)S(1)} %get-tuple-element.56), channel_id=1, source_target_pairs={{0,3},{1,2},{2,1},{3,0},{4,7},{5,6},{6,5},{7,4},{8,11},{9,10},{10,... | collective-permute-start | bytes 1572872 | tf_op jit(solution)/shard_map/ppermute | solution.py:227
  17.9 0.0 copy-done
  18.0 0.0 copy-done.3
  18.0 0.0 copy-done.4
  18.0 0.0 copy-done.5
  18.0 0.1 bitcast_multiply_fusion
  18.1 0.0 collective-permute-done.2.parcel.upper
  18.1 5.2 %plane.1 = f32[4,512]{1,0:T(4,128)S(1)} custom-call(s32[2]{0:T(128)S(1)} %pad_add_fusion.place, bf16[512,512]{1,0:T(8,128)(2,1)S(1)} %get-tuple-element.46.near, bf16[512,512]{1,0:T(8,128)(2,1)S(1)} %get-tuple-element.39.far, bf16[512,256]{1,0:T(8,128)(2,1)S(1)} %get-tuple-element.47.rim, bf16[512,1280]{1,0:T(8,128)(2,1)S(1)} %collective-permute-done.2.parcel.upper, ...), custom_call_target="tpu_custom_call" | custom-call | flops 3221225472 | bytes 8388608 | tf_op jit(solution)/shard_map/plane/pallas_call | solution.py:231
  23.3 0.5 %collective-permute-start.3 = (f32[4,512]{1,0:T(4,128)S(1)}, f32[4,512]{1,0:T(4,128)S(1)}, u32[]{:S(2)}, u32[]{:S(2)}) collective-permute-start(f32[4,512]{1,0:T(4,128)S(1)} %plane.1), channel_id=1, source_target_pairs={{0,1},{1,0},{2,3},{3,2},{4,5},{5,4},{6,7},{7,6},{8,9},{9,8},{10,11... | collective-permute-start | bytes 24584 | tf_op jit(solution)/shard_map/ppermute | solution.py:255
  23.8 0.0 collective-permute-done.near_in
  23.8 0.0 collective-permute-done.1.far_in
  23.8 1.4 %early.1 = (f32[512,512]{1,0:T(8,128)S(1)}, f32[512,512]{1,0:T(8,128)S(1)}, f32[8,512]{1,0:T(8,128)S(1)}, f32[8,512]{1,0:T(8,128)S(1)}) custom-call(bf16[512,512]{1,0:T(8,128)(2,1)S(1)} %get-tuple-element.39.far, bf16[512,512]{1,0:T(8,128)(2,1)S(1)} %collective-permute-done.near_in, bf16[512,512]{1,0:T(8,128)(2,1)S(1)} %collective-permute-done.1.far_in, ...), custom_call_target="tpu_custom_call" | custom-call | flops 2147483648 | bytes 8388608 | tf_op jit(solution)/shard_map/early/pallas_call | solution.py:262
  25.2 0.0 collective-permute-done.3
  25.2 0.1 fusion.22
  25.3 4.7 %collective-permute-done.5.lower = bf16[512,512]{1,0:T(8,128)(2,1)S(1)} collective-permute-done((bf16[512,512]{1,0:T(8,128)(2,1)S(1)}, bf16[512,512]{1,0:T(8,128)(2,1)S(1)}, u32[]{:S(2)}, u32[]{:S(2)}) %collective-permute-start.5) | collective-permute-done | bytes 524320 | tf_op jit(solution)/shard_map/ppermute | solution.py:227
  30.0 0.5 %close_a.1 = f32[1,512]{1,0:T(1,128)S(1)} custom-call(bf16[512,1280]{1,0:T(8,128)(2,1)S(1)} %collective-permute-done.2.parcel.upper, bf16[512,512]{1,0:T(8,128)(2,1)S(1)} %collective-permute-done.5.lower, bf16[1024,1024]{1,0:T(8,128)(2,1)S(1)} %fusion.10.weights, f32[512,512]{1,0:T(8,128)S(1)} %get-tuple-element.57.carry, f32[8,512]{1,0:T(8,128)S(1)} %get-tuple-element.58.early), custom_call_target="tpu_custom_call" | custom-call | flops 536870912 | bytes 4194304 | tf_op jit(solution)/shard_map/close_a/pallas_call | solution.py:276
  30.6 1.1 %collective-permute-done.4.upper = bf16[512,512]{1,0:T(8,128)(2,1)S(1)} collective-permute-done((bf16[512,512]{1,0:T(8,128)(2,1)S(1)}, bf16[512,512]{1,0:T(8,128)(2,1)S(1)}, u32[]{:S(2)}, u32[]{:S(2)}) %collective-permute-start.4) | collective-permute-done | bytes 524320 | tf_op jit(solution)/shard_map/ppermute | solution.py:228
  31.6 0.5 %close_b.1 = f32[1,512]{1,0:T(1,128)S(1)} custom-call(bf16[512,512]{1,0:T(8,128)(2,1)S(1)} %collective-permute-done.4.upper, bf16[512,512]{1,0:T(8,128)(2,1)S(1)} %collective-permute-done.5.lower, bf16[1024,1024]{1,0:T(8,128)(2,1)S(1)} %fusion.10.weights, f32[512,512]{1,0:T(8,128)S(1)} %get-tuple-element.61.carry, f32[8,512]{1,0:T(8,128)S(1)} %get-tuple-element.62.early), custom_call_target="tpu_custom_call" | custom-call | flops 536870912 | bytes 4194304 | tf_op jit(solution)/shard_map/close_b/pallas_call | solution.py:276
  32.1 1.3 %collective-permute-start.7 = (f32[1,512]{1,0:T(1,128)S(1)}, f32[1,512]{1,0:T(1,128)S(1)}, u32[]{:S(2)}, u32[]{:S(2)}) collective-permute-start(f32[1,512]{1,0:T(1,128)S(1)} %close_b.1), channel_id=1, source_target_pairs={{0,2},{1,3},{2,0},{3,1},{4,6},{5,7},{6,4},{7,5},{8,10},{9,11},{10,... | collective-permute-start | bytes 6152 | tf_op jit(solution)/shard_map/ppermute | solution.py:286
  33.4 1.4 %collective-permute-start.8 = (f32[1,512]{1,0:T(1,128)S(1)}, f32[1,512]{1,0:T(1,128)S(1)}, u32[]{:S(2)}, u32[]{:S(2)}) collective-permute-start(f32[1,512]{1,0:T(1,128)S(1)} %close_b.1), channel_id=1, source_target_pairs={{0,3},{1,2},{2,1},{3,0},{4,7},{5,6},{6,5},{7,4},{8,11},{9,10},{10,... | collective-permute-start | bytes 6152 | tf_op jit(solution)/shard_map/ppermute | solution.py:285
  34.8 0.0 collective-permute-start.6
  34.8 0.9 %collective-permute-done.7 = f32[1,512]{1,0:T(1,128)S(1)} collective-permute-done((f32[1,512]{1,0:T(1,128)S(1)}, f32[1,512]{1,0:T(1,128)S(1)}, u32[]{:S(2)}, u32[]{:S(2)}) %collective-permute-start.7) | collective-permute-done | bytes 2080 | tf_op jit(solution)/shard_map/ppermute | solution.py:286
  35.8 0.6 %collective-permute-done.8 = f32[1,512]{1,0:T(1,128)S(1)} collective-permute-done((f32[1,512]{1,0:T(1,128)S(1)}, f32[1,512]{1,0:T(1,128)S(1)}, u32[]{:S(2)}, u32[]{:S(2)}) %collective-permute-start.8) | collective-permute-done | bytes 2080 | tf_op jit(solution)/shard_map/ppermute | solution.py:285
  36.4 0.0 collective-permute-done.6
  36.4 0.7 %fusion.14 = (f32[2,1024]{1,0:T(2,128)}, f32[2,1024]{1,0:T(2,128)}) fusion(f32[2,1024]{1,0:T(2,128)S(1)} %get-tuple-element.65, f32[2,1024]{1,0:T(2,128)S(1)} %get-tuple-element.64, pred[2]{0:T(512)(128)(4,1)S(1)} %iota_compare_fusion, f32[1024]{0:T(1024)S(1)} %maximum_select_fusion.5, f32[1024]{0:T(1024)S(1)} %maximum_select_fusion.4, ...), kind=kLoop, calls=%fused_computation.17 | loop fusion | flops 10240 | bytes 57346 | tf_op jit(solution)/shard_map/add | solution.py:288
  (12 shorter events, 0.1 us)
Async XLA Ops:
  2.9 5.8 %copy-start.1 = (s32[1024]{0:T(1024)S(1)}, s32[1024]{0:T(1024)}, u32[]{:S(2)}) copy-start(s32[1024]{0:T(1024)} %param.9) | copy-start | bytes 12292
  2.9 5.9 %copy-start.6 = (bf16[1024]{0:T(1024)(128)(2,1)S(1)}, bf16[1024]{0:T(1024)(128)(2,1)}, u32[]{:S(2)}) copy-start(bf16[1024]{0:T(1024)(128)(2,1)} %param.11) | copy-start | bytes 6148
  2.9 5.9 %copy-start.2 = (s32[1024,4]{0,1:T(4,128)S(1)}, s32[1024,4]{0,1:T(4,128)}, u32[]{:S(2)}) copy-start(s32[1024,4]{0,1:T(4,128)} %param.10) | copy-start | bytes 49156
  3.6 20.2 %collective-permute-start = (bf16[512,512]{1,0:T(8,128)(2,1)S(1)}, bf16[512,512]{1,0:T(8,128)(2,1)S(1)}, u32[]{:S(2)}, u32[]{:S(2)}) collective-permute-start(bf16[512,512]{1,0:T(8,128)(2,1)S(1)} %get-tuple-element.46.near), channel_id=1, source_target_pairs={{0,2},{1,3},{2,0},{3,1},{4,6},{5,7},{6,4},{7,5},{8,10},{9,11},{10,... | collective-permute-start | bytes 1572872 | tf_op jit(solution)/shard_map/ppermute | solution.py:207
  6.6 17.2 %collective-permute-start.1 = (bf16[512,512]{1,0:T(8,128)(2,1)S(1)}, bf16[512,512]{1,0:T(8,128)(2,1)S(1)}, u32[]{:S(2)}, u32[]{:S(2)}) collective-permute-start(bf16[512,512]{1,0:T(8,128)(2,1)S(1)} %get-tuple-element.39.far), channel_id=1, source_target_pairs={{4,0},{5,1},{8,4},{9,5},{12,8},{13,9},{2,6},{3,7},{6,10},{7,11},{1... | collective-permute-start | bytes 1572872 | tf_op jit(solution)/shard_map/ppermute | solution.py:208
  8.7 9.4 %collective-permute-start.2 = (bf16[512,1280]{1,0:T(8,128)(2,1)S(1)}, bf16[512,1280]{1,0:T(8,128)(2,1)S(1)}, u32[]{:S(2)}, u32[]{:S(2)}) collective-permute-start(bf16[512,1280]{1,0:T(8,128)(2,1)S(1)} %get-tuple-element.48), channel_id=1, source_target_pairs={{0,1},{1,0},{2,3},{3,2},{4,5},{5,4},{6,7},{7,6},{8,9},{9,8},{10,11... | collective-permute-start | bytes 3932168 | tf_op jit(solution)/shard_map/ppermute | solution.py:218
  11.7 6.3 %copy-start = (f32[3,2,1024]{2,1,0:T(2,128)S(1)}, f32[3,2,1024]{2,1,0:T(2,128)}, u32[]{:S(2)}) copy-start(f32[3,2,1024]{2,1,0:T(2,128)} %param.15) | copy-start | bytes 73732
  11.7 6.3 %copy-start.3 = (f32[2,1024]{1,0:T(2,128)S(1)}, f32[2,1024]{1,0:T(2,128)}, u32[]{:S(2)}) copy-start(f32[2,1024]{1,0:T(2,128)} %param.13) | copy-start | bytes 24580
  11.7 6.3 %copy-start.4 = (f32[2,1024]{1,0:T(2,128)S(1)}, f32[2,1024]{1,0:T(2,128)}, u32[]{:S(2)}) copy-start(f32[2,1024]{1,0:T(2,128)} %param.14) | copy-start | bytes 24580
  11.7 6.3 %copy-start.5 = (f32[2,1024]{1,0:T(2,128)S(1)}, f32[2,1024]{1,0:T(2,128)}, u32[]{:S(2)}) copy-start(f32[2,1024]{1,0:T(2,128)} %param.12) | copy-start | bytes 24580
  11.9 19.7 %collective-permute-start.4 = (bf16[512,512]{1,0:T(8,128)(2,1)S(1)}, bf16[512,512]{1,0:T(8,128)(2,1)S(1)}, u32[]{:S(2)}, u32[]{:S(2)}) collective-permute-start(bf16[512,512]{1,0:T(8,128)(2,1)S(1)} %get-tuple-element.55), channel_id=1, source_target_pairs={{4,1},{5,0},{8,5},{9,4},{12,9},{13,8},{2,7},{3,6},{6,11},{7,10},{1... | collective-permute-start | bytes 1572872 | tf_op jit(solution)/shard_map/ppermute | solution.py:228
  13.2 16.8 %collective-permute-start.5 = (bf16[512,512]{1,0:T(8,128)(2,1)S(1)}, bf16[512,512]{1,0:T(8,128)(2,1)S(1)}, u32[]{:S(2)}, u32[]{:S(2)}) collective-permute-start(bf16[512,512]{1,0:T(8,128)(2,1)S(1)} %get-tuple-element.56), channel_id=1, source_target_pairs={{0,3},{1,2},{2,1},{3,0},{4,7},{5,6},{6,5},{7,4},{8,11},{9,10},{10,... | collective-permute-start | bytes 1572872 | tf_op jit(solution)/shard_map/ppermute | solution.py:227
  23.3 1.9 %collective-permute-start.3 = (f32[4,512]{1,0:T(4,128)S(1)}, f32[4,512]{1,0:T(4,128)S(1)}, u32[]{:S(2)}, u32[]{:S(2)}) collective-permute-start(f32[4,512]{1,0:T(4,128)S(1)} %plane.1), channel_id=1, source_target_pairs={{0,1},{1,0},{2,3},{3,2},{4,5},{5,4},{6,7},{7,6},{8,9},{9,8},{10,11... | collective-permute-start | bytes 24584 | tf_op jit(solution)/shard_map/ppermute | solution.py:255
  32.1 3.7 %collective-permute-start.7 = (f32[1,512]{1,0:T(1,128)S(1)}, f32[1,512]{1,0:T(1,128)S(1)}, u32[]{:S(2)}, u32[]{:S(2)}) collective-permute-start(f32[1,512]{1,0:T(1,128)S(1)} %close_b.1), channel_id=1, source_target_pairs={{0,2},{1,3},{2,0},{3,1},{4,6},{5,7},{6,4},{7,5},{8,10},{9,11},{10,... | collective-permute-start | bytes 6152 | tf_op jit(solution)/shard_map/ppermute | solution.py:286
  33.4 3.0 %collective-permute-start.8 = (f32[1,512]{1,0:T(1,128)S(1)}, f32[1,512]{1,0:T(1,128)S(1)}, u32[]{:S(2)}, u32[]{:S(2)}) collective-permute-start(f32[1,512]{1,0:T(1,128)S(1)} %close_b.1), channel_id=1, source_target_pairs={{0,3},{1,2},{2,1},{3,0},{4,7},{5,6},{6,5},{7,4},{8,11},{9,10},{10,... | collective-permute-start | bytes 6152 | tf_op jit(solution)/shard_map/ppermute | solution.py:285
  34.8 1.6 %collective-permute-start.6 = (f32[1,512]{1,0:T(1,128)S(1)}, f32[1,512]{1,0:T(1,128)S(1)}, u32[]{:S(2)}, u32[]{:S(2)}) collective-permute-start(f32[1,512]{1,0:T(1,128)S(1)} %close_a.1), channel_id=1, source_target_pairs={{0,1},{1,0},{2,3},{3,2},{4,5},{5,4},{6,7},{7,6},{8,9},{9,8},{10,11... | collective-permute-start | bytes 6152 | tf_op jit(solution)/shard_map/ppermute | solution.py:281

commit v5 on v4

--- a/solution.py
+++ b/solution.py
@@ -11,9 +11,8 @@
 VMEM = pl.BlockSpec(memory_space=pltpu.VMEM)
 SMEM = pl.BlockSpec(memory_space=pltpu.SMEM)
 MIB = 2**20
-LATER = True
+FIRST = 51
 HOLD = True
-AFTER = True
 
 
 def call(kernel, outs, specs, name, scratch=(), limit=8, flops=0, moved=0):
@@ -33,34 +32,48 @@
     return jnp.dot(left, right, preferred_element_type=jnp.float32)
 
 
-def keep_kernel(place, field, near, far):
+def levels(block, odd):
+    layers = jnp.swapaxes(block, 0, 1)
+    return jnp.where(odd == 1, layers[0], layers[1]), jnp.where(odd == 1, layers[1], layers[0])
+
+
+def keep_kernel(place, potentials, near, far, raw, sems):
     odd, core = place[0], place[1]
-    half = near.shape[1]
-    for k in range(2):
-
-        @pl.when(core == k)
-        def _():
-            near[...] = field[1 - odd, :, k * half : (k + 1) * half]
-            far[...] = field[odd, :, k * half : (k + 1) * half]
-
-
-def give_kernel(place, field, near, far, parcel, rim):
+    rows, half = near.shape
+    size = rows // sems.shape[0]
+    cells = pl.ds(pl.multiple_of(core * half, LANES), half)
+    copies = []
+    for i in range(sems.shape[0]):
+        part = pl.ds(i * size, size)
+        copies.append(pltpu.make_async_copy(potentials.at[part, :, cells], raw.at[part], sems.at[i]))
+        copies[-1].start()
+    for i, copy in enumerate(copies):
+        copy.wait()
+        for r in range(i * size, (i + 1) * size, 32):
+            near[r : r + 32, :], far[r : r + 32, :] = levels(raw[r : r + 32], odd)
+
+
+def give_kernel(place, potentials, near, far, parcel, rim):
     odd, core = place[0], place[1]
-    half = near.shape[1]
+    rows, half = near.shape
     for k in range(2):
         low, high = slice(half - LANES, half), slice(half, half + LANES)
         inner, outer = (low, high) if k == 0 else (high, low)
+        theirs = slice((1 - k) * half, (2 - k) * half)
 
         @pl.when(core == k)
         def _():
-            near[...] = field[1 - odd, :, (1 - k) * half : (2 - k) * half]
-            far[...] = field[odd, :, (1 - k) * half : (2 - k) * half]
-            parcel[:, :half] = field[1 - odd, :, (1 - k) * half : (2 - k) * half]
-            parcel[:, half : 2 * half] = field[odd, :, (1 - k) * half : (2 - k) * half]
-            parcel[:, 2 * half : 2 * half + LANES] = field[1 - odd, :, inner]
-            parcel[:, 2 * half + LANES :] = field[odd, :, inner]
-            rim[:, :LANES] = field[1 - odd, :, outer]
-            rim[:, LANES:] = field[odd, :, outer]
+            for r in range(0, rows, 32):
+                at = slice(r, r + 32)
+                near_v, far_v = levels(potentials[at], odd)
+                near[at, :] = near_v[:, theirs]
+                far[at, :] = far_v[:, theirs]
+                parcel[at, :half] = near_v[:, theirs]
+                parcel[at, half : 2 * half] = far_v[:, theirs]
+                parcel[at, 2 * half : 2 * half + LANES] = near_v[:, inner]
+                parcel[at, 2 * half + LANES :] = far_v[:, inner]
+                rim[at, :LANES] = near_v[:, outer]
+                rim[at, LANES:] = far_v[:, outer]
 
 
 def cross_kernel(weights, out):
@@ -200,25 +213,32 @@
     def joint(pairs, cross):
         return [(2 * i + k, 2 * j + (k ^ cross)) for i, j in pairs for k in range(2)]
 
-    field = jnp.transpose(potentials, (1, 0, 2))
     piece = shape((rows, half), bf16)
     strip = shape((rows, 2 * LANES), bf16)
-    near, far = call(keep_kernel, (piece,) * 2, [SMEM, VMEM], "keep", moved=rows * cells * 4, limit=2)(place, field)
+    near, far = call(
+        keep_kernel,
+        (piece,) * 2,
+        [SMEM, pl.BlockSpec(memory_space=pl.ANY)],
+        "keep",
+        scratch=[pltpu.VMEM((rows, layers, half), bf16), pltpu.SemaphoreType.DMA((4,))],
+        moved=rows * cells * 4,
+        limit=FIRST,
+    )(place, potentials)
     near_in_0 = lax.ppermute(near, both, joint(to_mate, 0))
     far_in_0 = lax.ppermute(far, both, joint(ahead, 0))
-    field, near, far = lax.optimization_barrier((field, near, far))
+    place_b, near, far, potentials = lax.optimization_barrier((place, near, far, potentials))
     near_give, far_give, parcel, rim = call(
         give_kernel,
         (piece, piece, shape((rows, 2 * half + 2 * LANES), bf16), strip),
         [SMEM, VMEM],
         "give",
         moved=rows * cells * 8,
-        limit=2,
-    )(place, field)
+        limit=4,
+    )(place_b, potentials)
     parcel = lax.ppermute(parcel, "elec", swap)
 
     order = jnp.where(low_core, elec_order, jnp.concatenate([elec_order[rows:], elec_order[:rows]]))
-    if AFTER:
+    if True:
         quadripoles, near_give = lax.optimization_barrier((quadripoles, near_give))
     weights = assemble(quadripoles, weighted_misfit, order)
     cross = call(cross_kernel, shape((rows, rows), bf16), [VMEM], "cross", moved=4 * rows * rows * 2)(weights)

time: 37.3 us -> 36.6 us (0.981)
  local copies, waits for them, and re-layouts: 2.28 us -> 0.08 us
  Pallas kernels: 9.24 us -> 10.7 us
    optimization_barrier x1 -> x0, local copies, waits for them, and re-layouts: 2.2 us -> none  [local(): lax.optimization_barrier((potentials, odd, c, low_core, near_level))]
    pallas_call x1, Pallas kernels: 0.62 us -> 1.89 us  [local(): call(keep_kernel, (piece,) * 2, [SMEM, pl.BlockSpec(memory_space=pl.ANY)]...]
  transfers between devices with their start and end apart: 9 -> 9, of which waited for: 4 -> 4; matrix products, arithmetic and copies ran while one was open for 8% -> 8% of each run, Pallas kernels for 22% -> 23%
where the time goes in v5:
time: 36.6 us; the launch traced here: 36.4 us
  starting transfers between devices  13.6 us (37%)
  Pallas kernels  10.7 us (29%)
  waiting for transfers between devices  7.37 us (20%)
  matrix products  2.81 us (8%)
  other arithmetic  0.97 us (3%)
  between operations  0.92 us (3%)
    pallas_call x1, Pallas kernels, local(): call(plane_kernel, shape((2 * layers, half), f32), [SMEM] + [VMEM] * 6, '...  5.22 us
    ppermute x1, waiting for transfers between devices, local(): near_in_1 = lax.ppermute(near_give, both, joint(to_mate, 1))  4.71 us
    ppermute x1, starting transfers between devices, local(): near_in_1 = lax.ppermute(near_give, both, joint(to_mate, 1))  4.7 us
    ppermute x1, starting transfers between devices, local(): near_in_0 = lax.ppermute(near, both, joint(to_mate, 0))  3.03 us
    dot_general x1, matrix products, dot(): return jnp.dot(left, right, preferred_element_type=jnp.float32)  2.81 us
    pallas_call x1, Pallas kernels, local(): call(keep_kernel, (piece,) * 2, [SMEM, pl.BlockSpec(memory_space=pl.ANY)]...  1.89 us
    ppermute x1, starting transfers between devices, local(): b_same = lax.ppermute(form_b, both, joint(to_mate, 0))  1.52 us
    pallas_call x1, Pallas kernels, local(): call(early_kernel, (shape((rows, half), f32),) * 2 + (shape((8, half), f3...  1.37 us
  transfers between devices with their start and end apart: 9, of which 4 were waited for; matrix products, arithmetic and copies ran while one was open for 8% of the time, Pallas kernels for 23%

profile of v5, /device:TPU:0, one launch (start us, length us, event | category | flops | bytes accessed | tf_op | source)
XLA Modules:
  0.0 36.4 jit_solution(2961653836473644764)
XLA Ops:
  0.6 0.0 copy-start
  0.7 0.1 pad_add_fusion.place
  0.7 0.0 copy-start.2
  0.7 0.0 copy-start.7
  0.7 0.0 copy-start.3
  0.7 1.9 %keep.1 = (bf16[512,512]{1,0:T(8,128)(2,1)S(1)}, bf16[512,512]{1,0:T(8,128)(2,1)S(1)}) custom-call(s32[2]{0:T(128)S(1)} %pad_add_fusion.place, bf16[512,2,1024]{2,1,0:T(2,128)(2,1)} %potentials.1), custom_call_target="tpu_custom_call" | custom-call | bytes 2097152 | tf_op jit(solution)/shard_map/keep/pallas_call | solution.py:218
  2.6 3.0 %collective-permute-start = (bf16[512,512]{1,0:T(8,128)(2,1)S(1)}, bf16[512,512]{1,0:T(8,128)(2,1)S(1)}, u32[]{:S(2)}, u32[]{:S(2)}) collective-permute-start(bf16[512,512]{1,0:T(8,128)(2,1)S(1)} %get-tuple-element.48.near), channel_id=1, source_target_pairs={{0,2},{1,3},{2,0},{3,1},{4,6},{5,7},{6,4},{7,5},{8,10},{9,11},{10,... | collective-permute-start | bytes 1572872 | tf_op jit(solution)/shard_map/ppermute | solution.py:227
  5.7 1.3 %collective-permute-start.1 = (bf16[512,512]{1,0:T(8,128)(2,1)S(1)}, bf16[512,512]{1,0:T(8,128)(2,1)S(1)}, u32[]{:S(2)}, u32[]{:S(2)}) collective-permute-start(bf16[512,512]{1,0:T(8,128)(2,1)S(1)} %get-tuple-element.40.far), channel_id=1, source_target_pairs={{4,0},{5,1},{8,4},{9,5},{12,8},{13,9},{2,6},{3,7},{6,10},{7,11},{1... | collective-permute-start | bytes 1572872 | tf_op jit(solution)/shard_map/ppermute | solution.py:228
  7.0 0.0 copy-done
  7.0 1.0 %give.1 = (bf16[512,512]{1,0:T(8,128)(2,1)S(1)}, bf16[512,512]{1,0:T(8,128)(2,1)S(1)}, bf16[512,1280]{1,0:T(8,128)(2,1)S(1)}, bf16[512,256]{1,0:T(8,128)(2,1)S(1)}) custom-call(s32[2]{0:T(128)S(1)} %pad_add_fusion.place, bf16[512,2,1024]{2,1,0:T(2,128)(2,1)S(1)} %copy-done), custom_call_target="tpu_custom_call" | custom-call | bytes 4194304 | tf_op jit(solution)/shard_map/give/pallas_call | solution.py:230
  8.0 0.1 collective-permute-start.2
  8.1 0.0 copy-done.2
  8.1 0.0 copy-done.7
  8.1 0.0 copy-done.3
  8.2 2.8 %fusion.10.weights = bf16[1024,1024]{1,0:T(8,128)(2,1)S(1)} fusion(s32[1024]{0:T(1024)S(1)} %add_select_fusion.1, f32[1024]{0:T(1024)S(1)} %convert_element_type.23, s32[1024]{0:T(1024)S(1)} %bitcast.41, s32[1024]{0:T(1024)S(1)} %bitcast.42, s32[1024]{0:T(1024)S(1)} %bitcast.43, s32[1024]{0:T(1024)S(1)} %bitcast.40), kind=kOutput, calls=%fused_computation.12 | convolution fusion | flops 2161115136 | bytes 2121728 | tf_op jit(solution)/shard_map/dot_general | solution.py:32
  11.0 0.0 copy-start.1
  11.0 0.0 copy-start.4
  11.0 0.0 copy-start.5
  11.0 0.0 copy-start.6
  11.0 0.2 cross.1
  11.3 1.3 %collective-permute-start.4 = (bf16[512,512]{1,0:T(8,128)(2,1)S(1)}, bf16[512,512]{1,0:T(8,128)(2,1)S(1)}, u32[]{:S(2)}, u32[]{:S(2)}) collective-permute-start(bf16[512,512]{1,0:T(8,128)(2,1)S(1)} %get-tuple-element.57), channel_id=1, source_target_pairs={{4,1},{5,0},{8,5},{9,4},{12,9},{13,8},{2,7},{3,6},{6,11},{7,10},{1... | collective-permute-start | bytes 1572872 | tf_op jit(solution)/shard_map/ppermute | solution.py:248
  12.6 4.7 %collective-permute-start.5 = (bf16[512,512]{1,0:T(8,128)(2,1)S(1)}, bf16[512,512]{1,0:T(8,128)(2,1)S(1)}, u32[]{:S(2)}, u32[]{:S(2)}) collective-permute-start(bf16[512,512]{1,0:T(8,128)(2,1)S(1)} %get-tuple-element.58), channel_id=1, source_target_pairs={{0,3},{1,2},{2,1},{3,0},{4,7},{5,6},{6,5},{7,4},{8,11},{9,10},{10,... | collective-permute-start | bytes 1572872 | tf_op jit(solution)/shard_map/ppermute | solution.py:247
  17.3 0.0 copy-done.1
  17.3 0.0 copy-done.4
  17.3 0.0 copy-done.5
  17.3 0.0 copy-done.6
  17.3 0.1 bitcast_multiply_fusion
  17.4 0.0 collective-permute-done.2.parcel.upper
  17.4 5.2 %plane.1 = f32[4,512]{1,0:T(4,128)S(1)} custom-call(s32[2]{0:T(128)S(1)} %pad_add_fusion.place, bf16[512,512]{1,0:T(8,128)(2,1)S(1)} %get-tuple-element.48.near, bf16[512,512]{1,0:T(8,128)(2,1)S(1)} %get-tuple-element.40.far, bf16[512,256]{1,0:T(8,128)(2,1)S(1)} %get-tuple-element.49.rim, bf16[512,1280]{1,0:T(8,128)(2,1)S(1)} %collective-permute-done.2.parcel.upper, ...), custom_call_target="tpu_custom_call" | custom-call | flops 3221225472 | bytes 8388608 | tf_op jit(solution)/shard_map/plane/pallas_call | solution.py:251
  22.6 0.5 %collective-permute-start.3 = (f32[4,512]{1,0:T(4,128)S(1)}, f32[4,512]{1,0:T(4,128)S(1)}, u32[]{:S(2)}, u32[]{:S(2)}) collective-permute-start(f32[4,512]{1,0:T(4,128)S(1)} %plane.1), channel_id=1, source_target_pairs={{0,1},{1,0},{2,3},{3,2},{4,5},{5,4},{6,7},{7,6},{8,9},{9,8},{10,11... | collective-permute-start | bytes 24584 | tf_op jit(solution)/shard_map/ppermute | solution.py:275
  23.1 0.0 collective-permute-done.near_in
  23.1 0.0 collective-permute-done.1.far_in
  23.1 1.4 %early.1 = (f32[512,512]{1,0:T(8,128)S(1)}, f32[512,512]{1,0:T(8,128)S(1)}, f32[8,512]{1,0:T(8,128)S(1)}, f32[8,512]{1,0:T(8,128)S(1)}) custom-call(bf16[512,512]{1,0:T(8,128)(2,1)S(1)} %get-tuple-element.40.far, bf16[512,512]{1,0:T(8,128)(2,1)S(1)} %collective-permute-done.near_in, bf16[512,512]{1,0:T(8,128)(2,1)S(1)} %collective-permute-done.1.far_in, ...), custom_call_target="tpu_custom_call" | custom-call | flops 2147483648 | bytes 8388608 | tf_op jit(solution)/shard_map/early/pallas_call | solution.py:282
  24.5 0.0 collective-permute-done.3
  24.5 0.1 fusion.22
  24.6 4.7 %collective-permute-done.5.lower = bf16[512,512]{1,0:T(8,128)(2,1)S(1)} collective-permute-done((bf16[512,512]{1,0:T(8,128)(2,1)S(1)}, bf16[512,512]{1,0:T(8,128)(2,1)S(1)}, u32[]{:S(2)}, u32[]{:S(2)}) %collective-permute-start.5) | collective-permute-done | bytes 524320 | tf_op jit(solution)/shard_map/ppermute | solution.py:247
  29.4 0.5 %close_a.1 = f32[1,512]{1,0:T(1,128)S(1)} custom-call(bf16[512,1280]{1,0:T(8,128)(2,1)S(1)} %collective-permute-done.2.parcel.upper, bf16[512,512]{1,0:T(8,128)(2,1)S(1)} %collective-permute-done.5.lower, bf16[1024,1024]{1,0:T(8,128)(2,1)S(1)} %fusion.10.weights, f32[512,512]{1,0:T(8,128)S(1)} %get-tuple-element.59.carry, f32[8,512]{1,0:T(8,128)S(1)} %get-tuple-element.60.early), custom_call_target="tpu_custom_call" | custom-call | flops 536870912 | bytes 4194304 | tf_op jit(solution)/shard_map/close_a/pallas_call | solution.py:296
  29.9 0.8 %collective-permute-done.4.upper = bf16[512,512]{1,0:T(8,128)(2,1)S(1)} collective-permute-done((bf16[512,512]{1,0:T(8,128)(2,1)S(1)}, bf16[512,512]{1,0:T(8,128)(2,1)S(1)}, u32[]{:S(2)}, u32[]{:S(2)}) %collective-permute-start.4) | collective-permute-done | bytes 524320 | tf_op jit(solution)/shard_map/ppermute | solution.py:248
  30.7 0.5 %close_b.1 = f32[1,512]{1,0:T(1,128)S(1)} custom-call(bf16[512,512]{1,0:T(8,128)(2,1)S(1)} %collective-permute-done.4.upper, bf16[512,512]{1,0:T(8,128)(2,1)S(1)} %collective-permute-done.5.lower, bf16[1024,1024]{1,0:T(8,128)(2,1)S(1)} %fusion.10.weights, f32[512,512]{1,0:T(8,128)S(1)} %get-tuple-element.63.carry, f32[8,512]{1,0:T(8,128)S(1)} %get-tuple-element.64.early), custom_call_target="tpu_custom_call" | custom-call | flops 536870912 | bytes 4194304 | tf_op jit(solution)/shard_map/close_b/pallas_call | solution.py:296
  31.2 1.5 %collective-permute-start.7 = (f32[1,512]{1,0:T(1,128)S(1)}, f32[1,512]{1,0:T(1,128)S(1)}, u32[]{:S(2)}, u32[]{:S(2)}) collective-permute-start(f32[1,512]{1,0:T(1,128)S(1)} %close_b.1), channel_id=1, source_target_pairs={{0,2},{1,3},{2,0},{3,1},{4,6},{5,7},{6,4},{7,5},{8,10},{9,11},{10,... | collective-permute-start | bytes 6152 | tf_op jit(solution)/shard_map/ppermute | solution.py:306
  32.7 1.2 %collective-permute-start.8 = (f32[1,512]{1,0:T(1,128)S(1)}, f32[1,512]{1,0:T(1,128)S(1)}, u32[]{:S(2)}, u32[]{:S(2)}) collective-permute-start(f32[1,512]{1,0:T(1,128)S(1)} %close_b.1), channel_id=1, source_target_pairs={{0,3},{1,2},{2,1},{3,0},{4,7},{5,6},{6,5},{7,4},{8,11},{9,10},{10,... | collective-permute-start | bytes 6152 | tf_op jit(solution)/shard_map/ppermute | solution.py:305
  33.9 0.0 collective-permute-start.6
  33.9 0.9 %collective-permute-done.7 = f32[1,512]{1,0:T(1,128)S(1)} collective-permute-done((f32[1,512]{1,0:T(1,128)S(1)}, f32[1,512]{1,0:T(1,128)S(1)}, u32[]{:S(2)}, u32[]{:S(2)}) %collective-permute-start.7) | collective-permute-done | bytes 2080 | tf_op jit(solution)/shard_map/ppermute | solution.py:306
  34.9 0.9 %collective-permute-done.8 = f32[1,512]{1,0:T(1,128)S(1)} collective-permute-done((f32[1,512]{1,0:T(1,128)S(1)}, f32[1,512]{1,0:T(1,128)S(1)}, u32[]{:S(2)}, u32[]{:S(2)}) %collective-permute-start.8) | collective-permute-done | bytes 2080 | tf_op jit(solution)/shard_map/ppermute | solution.py:305
  35.7 0.0 collective-permute-done.6
  35.8 0.7 %fusion.14 = (f32[2,1024]{1,0:T(2,128)}, f32[2,1024]{1,0:T(2,128)}) fusion(f32[2,1024]{1,0:T(2,128)S(1)} %get-tuple-element.67, f32[2,1024]{1,0:T(2,128)S(1)} %get-tuple-element.66, pred[2]{0:T(512)(128)(4,1)S(1)} %iota_compare_fusion, f32[1024]{0:T(1024)S(1)} %maximum_select_fusion.5, f32[1024]{0:T(1024)S(1)} %maximum_select_fusion.4, ...), kind=kLoop, calls=%fused_computation.16 | loop fusion | flops 10240 | bytes 57346 | tf_op jit(solution)/shard_map/add | solution.py:308
  (12 shorter events, 0.1 us)
Async XLA Ops:
  0.6 6.3 %copy-start = (bf16[512,2,1024]{2,1,0:T(2,128)(2,1)S(1)}, bf16[512,2,1024]{2,1,0:T(2,128)(2,1)}, u32[]{:S(2)}) copy-start(bf16[512,2,1024]{2,1,0:T(2,128)(2,1)} %potentials.1) | copy-start | bytes 6291460
  0.7 7.3 %copy-start.2 = (s32[1024]{0:T(1024)S(1)}, s32[1024]{0:T(1024)}, u32[]{:S(2)}) copy-start(s32[1024]{0:T(1024)} %param.9) | copy-start | bytes 12292
  0.7 7.4 %copy-start.7 = (bf16[1024]{0:T(1024)(128)(2,1)S(1)}, bf16[1024]{0:T(1024)(128)(2,1)}, u32[]{:S(2)}) copy-start(bf16[1024]{0:T(1024)(128)(2,1)} %param.11) | copy-start | bytes 6148
  0.7 7.4 %copy-start.3 = (s32[1024,4]{0,1:T(4,128)S(1)}, s32[1024,4]{0,1:T(4,128)}, u32[]{:S(2)}) copy-start(s32[1024,4]{0,1:T(4,128)} %param.10) | copy-start | bytes 49156
  2.6 20.5 %collective-permute-start = (bf16[512,512]{1,0:T(8,128)(2,1)S(1)}, bf16[512,512]{1,0:T(8,128)(2,1)S(1)}, u32[]{:S(2)}, u32[]{:S(2)}) collective-permute-start(bf16[512,512]{1,0:T(8,128)(2,1)S(1)} %get-tuple-element.48.near), channel_id=1, source_target_pairs={{0,2},{1,3},{2,0},{3,1},{4,6},{5,7},{6,4},{7,5},{8,10},{9,11},{10,... | collective-permute-start | bytes 1572872 | tf_op jit(solution)/shard_map/ppermute | solution.py:227
  5.7 17.4 %collective-permute-start.1 = (bf16[512,512]{1,0:T(8,128)(2,1)S(1)}, bf16[512,512]{1,0:T(8,128)(2,1)S(1)}, u32[]{:S(2)}, u32[]{:S(2)}) collective-permute-start(bf16[512,512]{1,0:T(8,128)(2,1)S(1)} %get-tuple-element.40.far), channel_id=1, source_target_pairs={{4,0},{5,1},{8,4},{9,5},{12,8},{13,9},{2,6},{3,7},{6,10},{7,11},{1... | collective-permute-start | bytes 1572872 | tf_op jit(solution)/shard_map/ppermute | solution.py:228
  8.0 9.4 %collective-permute-start.2 = (bf16[512,1280]{1,0:T(8,128)(2,1)S(1)}, bf16[512,1280]{1,0:T(8,128)(2,1)S(1)}, u32[]{:S(2)}, u32[]{:S(2)}) collective-permute-start(bf16[512,1280]{1,0:T(8,128)(2,1)S(1)} %get-tuple-element.50), channel_id=1, source_target_pairs={{0,1},{1,0},{2,3},{3,2},{4,5},{5,4},{6,7},{7,6},{8,9},{9,8},{10,11... | collective-permute-start | bytes 3932168 | tf_op jit(solution)/shard_map/ppermute | solution.py:238
  11.0 6.3 %copy-start.1 = (f32[3,2,1024]{2,1,0:T(2,128)S(1)}, f32[3,2,1024]{2,1,0:T(2,128)}, u32[]{:S(2)}) copy-start(f32[3,2,1024]{2,1,0:T(2,128)} %param.15) | copy-start | bytes 73732
  11.0 6.3 %copy-start.4 = (f32[2,1024]{1,0:T(2,128)S(1)}, f32[2,1024]{1,0:T(2,128)}, u32[]{:S(2)}) copy-start(f32[2,1024]{1,0:T(2,128)} %param.13) | copy-start | bytes 24580
  11.0 6.3 %copy-start.5 = (f32[2,1024]{1,0:T(2,128)S(1)}, f32[2,1024]{1,0:T(2,128)}, u32[]{:S(2)}) copy-start(f32[2,1024]{1,0:T(2,128)} %param.14) | copy-start | bytes 24580
  11.0 6.3 %copy-start.6 = (f32[2,1024]{1,0:T(2,128)S(1)}, f32[2,1024]{1,0:T(2,128)}, u32[]{:S(2)}) copy-start(f32[2,1024]{1,0:T(2,128)} %param.12) | copy-start | bytes 24580
  11.3 19.4 %collective-permute-start.4 = (bf16[512,512]{1,0:T(8,128)(2,1)S(1)}, bf16[512,512]{1,0:T(8,128)(2,1)S(1)}, u32[]{:S(2)}, u32[]{:S(2)}) collective-permute-start(bf16[512,512]{1,0:T(8,128)(2,1)S(1)} %get-tuple-element.57), channel_id=1, source_target_pairs={{4,1},{5,0},{8,5},{9,4},{12,9},{13,8},{2,7},{3,6},{6,11},{7,10},{1... | collective-permute-start | bytes 1572872 | tf_op jit(solution)/shard_map/ppermute | solution.py:248
  12.6 16.8 %collective-permute-start.5 = (bf16[512,512]{1,0:T(8,128)(2,1)S(1)}, bf16[512,512]{1,0:T(8,128)(2,1)S(1)}, u32[]{:S(2)}, u32[]{:S(2)}) collective-permute-start(bf16[512,512]{1,0:T(8,128)(2,1)S(1)} %get-tuple-element.58), channel_id=1, source_target_pairs={{0,3},{1,2},{2,1},{3,0},{4,7},{5,6},{6,5},{7,4},{8,11},{9,10},{10,... | collective-permute-start | bytes 1572872 | tf_op jit(solution)/shard_map/ppermute | solution.py:247
  22.6 1.9 %collective-permute-start.3 = (f32[4,512]{1,0:T(4,128)S(1)}, f32[4,512]{1,0:T(4,128)S(1)}, u32[]{:S(2)}, u32[]{:S(2)}) collective-permute-start(f32[4,512]{1,0:T(4,128)S(1)} %plane.1), channel_id=1, source_target_pairs={{0,1},{1,0},{2,3},{3,2},{4,5},{5,4},{6,7},{7,6},{8,9},{9,8},{10,11... | collective-permute-start | bytes 24584 | tf_op jit(solution)/shard_map/ppermute | solution.py:275
  31.2 3.7 %collective-permute-start.7 = (f32[1,512]{1,0:T(1,128)S(1)}, f32[1,512]{1,0:T(1,128)S(1)}, u32[]{:S(2)}, u32[]{:S(2)}) collective-permute-start(f32[1,512]{1,0:T(1,128)S(1)} %close_b.1), channel_id=1, source_target_pairs={{0,2},{1,3},{2,0},{3,1},{4,6},{5,7},{6,4},{7,5},{8,10},{9,11},{10,... | collective-permute-start | bytes 6152 | tf_op jit(solution)/shard_map/ppermute | solution.py:306
  32.7 3.0 %collective-permute-start.8 = (f32[1,512]{1,0:T(1,128)S(1)}, f32[1,512]{1,0:T(1,128)S(1)}, u32[]{:S(2)}, u32[]{:S(2)}) collective-permute-start(f32[1,512]{1,0:T(1,128)S(1)} %close_b.1), channel_id=1, source_target_pairs={{0,3},{1,2},{2,1},{3,0},{4,7},{5,6},{6,5},{7,4},{8,11},{9,10},{10,... | collective-permute-start | bytes 6152 | tf_op jit(solution)/shard_map/ppermute | solution.py:305
  33.9 1.8 %collective-permute-start.6 = (f32[1,512]{1,0:T(1,128)S(1)}, f32[1,512]{1,0:T(1,128)S(1)}, u32[]{:S(2)}, u32[]{:S(2)}) collective-permute-start(f32[1,512]{1,0:T(1,128)S(1)} %close_a.1), channel_id=1, source_target_pairs={{0,1},{1,0},{2,3},{3,2},{4,5},{5,4},{6,7},{7,6},{8,9},{9,8},{10,11... | collective-permute-start | bytes 6152 | tf_op jit(solution)/shard_map/ppermute | solution.py:301

commit v6 on v5

--- a/solution.py
+++ b/solution.py
@@ -9,7 +9,6 @@
 NX = 32
 LANES = 128
 VMEM = pl.BlockSpec(memory_space=pltpu.VMEM)
-SMEM = pl.BlockSpec(memory_space=pltpu.SMEM)
 MIB = 2**20
 FIRST = 51
 HOLD = True
@@ -32,13 +31,20 @@
     return jnp.dot(left, right, preferred_element_type=jnp.float32)
 
 
+def spot():
+    index = lax.axis_index("space")
+    odd = lax.rem(index, 2)
+    inside = jnp.where(odd == 1, index >= 2, index + 2 < lax.axis_size("space"))
+    return odd, lax.axis_index("elec"), inside
+
+
 def levels(block, odd):
     layers = jnp.swapaxes(block, 0, 1)
     return jnp.where(odd == 1, layers[0], layers[1]), jnp.where(odd == 1, layers[1], layers[0])
 
 
-def keep_kernel(place, potentials, near, far, raw, sems):
-    odd, core = place[0], place[1]
+def keep_kernel(potentials, near, far, raw, sems):
+    odd, core, _ = spot()
     rows, half = near.shape
     size = rows // sems.shape[0]
     cells = pl.ds(pl.multiple_of(core * half, LANES), half)
@@ -53,8 +59,8 @@
             near[r : r + 32, :], far[r : r + 32, :] = levels(raw[r : r + 32], odd)
 
 
-def give_kernel(place, potentials, near, far, parcel, rim):
-    odd, core = place[0], place[1]
+def give_kernel(potentials, near, far, parcel, rim):
+    odd, core, _ = spot()
     rows, half = near.shape
     for k in range(2):
         low, high = slice(half - LANES, half), slice(half, half + LANES)
@@ -104,8 +110,8 @@
     return out
 
 
-def plane_kernel(place, near, far, rim, parcel, weights, cross, out, delta):
-    first = place[1] == 0
+def plane_kernel(near, far, rim, parcel, weights, cross, out, delta):
+    first = spot()[1] == 0
     rows, half = near.shape
     count = half // LANES
     step = 128
@@ -147,18 +153,19 @@
             out[2 * layer + part : 2 * layer + part + 1, :] = total[:1]
 
 
-def differences(far, near_in, far_in, rows):
+def differences(inside, far, near_in, far_in, rows):
     near_v = near_in[rows, :].astype(jnp.float32)
     change_a = far[rows, :].astype(jnp.float32) - near_v
-    change_b = far_in[rows, :].astype(jnp.float32) - near_v
+    change_b = jnp.where(inside, far_in[rows, :].astype(jnp.float32), 0.0) - near_v
     return change_a.astype(jnp.bfloat16), change_b.astype(jnp.bfloat16)
 
 
 def early_kernel(far, near_in, far_in, weights, cross, carry_a, carry_b, out_a, out_b, delta):
     rows, half = far.shape
+    inside = spot()[2]
     for r in range(0, rows, 128):
         at = pl.ds(r, 128)
-        delta[at, :half], delta[at, half:] = differences(far, near_in, far_in, at)
+        delta[at, :half], delta[at, half:] = differences(inside, far, near_in, far_in, at)
     total = jnp.zeros((8, 2 * half), jnp.float32)
     for r in range(0, rows, 256):
         mixed = dot(weights[r : r + 256, :rows], delta[...])
@@ -170,10 +177,15 @@
     out_b[...] = total[:, half:]
 
 
-def close_kernel(upper, lower, weights, carry, early, out, start=0):
+def close_kernel(upper, lower, weights, carry, early, out, start=0, masked=False):
     rows, half = lower.shape
     upper = upper.at[:, start : start + half]
-    changes = [(upper[r : r + 128, :].astype(jnp.float32) - lower[r : r + 128, :].astype(jnp.float32)) for r in range(0, rows, 128)]
+    changes = []
+    for r in range(0, rows, 128):
+        above = upper[r : r + 128, :].astype(jnp.float32)
+        if masked:
+            above = jnp.where(spot()[2], above, 0.0)
+        changes.append(above - lower[r : r + 128, :].astype(jnp.float32))
     delta = jnp.concatenate(changes, axis=0).astype(jnp.bfloat16)
     total = early[...]
     for r in range(0, rows, 256):
@@ -201,11 +213,11 @@
     half = cells // 2
     odd = lax.rem(s, 2)
     to_mate = [(i, i ^ 1) for i in range(blocks)]
-    ahead = [(i, i - 2) for i in range(2, blocks, 2)] + [(i, i + 2) for i in range(1, blocks - 2, 2)]
+    ahead = [(i, (i + (2 if i % 2 else -2)) % blocks) for i in range(blocks)]
+    inner = [(i, j) for i, j in ahead if abs(i - j) == 2]
     swap = [(0, 1), (1, 0)]
     low_core, near_level = c == 0, 1 - odd
     potentials, odd, c, low_core, near_level = lax.optimization_barrier((potentials, odd, c, low_core, near_level))
-    place = jnp.stack([odd, c]).astype(jnp.int32)
     shape = jax.ShapeDtypeStruct
     bf16, f32 = jnp.bfloat16, jnp.float32
     both = ("space", "elec")
@@ -218,23 +230,23 @@
     near, far = call(
         keep_kernel,
         (piece,) * 2,
-        [SMEM, pl.BlockSpec(memory_space=pl.ANY)],
+        [pl.BlockSpec(memory_space=pl.ANY)],
         "keep",
         scratch=[pltpu.VMEM((rows, layers, half), bf16), pltpu.SemaphoreType.DMA((4,))],
         moved=rows * cells * 4,
         limit=FIRST,
-    )(place, potentials)
+    )(potentials)
     near_in_0 = lax.ppermute(near, both, joint(to_mate, 0))
     far_in_0 = lax.ppermute(far, both, joint(ahead, 0))
-    place_b, near, far, potentials = lax.optimization_barrier((place, near, far, potentials))
+    near, far, potentials = lax.optimization_barrier((near, far, potentials))
     near_give, far_give, parcel, rim = call(
         give_kernel,
         (piece, piece, shape((rows, 2 * half + 2 * LANES), bf16), strip),
-        [SMEM, VMEM],
+        [VMEM],
         "give",
         moved=rows * cells * 8,
         limit=4,
-    )(place_b, potentials)
+    )(potentials)
     parcel = lax.ppermute(parcel, "elec", swap)
 
     order = jnp.where(low_core, elec_order, jnp.concatenate([elec_order[rows:], elec_order[:rows]]))
@@ -245,19 +257,19 @@
     near_give, weights = lax.optimization_barrier((near_give, weights))
     far_give, cross = lax.optimization_barrier((far_give, cross))
     near_in_1 = lax.ppermute(near_give, both, joint(to_mate, 1))
-    far_in_1 = lax.ppermute(far_give, both, joint(ahead, 1))
+    far_in_1 = lax.ppermute(far_give, both, joint(inner, 1))
 
     big = 2 * rows * rows * half * 2
     forms = call(
         plane_kernel,
         shape((2 * layers, half), f32),
-        [SMEM] + [VMEM] * 6,
+        [VMEM] * 6,
         "plane",
         scratch=[pltpu.VMEM((2, 2 * rows, half), bf16)],
         limit=16,
         flops=big * 6,
         moved=rows * cells * 16,
-    )(place, near, far, rim, parcel, weights, cross)
+    )(near, far, rim, parcel, weights, cross)
 
     bulk = 0.15 * salinity * water_content**cementation
     salt_scale = bulk / salinity
@@ -292,16 +304,16 @@
         (early_a, salt_base, water_base, salt_scale, water_scale)
     )
 
-    def close(name, start, *given):
+    def close(name, start, masked, *given):
         return call(
-            functools.partial(close_kernel, start=start), shape((1, half), f32), [VMEM] * 5, name, flops=big, moved=rows * cells * 8, limit=6
+            functools.partial(close_kernel, start=start, masked=masked), shape((1, half), f32), [VMEM] * 5, name, flops=big, moved=rows * cells * 8, limit=6
         )(*given)
 
-    form_a = close("close_a", half, parcel, near_in_1, weights, carry_a, early_a)
+    form_a = close("close_a", half, False, parcel, near_in_1, weights, carry_a, early_a)
     a_x = lax.ppermute(form_a, "elec", swap)
     if HOLD:
         far_in_1, form_a = lax.optimization_barrier((far_in_1, form_a))
-    form_b = close("close_b", 0, far_in_1, near_in_1, weights, carry_b, early_b)
+    form_b = close("close_b", 0, True, far_in_1, near_in_1, weights, carry_b, early_b)
     b_cross = lax.ppermute(form_b, both, joint(to_mate, 1))
     b_same = lax.ppermute(form_b, both, joint(to_mate, 0))
     form_z = spread(form_a, a_x, b_same, b_cross)

time: 36.6 us -> 34.2 us (0.934)
  starting transfers between devices: 13.6 us -> 11.3 us
  Pallas kernels: 10.7 us -> 9.19 us
  waiting for transfers between devices: 7.37 us -> 8.62 us
    ppermute x1, starting transfers between devices: 4.7 us -> 0.49 us  [local(): near_in_1 = lax.ppermute(near_give, both, joint(to_mate, 1))]
    ppermute x1, starting transfers between devices: 1.28 us -> 3.6 us  [local(): far_in_0 = lax.ppermute(far, both, joint(ahead, 0))]
    ppermute x1, waiting for transfers between devices: 4.71 us -> 6.72 us  [local(): near_in_1 = lax.ppermute(near_give, both, joint(to_mate, 1))]
    pallas_call x4, Pallas kernels: 8.12 us -> 7.11 us  [the longest x1 4.59 us: local(): call(plane_kernel, shape((2 * layers, half), f32), [VMEM] * 6, 'plane', s...]
    ppermute x1, starting transfers between devices: 1.52 us -> 0.83 us  [local(): b_same = lax.ppermute(form_b, both, joint(to_mate, 0))]
    ppermute x1, waiting for transfers between devices: 0.88 us -> 0.19 us  [local(): b_cross = lax.ppermute(form_b, both, joint(to_mate, 1))]
    ppermute x1, waiting for transfers between devices: 0.83 us -> 0.23 us  [local(): far_in_1 = lax.ppermute(far_give, both, joint(inner, 1))]
    pallas_call x1, Pallas kernels: 1.01 us -> 0.46 us  [local(): call(give_kernel, (piece, piece, shape((rows, 2 * half + 2 * LANES), bf16...]
  transfers between devices with their start and end apart: 9 -> 9, of which waited for: 4 -> 5; matrix products, arithmetic and copies ran while one was open for 8% -> 9% of each run, Pallas kernels for 23% -> 21%
where the time goes in v6:
time: 34.2 us; the launch traced here: 33.8 us
  starting transfers between devices  11.3 us (33%)
  Pallas kernels  9.19 us (27%)
  waiting for transfers between devices  8.62 us (25%)
  matrix products  2.81 us (8%)
  between operations  0.92 us (3%)
  other arithmetic  0.9 us (3%)
    ppermute x1, waiting for transfers between devices, local(): near_in_1 = lax.ppermute(near_give, both, joint(to_mate, 1))  6.72 us
    pallas_call x1, Pallas kernels, local(): call(plane_kernel, shape((2 * layers, half), f32), [VMEM] * 6, 'plane', s...  4.59 us
    ppermute x1, starting transfers between devices, local(): far_in_0 = lax.ppermute(far, both, joint(ahead, 0))  3.6 us
    ppermute x1, starting transfers between devices, local(): near_in_0 = lax.ppermute(near, both, joint(to_mate, 0))  3.03 us
    dot_general x1, matrix products, dot(): return jnp.dot(left, right, preferred_element_type=jnp.float32)  2.81 us
    ppermute x1, starting transfers between devices, local(): b_cross = lax.ppermute(form_b, both, joint(to_mate, 1))  1.51 us
    pallas_call x1, Pallas kernels, local(): call(keep_kernel, (piece,) * 2, [pl.BlockSpec(memory_space=pl.ANY)], 'kee...  1.47 us
    pallas_call x1, Pallas kernels, local(): call(early_kernel, (shape((rows, half), f32),) * 2 + (shape((8, half), f3...  1.38 us
  transfers between devices with their start and end apart: 9, of which 5 were waited for; matrix products, arithmetic and copies ran while one was open for 9% of the time, Pallas kernels for 21%

profile of v6, /device:TPU:0, one launch (start us, length us, event | category | flops | bytes accessed | tf_op | source)
XLA Modules:
  0.0 33.8 jit_solution(7767502016513571048)
XLA Ops:
  0.6 0.0 copy-start
  0.6 0.0 copy-start.2
  0.7 0.0 copy-start.7
  0.7 0.0 copy-start.3
  0.7 1.5 %keep.1 = (bf16[512,512]{1,0:T(8,128)(2,1)S(1)}, bf16[512,512]{1,0:T(8,128)(2,1)S(1)}) custom-call(bf16[512,2,1024]{2,1,0:T(2,128)(2,1)} %potentials.1), custom_call_target="tpu_custom_call" | custom-call | bytes 2097152 | tf_op jit(solution)/shard_map/keep/pallas_call | solution.py:230
  2.2 3.0 %collective-permute-start = (bf16[512,512]{1,0:T(8,128)(2,1)S(1)}, bf16[512,512]{1,0:T(8,128)(2,1)S(1)}, u32[]{:S(2)}, u32[]{:S(2)}) collective-permute-start(bf16[512,512]{1,0:T(8,128)(2,1)S(1)} %get-tuple-element.43.near), channel_id=1, source_target_pairs={{0,2},{1,3},{2,0},{3,1},{4,6},{5,7},{6,4},{7,5},{8,10},{9,11},{10,... | collective-permute-start | bytes 1572872 | tf_op jit(solution)/shard_map/ppermute | solution.py:239
  5.2 3.6 %collective-permute-start.1 = (bf16[512,512]{1,0:T(8,128)(2,1)S(1)}, bf16[512,512]{1,0:T(8,128)(2,1)S(1)}, u32[]{:S(2)}, u32[]{:S(2)}) collective-permute-start(bf16[512,512]{1,0:T(8,128)(2,1)S(1)} %get-tuple-element.36.far), channel_id=1, source_target_pairs={{0,12},{1,13},{2,6},{3,7},{4,0},{5,1},{6,10},{7,11},{8,4},{9,5},{1... | collective-permute-start | bytes 1572872 | tf_op jit(solution)/shard_map/ppermute | solution.py:240
  8.8 0.0 copy-done
  8.8 0.5 %give.1 = (bf16[512,512]{1,0:T(8,128)(2,1)S(1)}, bf16[512,512]{1,0:T(8,128)(2,1)S(1)}, bf16[512,1280]{1,0:T(8,128)(2,1)S(1)}, bf16[512,256]{1,0:T(8,128)(2,1)S(1)}) custom-call(bf16[512,2,1024]{2,1,0:T(2,128)(2,1)S(1)} %copy-done), custom_call_target="tpu_custom_call" | custom-call | bytes 4194304 | tf_op jit(solution)/shard_map/give/pallas_call | solution.py:242
  9.3 0.1 collective-permute-start.2
  9.3 0.0 copy-done.2
  9.4 0.0 copy-done.7
  9.4 0.0 copy-done.3
  9.4 2.8 %fusion.10.weights = bf16[1024,1024]{1,0:T(8,128)(2,1)S(1)} fusion(s32[1024]{0:T(1024)S(1)} %add_select_fusion.1, f32[1024]{0:T(1024)S(1)} %convert_element_type.23, s32[1024]{0:T(1024)S(1)} %bitcast.39, s32[1024]{0:T(1024)S(1)} %bitcast.40, s32[1024]{0:T(1024)S(1)} %bitcast.41, s32[1024]{0:T(1024)S(1)} %bitcast.38), kind=kOutput, calls=%fused_computation.12 | convolution fusion | flops 2161115136 | bytes 2121728 | tf_op jit(solution)/shard_map/dot_general | solution.py:31
  12.2 0.0 copy-start.1
  12.3 0.0 copy-start.4
  12.3 0.0 copy-start.5
  12.3 0.0 copy-start.6
  12.3 0.2 cross.1
  12.5 1.3 %collective-permute-start.4 = (bf16[512,512]{1,0:T(8,128)(2,1)S(1)}, bf16[512,512]{1,0:T(8,128)(2,1)S(1)}, u32[]{:S(2)}, u32[]{:S(2)}) collective-permute-start(bf16[512,512]{1,0:T(8,128)(2,1)S(1)} %get-tuple-element.53), channel_id=1, source_target_pairs={{2,7},{3,6},{4,1},{5,0},{6,11},{7,10},{8,5},{9,4},{10,15},{11,14},... | collective-permute-start | bytes 1572872 | tf_op jit(solution)/shard_map/ppermute | solution.py:260
  13.8 0.5 %collective-permute-start.5 = (bf16[512,512]{1,0:T(8,128)(2,1)S(1)}, bf16[512,512]{1,0:T(8,128)(2,1)S(1)}, u32[]{:S(2)}, u32[]{:S(2)}) collective-permute-start(bf16[512,512]{1,0:T(8,128)(2,1)S(1)} %get-tuple-element.54), channel_id=1, source_target_pairs={{0,3},{1,2},{2,1},{3,0},{4,7},{5,6},{6,5},{7,4},{8,11},{9,10},{10,... | collective-permute-start | bytes 1572872 | tf_op jit(solution)/shard_map/ppermute | solution.py:259
  14.3 0.0 copy-done.1
  14.3 0.0 copy-done.4
  14.3 0.0 copy-done.5
  14.3 0.0 copy-done.6
  14.3 0.1 bitcast_multiply_fusion
  14.4 0.0 collective-permute-done.2.parcel.upper
  14.4 4.6 %plane.1 = f32[4,512]{1,0:T(4,128)S(1)} custom-call(bf16[512,512]{1,0:T(8,128)(2,1)S(1)} %get-tuple-element.43.near, bf16[512,512]{1,0:T(8,128)(2,1)S(1)} %get-tuple-element.36.far, bf16[512,256]{1,0:T(8,128)(2,1)S(1)} %get-tuple-element.44.rim, bf16[512,1280]{1,0:T(8,128)(2,1)S(1)} %collective-permute-done.2.parcel.upper, ...), custom_call_target="tpu_custom_call" | custom-call | flops 3221225472 | bytes 8388608 | tf_op jit(solution)/shard_map/plane/pallas_call | solution.py:263
  19.0 0.5 %collective-permute-start.3 = (f32[4,512]{1,0:T(4,128)S(1)}, f32[4,512]{1,0:T(4,128)S(1)}, u32[]{:S(2)}, u32[]{:S(2)}) collective-permute-start(f32[4,512]{1,0:T(4,128)S(1)} %plane.1), channel_id=1, source_target_pairs={{0,1},{1,0},{2,3},{3,2},{4,5},{5,4},{6,7},{7,6},{8,9},{9,8},{10,11... | collective-permute-start | bytes 24584 | tf_op jit(solution)/shard_map/ppermute | solution.py:287
  19.5 0.0 collective-permute-done.near_in
  19.5 0.2 collective-permute-done.1.far_in
  19.7 1.4 %early.1 = (f32[512,512]{1,0:T(8,128)S(1)}, f32[512,512]{1,0:T(8,128)S(1)}, f32[8,512]{1,0:T(8,128)S(1)}, f32[8,512]{1,0:T(8,128)S(1)}) custom-call(bf16[512,512]{1,0:T(8,128)(2,1)S(1)} %get-tuple-element.36.far, bf16[512,512]{1,0:T(8,128)(2,1)S(1)} %collective-permute-done.near_in, bf16[512,512]{1,0:T(8,128)(2,1)S(1)} %collective-permute-done.1.far_in, ...), custom_call_target="tpu_custom_call" | custom-call | flops 2147483648 | bytes 8388608 | tf_op jit(solution)/shard_map/early/pallas_call | solution.py:294
  21.1 0.0 collective-permute-done.3
  21.1 0.1 fusion.22
  21.2 6.7 %collective-permute-done.5.lower = bf16[512,512]{1,0:T(8,128)(2,1)S(1)} collective-permute-done((bf16[512,512]{1,0:T(8,128)(2,1)S(1)}, bf16[512,512]{1,0:T(8,128)(2,1)S(1)}, u32[]{:S(2)}, u32[]{:S(2)}) %collective-permute-start.5) | collective-permute-done | bytes 524320 | tf_op jit(solution)/shard_map/ppermute | solution.py:259
  28.0 0.5 %close_a.1 = f32[1,512]{1,0:T(1,128)S(1)} custom-call(bf16[512,1280]{1,0:T(8,128)(2,1)S(1)} %collective-permute-done.2.parcel.upper, bf16[512,512]{1,0:T(8,128)(2,1)S(1)} %collective-permute-done.5.lower, bf16[1024,1024]{1,0:T(8,128)(2,1)S(1)} %fusion.10.weights, f32[512,512]{1,0:T(8,128)S(1)} %get-tuple-element.55.carry, f32[8,512]{1,0:T(8,128)S(1)} %get-tuple-element.56.early), custom_call_target="tpu_custom_call" | custom-call | flops 536870912 | bytes 4194304 | tf_op jit(solution)/shard_map/close_a/pallas_call | solution.py:308
  28.5 0.2 collective-permute-done.4.upper
  28.7 0.5 %close_b.1 = f32[1,512]{1,0:T(1,128)S(1)} custom-call(bf16[512,512]{1,0:T(8,128)(2,1)S(1)} %collective-permute-done.4.upper, bf16[512,512]{1,0:T(8,128)(2,1)S(1)} %collective-permute-done.5.lower, bf16[1024,1024]{1,0:T(8,128)(2,1)S(1)} %fusion.10.weights, f32[512,512]{1,0:T(8,128)S(1)} %get-tuple-element.59.carry, f32[8,512]{1,0:T(8,128)S(1)} %get-tuple-element.60.early), custom_call_target="tpu_custom_call" | custom-call | flops 536870912 | bytes 4194304 | tf_op jit(solution)/shard_map/close_b/pallas_call | solution.py:308
  29.3 0.8 %collective-permute-start.7 = (f32[1,512]{1,0:T(1,128)S(1)}, f32[1,512]{1,0:T(1,128)S(1)}, u32[]{:S(2)}, u32[]{:S(2)}) collective-permute-start(f32[1,512]{1,0:T(1,128)S(1)} %close_b.1), channel_id=1, source_target_pairs={{0,2},{1,3},{2,0},{3,1},{4,6},{5,7},{6,4},{7,5},{8,10},{9,11},{10,... | collective-permute-start | bytes 6152 | tf_op jit(solution)/shard_map/ppermute | solution.py:318
  30.1 1.5 %collective-permute-start.8 = (f32[1,512]{1,0:T(1,128)S(1)}, f32[1,512]{1,0:T(1,128)S(1)}, u32[]{:S(2)}, u32[]{:S(2)}) collective-permute-start(f32[1,512]{1,0:T(1,128)S(1)} %close_b.1), channel_id=1, source_target_pairs={{0,3},{1,2},{2,1},{3,0},{4,7},{5,6},{6,5},{7,4},{8,11},{9,10},{10,... | collective-permute-start | bytes 6152 | tf_op jit(solution)/shard_map/ppermute | solution.py:317
  31.6 0.0 collective-permute-start.6
  31.6 1.3 %collective-permute-done.7 = f32[1,512]{1,0:T(1,128)S(1)} collective-permute-done((f32[1,512]{1,0:T(1,128)S(1)}, f32[1,512]{1,0:T(1,128)S(1)}, u32[]{:S(2)}, u32[]{:S(2)}) %collective-permute-start.7) | collective-permute-done | bytes 2080 | tf_op jit(solution)/shard_map/ppermute | solution.py:318
  32.9 0.2 collective-permute-done.8
  33.1 0.0 collective-permute-done.6
  33.1 0.7 %fusion.14 = (f32[2,1024]{1,0:T(2,128)}, f32[2,1024]{1,0:T(2,128)}) fusion(f32[2,1024]{1,0:T(2,128)S(1)} %get-tuple-element.63, f32[2,1024]{1,0:T(2,128)S(1)} %get-tuple-element.62, pred[2]{0:T(512)(128)(4,1)S(1)} %iota_compare_fusion, f32[1024]{0:T(1024)S(1)} %maximum_select_fusion.5, f32[1024]{0:T(1024)S(1)} %maximum_select_fusion.4, ...), kind=kLoop, calls=%fused_computation.16 | loop fusion | flops 10240 | bytes 57346 | tf_op jit(solution)/shard_map/add | solution.py:320
  (12 shorter events, 0.1 us)
Async XLA Ops:
  0.6 8.2 %copy-start = (bf16[512,2,1024]{2,1,0:T(2,128)(2,1)S(1)}, bf16[512,2,1024]{2,1,0:T(2,128)(2,1)}, u32[]{:S(2)}) copy-start(bf16[512,2,1024]{2,1,0:T(2,128)(2,1)} %potentials.1) | copy-start | bytes 6291460
  0.6 8.7 %copy-start.2 = (s32[1024]{0:T(1024)S(1)}, s32[1024]{0:T(1024)}, u32[]{:S(2)}) copy-start(s32[1024]{0:T(1024)} %param.9) | copy-start | bytes 12292
  0.7 8.7 %copy-start.7 = (bf16[1024]{0:T(1024)(128)(2,1)S(1)}, bf16[1024]{0:T(1024)(128)(2,1)}, u32[]{:S(2)}) copy-start(bf16[1024]{0:T(1024)(128)(2,1)} %param.11) | copy-start | bytes 6148
  0.7 8.7 %copy-start.3 = (s32[1024,4]{0,1:T(4,128)S(1)}, s32[1024,4]{0,1:T(4,128)}, u32[]{:S(2)}) copy-start(s32[1024,4]{0,1:T(4,128)} %param.10) | copy-start | bytes 49156
  2.2 17.4 %collective-permute-start = (bf16[512,512]{1,0:T(8,128)(2,1)S(1)}, bf16[512,512]{1,0:T(8,128)(2,1)S(1)}, u32[]{:S(2)}, u32[]{:S(2)}) collective-permute-start(bf16[512,512]{1,0:T(8,128)(2,1)S(1)} %get-tuple-element.43.near), channel_id=1, source_target_pairs={{0,2},{1,3},{2,0},{3,1},{4,6},{5,7},{6,4},{7,5},{8,10},{9,11},{10,... | collective-permute-start | bytes 1572872 | tf_op jit(solution)/shard_map/ppermute | solution.py:239
  5.2 14.5 %collective-permute-start.1 = (bf16[512,512]{1,0:T(8,128)(2,1)S(1)}, bf16[512,512]{1,0:T(8,128)(2,1)S(1)}, u32[]{:S(2)}, u32[]{:S(2)}) collective-permute-start(bf16[512,512]{1,0:T(8,128)(2,1)S(1)} %get-tuple-element.36.far), channel_id=1, source_target_pairs={{0,12},{1,13},{2,6},{3,7},{4,0},{5,1},{6,10},{7,11},{8,4},{9,5},{1... | collective-permute-start | bytes 1572872 | tf_op jit(solution)/shard_map/ppermute | solution.py:240
  9.3 5.2 %collective-permute-start.2 = (bf16[512,1280]{1,0:T(8,128)(2,1)S(1)}, bf16[512,1280]{1,0:T(8,128)(2,1)S(1)}, u32[]{:S(2)}, u32[]{:S(2)}) collective-permute-start(bf16[512,1280]{1,0:T(8,128)(2,1)S(1)} %get-tuple-element.45), channel_id=1, source_target_pairs={{0,1},{1,0},{2,3},{3,2},{4,5},{5,4},{6,7},{7,6},{8,9},{9,8},{10,11... | collective-permute-start | bytes 3932168 | tf_op jit(solution)/shard_map/ppermute | solution.py:250
  12.2 2.1 %copy-start.1 = (f32[3,2,1024]{2,1,0:T(2,128)S(1)}, f32[3,2,1024]{2,1,0:T(2,128)}, u32[]{:S(2)}) copy-start(f32[3,2,1024]{2,1,0:T(2,128)} %param.15) | copy-start | bytes 73732
  12.3 2.1 %copy-start.4 = (f32[2,1024]{1,0:T(2,128)S(1)}, f32[2,1024]{1,0:T(2,128)}, u32[]{:S(2)}) copy-start(f32[2,1024]{1,0:T(2,128)} %param.13) | copy-start | bytes 24580
  12.3 2.1 %copy-start.5 = (f32[2,1024]{1,0:T(2,128)S(1)}, f32[2,1024]{1,0:T(2,128)}, u32[]{:S(2)}) copy-start(f32[2,1024]{1,0:T(2,128)} %param.14) | copy-start | bytes 24580
  12.3 2.1 %copy-start.6 = (f32[2,1024]{1,0:T(2,128)S(1)}, f32[2,1024]{1,0:T(2,128)}, u32[]{:S(2)}) copy-start(f32[2,1024]{1,0:T(2,128)} %param.12) | copy-start | bytes 24580
  12.5 16.2 %collective-permute-start.4 = (bf16[512,512]{1,0:T(8,128)(2,1)S(1)}, bf16[512,512]{1,0:T(8,128)(2,1)S(1)}, u32[]{:S(2)}, u32[]{:S(2)}) collective-permute-start(bf16[512,512]{1,0:T(8,128)(2,1)S(1)} %get-tuple-element.53), channel_id=1, source_target_pairs={{2,7},{3,6},{4,1},{5,0},{6,11},{7,10},{8,5},{9,4},{10,15},{11,14},... | collective-permute-start | bytes 1572872 | tf_op jit(solution)/shard_map/ppermute | solution.py:260
  13.8 14.1 %collective-permute-start.5 = (bf16[512,512]{1,0:T(8,128)(2,1)S(1)}, bf16[512,512]{1,0:T(8,128)(2,1)S(1)}, u32[]{:S(2)}, u32[]{:S(2)}) collective-permute-start(bf16[512,512]{1,0:T(8,128)(2,1)S(1)} %get-tuple-element.54), channel_id=1, source_target_pairs={{0,3},{1,2},{2,1},{3,0},{4,7},{5,6},{6,5},{7,4},{8,11},{9,10},{10,... | collective-permute-start | bytes 1572872 | tf_op jit(solution)/shard_map/ppermute | solution.py:259
  19.0 2.1 %collective-permute-start.3 = (f32[4,512]{1,0:T(4,128)S(1)}, f32[4,512]{1,0:T(4,128)S(1)}, u32[]{:S(2)}, u32[]{:S(2)}) collective-permute-start(f32[4,512]{1,0:T(4,128)S(1)} %plane.1), channel_id=1, source_target_pairs={{0,1},{1,0},{2,3},{3,2},{4,5},{5,4},{6,7},{7,6},{8,9},{9,8},{10,11... | collective-permute-start | bytes 24584 | tf_op jit(solution)/shard_map/ppermute | solution.py:287
  29.3 3.7 %collective-permute-start.7 = (f32[1,512]{1,0:T(1,128)S(1)}, f32[1,512]{1,0:T(1,128)S(1)}, u32[]{:S(2)}, u32[]{:S(2)}) collective-permute-start(f32[1,512]{1,0:T(1,128)S(1)} %close_b.1), channel_id=1, source_target_pairs={{0,2},{1,3},{2,0},{3,1},{4,6},{5,7},{6,4},{7,5},{8,10},{9,11},{10,... | collective-permute-start | bytes 6152 | tf_op jit(solution)/shard_map/ppermute | solution.py:318
  30.1 3.0 %collective-permute-start.8 = (f32[1,512]{1,0:T(1,128)S(1)}, f32[1,512]{1,0:T(1,128)S(1)}, u32[]{:S(2)}, u32[]{:S(2)}) collective-permute-start(f32[1,512]{1,0:T(1,128)S(1)} %close_b.1), channel_id=1, source_target_pairs={{0,3},{1,2},{2,1},{3,0},{4,7},{5,6},{6,5},{7,4},{8,11},{9,10},{10,... | collective-permute-start | bytes 6152 | tf_op jit(solution)/shard_map/ppermute | solution.py:317
  31.6 1.5 %collective-permute-start.6 = (f32[1,512]{1,0:T(1,128)S(1)}, f32[1,512]{1,0:T(1,128)S(1)}, u32[]{:S(2)}, u32[]{:S(2)}) collective-permute-start(f32[1,512]{1,0:T(1,128)S(1)} %close_a.1), channel_id=1, source_target_pairs={{0,1},{1,0},{2,3},{3,2},{4,5},{5,4},{6,7},{7,6},{8,9},{9,8},{10,11... | collective-permute-start | bytes 6152 | tf_op jit(solution)/shard_map/ppermute | solution.py:313

commit v7 on v6

--- a/solution.py
+++ b/solution.py
@@ -10,8 +10,6 @@
 LANES = 128
 VMEM = pl.BlockSpec(memory_space=pltpu.VMEM)
 MIB = 2**20
-FIRST = 51
-HOLD = True
 
 
 def call(kernel, outs, specs, name, scratch=(), limit=8, flops=0, moved=0):
@@ -55,8 +53,13 @@
         copies[-1].start()
     for i, copy in enumerate(copies):
         copy.wait()
-        for r in range(i * size, (i + 1) * size, 32):
-            near[r : r + 32, :], far[r : r + 32, :] = levels(raw[r : r + 32], odd)
+        for k in range(2):
+
+            @pl.when(odd == k)
+            def _():
+                for r in range(i * size, (i + 1) * size, 64):
+                    layers = jnp.swapaxes(raw[r : r + 64], 0, 1)
+                    near[r : r + 64, :], far[r : r + 64, :] = layers[1 - k], layers[k]
 
 
 def give_kernel(potentials, near, far, parcel, rim):
@@ -179,19 +182,21 @@
 
 def close_kernel(upper, lower, weights, carry, early, out, start=0, masked=False):
     rows, half = lower.shape
-    upper = upper.at[:, start : start + half]
-    changes = []
-    for r in range(0, rows, 128):
-        above = upper[r : r + 128, :].astype(jnp.float32)
-        if masked:
-            above = jnp.where(spot()[2], above, 0.0)
-        changes.append(above - lower[r : r + 128, :].astype(jnp.float32))
-    delta = jnp.concatenate(changes, axis=0).astype(jnp.bfloat16)
-    total = early[...]
-    for r in range(0, rows, 256):
-        mixed = carry[r : r + 256, :] + dot(weights[rows + r : rows + r + 256, rows:], delta)
-        total = total + jnp.sum((delta[r : r + 256, :].astype(jnp.float32) * mixed).reshape(-1, 8, half), axis=0)
-    out[...] = 0.25 * jnp.sum(total, axis=0, keepdims=True)
+    inside = spot()[2]
+    wide = half // 2
+    for c in range(0, half, wide):
+        changes = []
+        for r in range(0, rows, 128):
+            above = upper[r : r + 128, start + c : start + c + wide].astype(jnp.float32)
+            if masked:
+                above = jnp.where(inside, above, 0.0)
+            changes.append((above - lower[r : r + 128, c : c + wide].astype(jnp.float32)).astype(jnp.bfloat16))
+        delta = jnp.concatenate(changes, axis=0)
+        total = early[:, c : c + wide]
+        for r in range(0, rows, 256):
+            mixed = carry[r : r + 256, c : c + wide] + dot(weights[rows + r : rows + r + 256, rows:], delta)
+            total = total + jnp.sum((delta[r : r + 256, :].astype(jnp.float32) * mixed).reshape(-1, 8, wide), axis=0)
+        out[:, c : c + wide] = 0.25 * jnp.sum(total, axis=0, keepdims=True)
 
 
 def assemble(quadripoles, weighted_misfit, order):
@@ -234,7 +239,7 @@
         "keep",
         scratch=[pltpu.VMEM((rows, layers, half), bf16), pltpu.SemaphoreType.DMA((4,))],
         moved=rows * cells * 4,
-        limit=FIRST,
+        limit=51,
     )(potentials)
     near_in_0 = lax.ppermute(near, both, joint(to_mate, 0))
     far_in_0 = lax.ppermute(far, both, joint(ahead, 0))
@@ -250,8 +255,7 @@
     parcel = lax.ppermute(parcel, "elec", swap)
 
     order = jnp.where(low_core, elec_order, jnp.concatenate([elec_order[rows:], elec_order[:rows]]))
-    if True:
-        quadripoles, near_give = lax.optimization_barrier((quadripoles, near_give))
+    quadripoles, near_give = lax.optimization_barrier((quadripoles, near_give))
     weights = assemble(quadripoles, weighted_misfit, order)
     cross = call(cross_kernel, shape((rows, rows), bf16), [VMEM], "cross", moved=4 * rows * rows * 2)(weights)
     near_give, weights = lax.optimization_barrier((near_give, weights))
@@ -311,8 +315,7 @@
 
     form_a = close("close_a", half, False, parcel, near_in_1, weights, carry_a, early_a)
     a_x = lax.ppermute(form_a, "elec", swap)
-    if HOLD:
-        far_in_1, form_a = lax.optimization_barrier((far_in_1, form_a))
+    far_in_1, form_a = lax.optimization_barrier((far_in_1, form_a))
     form_b = close("close_b", 0, True, far_in_1, near_in_1, weights, carry_b, early_b)
     b_cross = lax.ppermute(form_b, both, joint(to_mate, 1))
     b_same = lax.ppermute(form_b, both, joint(to_mate, 0))

time: 34.2 us -> 34.2 us (level)
  no operation moved by 1% of the time
where the time goes in v7:
time: 34.2 us; the launch traced here: 33.8 us
  starting transfers between devices  11.3 us (33%)
  Pallas kernels  9.16 us (27%)
  waiting for transfers between devices  8.59 us (25%)
  matrix products  2.8 us (8%)
  between operations  0.91 us (3%)
  other arithmetic  0.9 us (3%)
    ppermute x1, waiting for transfers between devices, local(): near_in_1 = lax.ppermute(near_give, both, joint(to_mate, 1))  6.72 us
    pallas_call x1, Pallas kernels, local(): call(plane_kernel, shape((2 * layers, half), f32), [VMEM] * 6, 'plane', s...  4.6 us
    ppermute x1, starting transfers between devices, local(): far_in_0 = lax.ppermute(far, both, joint(ahead, 0))  3.6 us
    ppermute x1, starting transfers between devices, local(): near_in_0 = lax.ppermute(near, both, joint(to_mate, 0))  3.04 us
    dot_general x1, matrix products, dot(): return jnp.dot(left, right, preferred_element_type=jnp.float32)  2.8 us
    ppermute x1, starting transfers between devices, local(): b_cross = lax.ppermute(form_b, both, joint(to_mate, 1))  1.52 us
    pallas_call x1, Pallas kernels, local(): call(keep_kernel, (piece,) * 2, [pl.BlockSpec(memory_space=pl.ANY)], 'kee...  1.44 us
    pallas_call x1, Pallas kernels, local(): call(early_kernel, (shape((rows, half), f32),) * 2 + (shape((8, half), f3...  1.39 us
  transfers between devices with their start and end apart: 9, of which 5 were waited for; matrix products, arithmetic and copies ran while one was open for 9% of the time, Pallas kernels for 21%

profile of v7, /device:TPU:0, one launch (start us, length us, event | category | flops | bytes accessed | tf_op | source)
XLA Modules:
  0.0 33.8 jit_solution(9978182506512578441)
XLA Ops:
  0.6 0.0 copy-start
  0.6 0.0 copy-start.2
  0.7 0.0 copy-start.7
  0.7 0.0 copy-start.3
  0.7 1.4 %keep.1 = (bf16[512,512]{1,0:T(8,128)(2,1)S(1)}, bf16[512,512]{1,0:T(8,128)(2,1)S(1)}) custom-call(bf16[512,2,1024]{2,1,0:T(2,128)(2,1)} %potentials.1), custom_call_target="tpu_custom_call" | custom-call | bytes 2097152 | tf_op jit(solution)/shard_map/keep/pallas_call | solution.py:235
  2.1 3.0 %collective-permute-start = (bf16[512,512]{1,0:T(8,128)(2,1)S(1)}, bf16[512,512]{1,0:T(8,128)(2,1)S(1)}, u32[]{:S(2)}, u32[]{:S(2)}) collective-permute-start(bf16[512,512]{1,0:T(8,128)(2,1)S(1)} %get-tuple-element.43.near), channel_id=1, source_target_pairs={{0,2},{1,3},{2,0},{3,1},{4,6},{5,7},{6,4},{7,5},{8,10},{9,11},{10,... | collective-permute-start | bytes 1572872 | tf_op jit(solution)/shard_map/ppermute | solution.py:244
  5.2 3.6 %collective-permute-start.1 = (bf16[512,512]{1,0:T(8,128)(2,1)S(1)}, bf16[512,512]{1,0:T(8,128)(2,1)S(1)}, u32[]{:S(2)}, u32[]{:S(2)}) collective-permute-start(bf16[512,512]{1,0:T(8,128)(2,1)S(1)} %get-tuple-element.36.far), channel_id=1, source_target_pairs={{0,12},{1,13},{2,6},{3,7},{4,0},{5,1},{6,10},{7,11},{8,4},{9,5},{1... | collective-permute-start | bytes 1572872 | tf_op jit(solution)/shard_map/ppermute | solution.py:245
  8.8 0.0 copy-done
  8.8 0.5 %give.1 = (bf16[512,512]{1,0:T(8,128)(2,1)S(1)}, bf16[512,512]{1,0:T(8,128)(2,1)S(1)}, bf16[512,1280]{1,0:T(8,128)(2,1)S(1)}, bf16[512,256]{1,0:T(8,128)(2,1)S(1)}) custom-call(bf16[512,2,1024]{2,1,0:T(2,128)(2,1)S(1)} %copy-done), custom_call_target="tpu_custom_call" | custom-call | bytes 4194304 | tf_op jit(solution)/shard_map/give/pallas_call | solution.py:247
  9.2 0.1 collective-permute-start.2
  9.3 0.0 copy-done.2
  9.3 0.0 copy-done.7
  9.4 0.0 copy-done.3
  9.4 2.8 %fusion.10.weights = bf16[1024,1024]{1,0:T(8,128)(2,1)S(1)} fusion(s32[1024]{0:T(1024)S(1)} %add_select_fusion.1, f32[1024]{0:T(1024)S(1)} %convert_element_type.23, s32[1024]{0:T(1024)S(1)} %bitcast.39, s32[1024]{0:T(1024)S(1)} %bitcast.40, s32[1024]{0:T(1024)S(1)} %bitcast.41, s32[1024]{0:T(1024)S(1)} %bitcast.38), kind=kOutput, calls=%fused_computation.12 | convolution fusion | flops 2161115136 | bytes 2121728 | tf_op jit(solution)/shard_map/dot_general | solution.py:29
  12.2 0.0 copy-start.1
  12.2 0.0 copy-start.4
  12.3 0.0 copy-start.5
  12.3 0.0 copy-start.6
  12.3 0.2 cross.1
  12.5 1.3 %collective-permute-start.4 = (bf16[512,512]{1,0:T(8,128)(2,1)S(1)}, bf16[512,512]{1,0:T(8,128)(2,1)S(1)}, u32[]{:S(2)}, u32[]{:S(2)}) collective-permute-start(bf16[512,512]{1,0:T(8,128)(2,1)S(1)} %get-tuple-element.53), channel_id=1, source_target_pairs={{2,7},{3,6},{4,1},{5,0},{6,11},{7,10},{8,5},{9,4},{10,15},{11,14},... | collective-permute-start | bytes 1572872 | tf_op jit(solution)/shard_map/ppermute | solution.py:264
  13.8 0.5 %collective-permute-start.5 = (bf16[512,512]{1,0:T(8,128)(2,1)S(1)}, bf16[512,512]{1,0:T(8,128)(2,1)S(1)}, u32[]{:S(2)}, u32[]{:S(2)}) collective-permute-start(bf16[512,512]{1,0:T(8,128)(2,1)S(1)} %get-tuple-element.54), channel_id=1, source_target_pairs={{0,3},{1,2},{2,1},{3,0},{4,7},{5,6},{6,5},{7,4},{8,11},{9,10},{10,... | collective-permute-start | bytes 1572872 | tf_op jit(solution)/shard_map/ppermute | solution.py:263
  14.3 0.0 copy-done.1
  14.3 0.0 copy-done.4
  14.3 0.0 copy-done.5
  14.3 0.0 copy-done.6
  14.3 0.1 bitcast_multiply_fusion
  14.4 0.0 collective-permute-done.2.parcel.upper
  14.4 4.6 %plane.1 = f32[4,512]{1,0:T(4,128)S(1)} custom-call(bf16[512,512]{1,0:T(8,128)(2,1)S(1)} %get-tuple-element.43.near, bf16[512,512]{1,0:T(8,128)(2,1)S(1)} %get-tuple-element.36.far, bf16[512,256]{1,0:T(8,128)(2,1)S(1)} %get-tuple-element.44.rim, bf16[512,1280]{1,0:T(8,128)(2,1)S(1)} %collective-permute-done.2.parcel.upper, ...), custom_call_target="tpu_custom_call" | custom-call | flops 3221225472 | bytes 8388608 | tf_op jit(solution)/shard_map/plane/pallas_call | solution.py:267
  19.0 0.5 %collective-permute-start.3 = (f32[4,512]{1,0:T(4,128)S(1)}, f32[4,512]{1,0:T(4,128)S(1)}, u32[]{:S(2)}, u32[]{:S(2)}) collective-permute-start(f32[4,512]{1,0:T(4,128)S(1)} %plane.1), channel_id=1, source_target_pairs={{0,1},{1,0},{2,3},{3,2},{4,5},{5,4},{6,7},{7,6},{8,9},{9,8},{10,11... | collective-permute-start | bytes 24584 | tf_op jit(solution)/shard_map/ppermute | solution.py:291
  19.5 0.0 collective-permute-done.near_in
  19.5 0.2 collective-permute-done.1.far_in
  19.7 1.4 %early.1 = (f32[512,512]{1,0:T(8,128)S(1)}, f32[512,512]{1,0:T(8,128)S(1)}, f32[8,512]{1,0:T(8,128)S(1)}, f32[8,512]{1,0:T(8,128)S(1)}) custom-call(bf16[512,512]{1,0:T(8,128)(2,1)S(1)} %get-tuple-element.36.far, bf16[512,512]{1,0:T(8,128)(2,1)S(1)} %collective-permute-done.near_in, bf16[512,512]{1,0:T(8,128)(2,1)S(1)} %collective-permute-done.1.far_in, ...), custom_call_target="tpu_custom_call" | custom-call | flops 2147483648 | bytes 8388608 | tf_op jit(solution)/shard_map/early/pallas_call | solution.py:298
  21.1 0.0 collective-permute-done.3
  21.1 0.1 fusion.22
  21.2 6.7 %collective-permute-done.5.lower = bf16[512,512]{1,0:T(8,128)(2,1)S(1)} collective-permute-done((bf16[512,512]{1,0:T(8,128)(2,1)S(1)}, bf16[512,512]{1,0:T(8,128)(2,1)S(1)}, u32[]{:S(2)}, u32[]{:S(2)}) %collective-permute-start.5) | collective-permute-done | bytes 524320 | tf_op jit(solution)/shard_map/ppermute | solution.py:263
  27.9 0.5 %close_a.1 = f32[1,512]{1,0:T(1,128)S(1)} custom-call(bf16[512,1280]{1,0:T(8,128)(2,1)S(1)} %collective-permute-done.2.parcel.upper, bf16[512,512]{1,0:T(8,128)(2,1)S(1)} %collective-permute-done.5.lower, bf16[1024,1024]{1,0:T(8,128)(2,1)S(1)} %fusion.10.weights, f32[512,512]{1,0:T(8,128)S(1)} %get-tuple-element.55.carry, f32[8,512]{1,0:T(8,128)S(1)} %get-tuple-element.56.early), custom_call_target="tpu_custom_call" | custom-call | flops 536870912 | bytes 4194304 | tf_op jit(solution)/shard_map/close_a/pallas_call | solution.py:312
  28.5 0.2 collective-permute-done.4.upper
  28.7 0.5 %close_b.1 = f32[1,512]{1,0:T(1,128)S(1)} custom-call(bf16[512,512]{1,0:T(8,128)(2,1)S(1)} %collective-permute-done.4.upper, bf16[512,512]{1,0:T(8,128)(2,1)S(1)} %collective-permute-done.5.lower, bf16[1024,1024]{1,0:T(8,128)(2,1)S(1)} %fusion.10.weights, f32[512,512]{1,0:T(8,128)S(1)} %get-tuple-element.59.carry, f32[8,512]{1,0:T(8,128)S(1)} %get-tuple-element.60.early), custom_call_target="tpu_custom_call" | custom-call | flops 536870912 | bytes 4194304 | tf_op jit(solution)/shard_map/close_b/pallas_call | solution.py:312
  29.2 0.8 %collective-permute-start.7 = (f32[1,512]{1,0:T(1,128)S(1)}, f32[1,512]{1,0:T(1,128)S(1)}, u32[]{:S(2)}, u32[]{:S(2)}) collective-permute-start(f32[1,512]{1,0:T(1,128)S(1)} %close_b.1), channel_id=1, source_target_pairs={{0,2},{1,3},{2,0},{3,1},{4,6},{5,7},{6,4},{7,5},{8,10},{9,11},{10,... | collective-permute-start | bytes 6152 | tf_op jit(solution)/shard_map/ppermute | solution.py:321
  30.0 1.5 %collective-permute-start.8 = (f32[1,512]{1,0:T(1,128)S(1)}, f32[1,512]{1,0:T(1,128)S(1)}, u32[]{:S(2)}, u32[]{:S(2)}) collective-permute-start(f32[1,512]{1,0:T(1,128)S(1)} %close_b.1), channel_id=1, source_target_pairs={{0,3},{1,2},{2,1},{3,0},{4,7},{5,6},{6,5},{7,4},{8,11},{9,10},{10,... | collective-permute-start | bytes 6152 | tf_op jit(solution)/shard_map/ppermute | solution.py:320
  31.6 0.0 collective-permute-start.6
  31.6 1.3 %collective-permute-done.7 = f32[1,512]{1,0:T(1,128)S(1)} collective-permute-done((f32[1,512]{1,0:T(1,128)S(1)}, f32[1,512]{1,0:T(1,128)S(1)}, u32[]{:S(2)}, u32[]{:S(2)}) %collective-permute-start.7) | collective-permute-done | bytes 2080 | tf_op jit(solution)/shard_map/ppermute | solution.py:321
  32.9 0.2 collective-permute-done.8
  33.1 0.0 collective-permute-done.6
  33.1 0.7 %fusion.14 = (f32[2,1024]{1,0:T(2,128)}, f32[2,1024]{1,0:T(2,128)}) fusion(f32[2,1024]{1,0:T(2,128)S(1)} %get-tuple-element.63, f32[2,1024]{1,0:T(2,128)S(1)} %get-tuple-element.62, pred[2]{0:T(512)(128)(4,1)S(1)} %iota_compare_fusion, f32[1024]{0:T(1024)S(1)} %maximum_select_fusion.5, f32[1024]{0:T(1024)S(1)} %maximum_select_fusion.4, ...), kind=kLoop, calls=%fused_computation.16 | loop fusion | flops 10240 | bytes 57346 | tf_op jit(solution)/shard_map/add | solution.py:323
  (12 shorter events, 0.1 us)
Async XLA Ops:
  0.6 8.1 %copy-start = (bf16[512,2,1024]{2,1,0:T(2,128)(2,1)S(1)}, bf16[512,2,1024]{2,1,0:T(2,128)(2,1)}, u32[]{:S(2)}) copy-start(bf16[512,2,1024]{2,1,0:T(2,128)(2,1)} %potentials.1) | copy-start | bytes 6291460
  0.6 8.7 %copy-start.2 = (s32[1024]{0:T(1024)S(1)}, s32[1024]{0:T(1024)}, u32[]{:S(2)}) copy-start(s32[1024]{0:T(1024)} %param.9) | copy-start | bytes 12292
  0.7 8.7 %copy-start.7 = (bf16[1024]{0:T(1024)(128)(2,1)S(1)}, bf16[1024]{0:T(1024)(128)(2,1)}, u32[]{:S(2)}) copy-start(bf16[1024]{0:T(1024)(128)(2,1)} %param.11) | copy-start | bytes 6148
  0.7 8.7 %copy-start.3 = (s32[1024,4]{0,1:T(4,128)S(1)}, s32[1024,4]{0,1:T(4,128)}, u32[]{:S(2)}) copy-start(s32[1024,4]{0,1:T(4,128)} %param.10) | copy-start | bytes 49156
  2.1 17.4 %collective-permute-start = (bf16[512,512]{1,0:T(8,128)(2,1)S(1)}, bf16[512,512]{1,0:T(8,128)(2,1)S(1)}, u32[]{:S(2)}, u32[]{:S(2)}) collective-permute-start(bf16[512,512]{1,0:T(8,128)(2,1)S(1)} %get-tuple-element.43.near), channel_id=1, source_target_pairs={{0,2},{1,3},{2,0},{3,1},{4,6},{5,7},{6,4},{7,5},{8,10},{9,11},{10,... | collective-permute-start | bytes 1572872 | tf_op jit(solution)/shard_map/ppermute | solution.py:244
  5.2 14.5 %collective-permute-start.1 = (bf16[512,512]{1,0:T(8,128)(2,1)S(1)}, bf16[512,512]{1,0:T(8,128)(2,1)S(1)}, u32[]{:S(2)}, u32[]{:S(2)}) collective-permute-start(bf16[512,512]{1,0:T(8,128)(2,1)S(1)} %get-tuple-element.36.far), channel_id=1, source_target_pairs={{0,12},{1,13},{2,6},{3,7},{4,0},{5,1},{6,10},{7,11},{8,4},{9,5},{1... | collective-permute-start | bytes 1572872 | tf_op jit(solution)/shard_map/ppermute | solution.py:245
  9.2 5.2 %collective-permute-start.2 = (bf16[512,1280]{1,0:T(8,128)(2,1)S(1)}, bf16[512,1280]{1,0:T(8,128)(2,1)S(1)}, u32[]{:S(2)}, u32[]{:S(2)}) collective-permute-start(bf16[512,1280]{1,0:T(8,128)(2,1)S(1)} %get-tuple-element.45), channel_id=1, source_target_pairs={{0,1},{1,0},{2,3},{3,2},{4,5},{5,4},{6,7},{7,6},{8,9},{9,8},{10,11... | collective-permute-start | bytes 3932168 | tf_op jit(solution)/shard_map/ppermute | solution.py:255
  12.2 2.1 %copy-start.1 = (f32[3,2,1024]{2,1,0:T(2,128)S(1)}, f32[3,2,1024]{2,1,0:T(2,128)}, u32[]{:S(2)}) copy-start(f32[3,2,1024]{2,1,0:T(2,128)} %param.15) | copy-start | bytes 73732
  12.2 2.1 %copy-start.4 = (f32[2,1024]{1,0:T(2,128)S(1)}, f32[2,1024]{1,0:T(2,128)}, u32[]{:S(2)}) copy-start(f32[2,1024]{1,0:T(2,128)} %param.13) | copy-start | bytes 24580
  12.3 2.0 %copy-start.5 = (f32[2,1024]{1,0:T(2,128)S(1)}, f32[2,1024]{1,0:T(2,128)}, u32[]{:S(2)}) copy-start(f32[2,1024]{1,0:T(2,128)} %param.14) | copy-start | bytes 24580
  12.3 2.0 %copy-start.6 = (f32[2,1024]{1,0:T(2,128)S(1)}, f32[2,1024]{1,0:T(2,128)}, u32[]{:S(2)}) copy-start(f32[2,1024]{1,0:T(2,128)} %param.12) | copy-start | bytes 24580
  12.5 16.2 %collective-permute-start.4 = (bf16[512,512]{1,0:T(8,128)(2,1)S(1)}, bf16[512,512]{1,0:T(8,128)(2,1)S(1)}, u32[]{:S(2)}, u32[]{:S(2)}) collective-permute-start(bf16[512,512]{1,0:T(8,128)(2,1)S(1)} %get-tuple-element.53), channel_id=1, source_target_pairs={{2,7},{3,6},{4,1},{5,0},{6,11},{7,10},{8,5},{9,4},{10,15},{11,14},... | collective-permute-start | bytes 1572872 | tf_op jit(solution)/shard_map/ppermute | solution.py:264
  13.8 14.1 %collective-permute-start.5 = (bf16[512,512]{1,0:T(8,128)(2,1)S(1)}, bf16[512,512]{1,0:T(8,128)(2,1)S(1)}, u32[]{:S(2)}, u32[]{:S(2)}) collective-permute-start(bf16[512,512]{1,0:T(8,128)(2,1)S(1)} %get-tuple-element.54), channel_id=1, source_target_pairs={{0,3},{1,2},{2,1},{3,0},{4,7},{5,6},{6,5},{7,4},{8,11},{9,10},{10,... | collective-permute-start | bytes 1572872 | tf_op jit(solution)/shard_map/ppermute | solution.py:263
  19.0 2.1 %collective-permute-start.3 = (f32[4,512]{1,0:T(4,128)S(1)}, f32[4,512]{1,0:T(4,128)S(1)}, u32[]{:S(2)}, u32[]{:S(2)}) collective-permute-start(f32[4,512]{1,0:T(4,128)S(1)} %plane.1), channel_id=1, source_target_pairs={{0,1},{1,0},{2,3},{3,2},{4,5},{5,4},{6,7},{7,6},{8,9},{9,8},{10,11... | collective-permute-start | bytes 24584 | tf_op jit(solution)/shard_map/ppermute | solution.py:291
  29.2 3.7 %collective-permute-start.7 = (f32[1,512]{1,0:T(1,128)S(1)}, f32[1,512]{1,0:T(1,128)S(1)}, u32[]{:S(2)}, u32[]{:S(2)}) collective-permute-start(f32[1,512]{1,0:T(1,128)S(1)} %close_b.1), channel_id=1, source_target_pairs={{0,2},{1,3},{2,0},{3,1},{4,6},{5,7},{6,4},{7,5},{8,10},{9,11},{10,... | collective-permute-start | bytes 6152 | tf_op jit(solution)/shard_map/ppermute | solution.py:321
  30.0 3.0 %collective-permute-start.8 = (f32[1,512]{1,0:T(1,128)S(1)}, f32[1,512]{1,0:T(1,128)S(1)}, u32[]{:S(2)}, u32[]{:S(2)}) collective-permute-start(f32[1,512]{1,0:T(1,128)S(1)} %close_b.1), channel_id=1, source_target_pairs={{0,3},{1,2},{2,1},{3,0},{4,7},{5,6},{6,5},{7,4},{8,11},{9,10},{10,... | collective-permute-start | bytes 6152 | tf_op jit(solution)/shard_map/ppermute | solution.py:320
  31.6 1.5 %collective-permute-start.6 = (f32[1,512]{1,0:T(1,128)S(1)}, f32[1,512]{1,0:T(1,128)S(1)}, u32[]{:S(2)}, u32[]{:S(2)}) collective-permute-start(f32[1,512]{1,0:T(1,128)S(1)} %close_a.1), channel_id=1, source_target_pairs={{0,1},{1,0},{2,3},{3,2},{4,5},{5,4},{6,7},{7,6},{8,9},{9,8},{10,11... | collective-permute-start | bytes 6152 | tf_op jit(solution)/shard_map/ppermute | solution.py:317

commit v8 on v7

--- a/solution.py
+++ b/solution.py
@@ -192,11 +192,24 @@
                 above = jnp.where(inside, above, 0.0)
             changes.append((above - lower[r : r + 128, c : c + wide].astype(jnp.float32)).astype(jnp.bfloat16))
         delta = jnp.concatenate(changes, axis=0)
-        total = early[:, c : c + wide]
-        for r in range(0, rows, 256):
-            mixed = carry[r : r + 256, c : c + wide] + dot(weights[rows + r : rows + r + 256, rows:], delta)
-            total = total + jnp.sum((delta[r : r + 256, :].astype(jnp.float32) * mixed).reshape(-1, 8, wide), axis=0)
+        mixed = carry[:, c : c + wide] + dot(weights[rows:, rows:], delta)
+        total = early[:, c : c + wide] + jnp.sum((delta.astype(jnp.float32) * mixed).reshape(-1, 8, wide), axis=0)
         out[:, c : c + wide] = 0.25 * jnp.sum(total, axis=0, keepdims=True)
+
+
+def finish_kernel(b, b_x, a_x, a, salt_scale, salt_base, water_scale, water_base, salt, water):
+    odd, core, _ = spot()
+    half = a.shape[1]
+    for k in range(2):
+        for n in range(2):
+
+            @pl.when((odd == n) & (core == k))
+            def _():
+                for mine, other, row in ((a, a_x, 1 - n), (b, b_x, n)):
+                    for value, side in ((mine, k), (other, 1 - k)):
+                        at = (slice(row, row + 1), slice(side * half, (side + 1) * half))
+                        salt[at] = salt_scale[at] * value[...] + salt_base[at]
+                        water[at] = water_scale[at] * value[...] + water_base[at]
 
 
 def assemble(quadripoles, weighted_misfit, order):
@@ -260,8 +273,8 @@
     cross = call(cross_kernel, shape((rows, rows), bf16), [VMEM], "cross", moved=4 * rows * rows * 2)(weights)
     near_give, weights = lax.optimization_barrier((near_give, weights))
     far_give, cross = lax.optimization_barrier((far_give, cross))
+    far_in_1 = lax.ppermute(far_give, both, joint(inner, 1))
     near_in_1 = lax.ppermute(near_give, both, joint(to_mate, 1))
-    far_in_1 = lax.ppermute(far_give, both, joint(inner, 1))
 
     big = 2 * rows * rows * half * 2
     forms = call(
@@ -317,10 +330,17 @@
     a_x = lax.ppermute(form_a, "elec", swap)
     far_in_1, form_a = lax.optimization_barrier((far_in_1, form_a))
     form_b = close("close_b", 0, True, far_in_1, near_in_1, weights, carry_b, early_b)
+    b_same = lax.ppermute(form_b, both, joint(to_mate, 0))
     b_cross = lax.ppermute(form_b, both, joint(to_mate, 1))
-    b_same = lax.ppermute(form_b, both, joint(to_mate, 0))
-    form_z = spread(form_a, a_x, b_same, b_cross)
-    return salt_scale * form_z + salt_base, water_scale * form_z + water_base
+    done = shape((layers, cells), f32)
+    return pl.pallas_call(
+        finish_kernel,
+        out_shape=(done, done),
+        in_specs=[VMEM] * 8,
+        compiler_params=pltpu.CompilerParams(vmem_limit_bytes=2 * MIB),
+        cost_estimate=pl.CostEstimate(flops=0, bytes_accessed=cells * 64, transcendentals=0),
+        name="finish",
+    )(b_same, b_cross, a_x, form_a, salt_scale, salt_base, water_scale, water_base)
 
 
 def solution(mesh):

time: 34.2 us -> 34.1 us (level)
  other arithmetic: 0.9 us -> 0.2 us
  Pallas kernels: 9.16 us -> 9.76 us
    add x1 -> x0, other arithmetic: 0.68 us -> none  [local(): return (salt_scale * form_z + salt_base, water_scale * form_z + water_base)]
    pallas_call x0 -> x1, Pallas kernels: none -> 0.62 us  [local(): pl.pallas_call(finish_kernel, out_shape=(done, done), in_specs=[VMEM] * 8...]
where the time goes in v8:
time: 34.1 us; the launch traced here: 33.7 us
  starting transfers between devices  11.3 us (33%)
  Pallas kernels  9.76 us (29%)
  waiting for transfers between devices  8.61 us (25%)
  matrix products  2.8 us (8%)
  between operations  0.9 us (3%)
    ppermute x1, waiting for transfers between devices, local(): near_in_1 = lax.ppermute(near_give, both, joint(to_mate, 1))  6.72 us
    pallas_call x1, Pallas kernels, local(): call(plane_kernel, shape((2 * layers, half), f32), [VMEM] * 6, 'plane', s...  4.6 us
    ppermute x1, starting transfers between devices, local(): far_in_0 = lax.ppermute(far, both, joint(ahead, 0))  3.6 us
    ppermute x1, starting transfers between devices, local(): near_in_0 = lax.ppermute(near, both, joint(to_mate, 0))  3.04 us
    dot_general x1, matrix products, dot(): return jnp.dot(left, right, preferred_element_type=jnp.float32)  2.8 us
    ppermute x1, starting transfers between devices, local(): b_cross = lax.ppermute(form_b, both, joint(to_mate, 1))  1.53 us
    pallas_call x1, Pallas kernels, local(): call(keep_kernel, (piece,) * 2, [pl.BlockSpec(memory_space=pl.ANY)], 'kee...  1.44 us
    pallas_call x1, Pallas kernels, local(): call(early_kernel, (shape((rows, half), f32),) * 2 + (shape((8, half), f3...  1.39 us
  transfers between devices with their start and end apart: 9, of which 5 were waited for; matrix products, arithmetic and copies ran while one was open for 9% of the time, Pallas kernels for 21%

profile of v8, /device:TPU:0, one launch (start us, length us, event | category | flops | bytes accessed | tf_op | source)
XLA Modules:
  0.0 33.7 jit_solution(1686622171875319659)
XLA Ops:
  0.6 0.0 copy-start
  0.6 0.0 copy-start.2
  0.7 0.0 copy-start.7
  0.7 0.0 copy-start.3
  0.7 1.4 %keep.1 = (bf16[512,512]{1,0:T(8,128)(2,1)S(1)}, bf16[512,512]{1,0:T(8,128)(2,1)S(1)}) custom-call(bf16[512,2,1024]{2,1,0:T(2,128)(2,1)} %potentials.1), custom_call_target="tpu_custom_call" | custom-call | bytes 2097152 | tf_op jit(solution)/shard_map/keep/pallas_call | solution.py:248
  2.1 3.0 %collective-permute-start.3 = (bf16[512,512]{1,0:T(8,128)(2,1)S(1)}, bf16[512,512]{1,0:T(8,128)(2,1)S(1)}, u32[]{:S(2)}, u32[]{:S(2)}) collective-permute-start(bf16[512,512]{1,0:T(8,128)(2,1)S(1)} %get-tuple-element.47.near), channel_id=1, source_target_pairs={{0,2},{1,3},{2,0},{3,1},{4,6},{5,7},{6,4},{7,5},{8,10},{9,11},{10,... | collective-permute-start | bytes 1572872 | tf_op jit(solution)/shard_map/ppermute | solution.py:257
  5.2 3.6 %collective-permute-start.4 = (bf16[512,512]{1,0:T(8,128)(2,1)S(1)}, bf16[512,512]{1,0:T(8,128)(2,1)S(1)}, u32[]{:S(2)}, u32[]{:S(2)}) collective-permute-start(bf16[512,512]{1,0:T(8,128)(2,1)S(1)} %get-tuple-element.46.far), channel_id=1, source_target_pairs={{0,12},{1,13},{2,6},{3,7},{4,0},{5,1},{6,10},{7,11},{8,4},{9,5},{1... | collective-permute-start | bytes 1572872 | tf_op jit(solution)/shard_map/ppermute | solution.py:258
  8.8 0.0 copy-done
  8.8 0.5 %give.1 = (bf16[512,512]{1,0:T(8,128)(2,1)S(1)}, bf16[512,512]{1,0:T(8,128)(2,1)S(1)}, bf16[512,1280]{1,0:T(8,128)(2,1)S(1)}, bf16[512,256]{1,0:T(8,128)(2,1)S(1)}) custom-call(bf16[512,2,1024]{2,1,0:T(2,128)(2,1)S(1)} %copy-done), custom_call_target="tpu_custom_call" | custom-call | bytes 4194304 | tf_op jit(solution)/shard_map/give/pallas_call | solution.py:260
  9.2 0.1 collective-permute-start.1
  9.3 0.0 copy-done.2
  9.3 0.0 copy-done.7
  9.4 0.0 copy-done.3
  9.4 2.8 %fusion.10.weights = bf16[1024,1024]{1,0:T(8,128)(2,1)S(1)} fusion(s32[1024]{0:T(1024)S(1)} %add_select_fusion.1, f32[1024]{0:T(1024)S(1)} %convert_element_type.23, s32[1024]{0:T(1024)S(1)} %bitcast.34, s32[1024]{0:T(1024)S(1)} %bitcast.35, s32[1024]{0:T(1024)S(1)} %bitcast.36, s32[1024]{0:T(1024)S(1)} %bitcast.33), kind=kOutput, calls=%fused_computation.12 | convolution fusion | flops 2161115136 | bytes 2121728 | tf_op jit(solution)/shard_map/dot_general | solution.py:29
  12.2 0.0 copy-start.1
  12.2 0.0 copy-start.4
  12.3 0.0 copy-start.5
  12.3 0.0 copy-start.6
  12.3 0.2 cross.1
  12.5 1.3 %collective-permute-start = (bf16[512,512]{1,0:T(8,128)(2,1)S(1)}, bf16[512,512]{1,0:T(8,128)(2,1)S(1)}, u32[]{:S(2)}, u32[]{:S(2)}) collective-permute-start(bf16[512,512]{1,0:T(8,128)(2,1)S(1)} %get-tuple-element.41), channel_id=1, source_target_pairs={{2,7},{3,6},{4,1},{5,0},{6,11},{7,10},{8,5},{9,4},{10,15},{11,14},... | collective-permute-start | bytes 1572872 | tf_op jit(solution)/shard_map/ppermute | solution.py:276
  13.8 0.5 %collective-permute-start.2 = (bf16[512,512]{1,0:T(8,128)(2,1)S(1)}, bf16[512,512]{1,0:T(8,128)(2,1)S(1)}, u32[]{:S(2)}, u32[]{:S(2)}) collective-permute-start(bf16[512,512]{1,0:T(8,128)(2,1)S(1)} %get-tuple-element.44), channel_id=1, source_target_pairs={{0,3},{1,2},{2,1},{3,0},{4,7},{5,6},{6,5},{7,4},{8,11},{9,10},{10,... | collective-permute-start | bytes 1572872 | tf_op jit(solution)/shard_map/ppermute | solution.py:277
  14.3 0.0 copy-done.1
  14.3 0.0 copy-done.4
  14.3 0.0 copy-done.5
  14.3 0.0 copy-done.6
  14.3 0.1 bitcast_multiply_fusion
  14.4 0.0 collective-permute-done.1.parcel.upper
  14.4 4.6 %plane.1 = f32[4,512]{1,0:T(4,128)S(1)} custom-call(bf16[512,512]{1,0:T(8,128)(2,1)S(1)} %get-tuple-element.47.near, bf16[512,512]{1,0:T(8,128)(2,1)S(1)} %get-tuple-element.46.far, bf16[512,256]{1,0:T(8,128)(2,1)S(1)} %get-tuple-element.48.rim, bf16[512,1280]{1,0:T(8,128)(2,1)S(1)} %collective-permute-done.1.parcel.upper, ...), custom_call_target="tpu_custom_call" | custom-call | flops 3221225472 | bytes 8388608 | tf_op jit(solution)/shard_map/plane/pallas_call | solution.py:280
  19.0 0.5 %collective-permute-start.5 = (f32[4,512]{1,0:T(4,128)S(1)}, f32[4,512]{1,0:T(4,128)S(1)}, u32[]{:S(2)}, u32[]{:S(2)}) collective-permute-start(f32[4,512]{1,0:T(4,128)S(1)} %plane.1), channel_id=1, source_target_pairs={{0,1},{1,0},{2,3},{3,2},{4,5},{5,4},{6,7},{7,6},{8,9},{9,8},{10,11... | collective-permute-start | bytes 24584 | tf_op jit(solution)/shard_map/ppermute | solution.py:304
  19.5 0.0 collective-permute-done.3.near_in
  19.5 0.2 collective-permute-done.4.far_in
  19.7 1.4 %early.1 = (f32[512,512]{1,0:T(8,128)S(1)}, f32[512,512]{1,0:T(8,128)S(1)}, f32[8,512]{1,0:T(8,128)S(1)}, f32[8,512]{1,0:T(8,128)S(1)}) custom-call(bf16[512,512]{1,0:T(8,128)(2,1)S(1)} %get-tuple-element.46.far, bf16[512,512]{1,0:T(8,128)(2,1)S(1)} %collective-permute-done.3.near_in, bf16[512,512]{1,0:T(8,128)(2,1)S(1)} %collective-permute-done.4.far_in, ...), custom_call_target="tpu_custom_call" | custom-call | flops 2147483648 | bytes 8388608 | tf_op jit(solution)/shard_map/early/pallas_call | solution.py:311
  21.1 0.0 collective-permute-done.5
  21.1 0.1 fusion.20
  21.2 6.7 %collective-permute-done.2.lower = bf16[512,512]{1,0:T(8,128)(2,1)S(1)} collective-permute-done((bf16[512,512]{1,0:T(8,128)(2,1)S(1)}, bf16[512,512]{1,0:T(8,128)(2,1)S(1)}, u32[]{:S(2)}, u32[]{:S(2)}) %collective-permute-start.2) | collective-permute-done | bytes 524320 | tf_op jit(solution)/shard_map/ppermute | solution.py:277
  27.9 0.5 %close_a.1.a = f32[1,512]{1,0:T(1,128)S(1)} custom-call(bf16[512,1280]{1,0:T(8,128)(2,1)S(1)} %collective-permute-done.1.parcel.upper, bf16[512,512]{1,0:T(8,128)(2,1)S(1)} %collective-permute-done.2.lower, bf16[1024,1024]{1,0:T(8,128)(2,1)S(1)} %fusion.10.weights, f32[512,512]{1,0:T(8,128)S(1)} %get-tuple-element.51.carry, f32[8,512]{1,0:T(8,128)S(1)} %get-tuple-element.55.early), custom_call_target="tpu_custom_call" | custom-call | flops 536870912 | bytes 4194304 | tf_op jit(solution)/shard_map/close_a/pallas_call | solution.py:325
  28.4 0.2 collective-permute-done.upper
  28.7 0.5 %close_b.1 = f32[1,512]{1,0:T(1,128)S(1)} custom-call(bf16[512,512]{1,0:T(8,128)(2,1)S(1)} %collective-permute-done.upper, bf16[512,512]{1,0:T(8,128)(2,1)S(1)} %collective-permute-done.2.lower, bf16[1024,1024]{1,0:T(8,128)(2,1)S(1)} %fusion.10.weights, f32[512,512]{1,0:T(8,128)S(1)} %get-tuple-element.57.carry, f32[8,512]{1,0:T(8,128)S(1)} %get-tuple-element.58.early), custom_call_target="tpu_custom_call" | custom-call | flops 536870912 | bytes 4194304 | tf_op jit(solution)/shard_map/close_b/pallas_call | solution.py:325
  29.2 0.8 %collective-permute-start.6 = (f32[1,512]{1,0:T(1,128)S(1)}, f32[1,512]{1,0:T(1,128)S(1)}, u32[]{:S(2)}, u32[]{:S(2)}) collective-permute-start(f32[1,512]{1,0:T(1,128)S(1)} %close_b.1), channel_id=1, source_target_pairs={{0,2},{1,3},{2,0},{3,1},{4,6},{5,7},{6,4},{7,5},{8,10},{9,11},{10,... | collective-permute-start | bytes 6152 | tf_op jit(solution)/shard_map/ppermute | solution.py:333
  30.0 1.5 %collective-permute-start.7 = (f32[1,512]{1,0:T(1,128)S(1)}, f32[1,512]{1,0:T(1,128)S(1)}, u32[]{:S(2)}, u32[]{:S(2)}) collective-permute-start(f32[1,512]{1,0:T(1,128)S(1)} %close_b.1), channel_id=1, source_target_pairs={{0,3},{1,2},{2,1},{3,0},{4,7},{5,6},{6,5},{7,4},{8,11},{9,10},{10,... | collective-permute-start | bytes 6152 | tf_op jit(solution)/shard_map/ppermute | solution.py:334
  31.6 0.0 collective-permute-start.8
  31.6 1.3 %collective-permute-done.6.b = f32[1,512]{1,0:T(1,128)S(1)} collective-permute-done((f32[1,512]{1,0:T(1,128)S(1)}, f32[1,512]{1,0:T(1,128)S(1)}, u32[]{:S(2)}, u32[]{:S(2)}) %collective-permute-start.6) | collective-permute-done | bytes 2080 | tf_op jit(solution)/shard_map/ppermute | solution.py:333
  32.9 0.2 collective-permute-done.7.b_x
  33.0 0.0 collective-permute-done.8.a_x
  33.0 0.6 %finish.1 = (f32[2,1024]{1,0:T(2,128)}, f32[2,1024]{1,0:T(2,128)}) custom-call(f32[1,512]{1,0:T(1,128)S(1)} %collective-permute-done.6.b, f32[1,512]{1,0:T(1,128)S(1)} %collective-permute-done.7.b_x, f32[1,512]{1,0:T(1,128)S(1)} %collective-permute-done.8.a_x, f32[1,512]{1,0:T(1,128)S(1)} %close_a.1.a, f32[2,1024]{1,0:T(2,128)S(1)} %get-tuple-element.60.salt_scale, ...), custom_call_target="tpu_custom_call" | custom-call | bytes 65536 | tf_op jit(solution)/shard_map/finish/pallas_call | solution.py:336
  (10 shorter events, 0.1 us)
Async XLA Ops:
  0.6 8.1 %copy-start = (bf16[512,2,1024]{2,1,0:T(2,128)(2,1)S(1)}, bf16[512,2,1024]{2,1,0:T(2,128)(2,1)}, u32[]{:S(2)}) copy-start(bf16[512,2,1024]{2,1,0:T(2,128)(2,1)} %potentials.1) | copy-start | bytes 6291460
  0.6 8.7 %copy-start.2 = (s32[1024]{0:T(1024)S(1)}, s32[1024]{0:T(1024)}, u32[]{:S(2)}) copy-start(s32[1024]{0:T(1024)} %param.9) | copy-start | bytes 12292
  0.7 8.7 %copy-start.7 = (bf16[1024]{0:T(1024)(128)(2,1)S(1)}, bf16[1024]{0:T(1024)(128)(2,1)}, u32[]{:S(2)}) copy-start(bf16[1024]{0:T(1024)(128)(2,1)} %param.11) | copy-start | bytes 6148
  0.7 8.7 %copy-start.3 = (s32[1024,4]{0,1:T(4,128)S(1)}, s32[1024,4]{0,1:T(4,128)}, u32[]{:S(2)}) copy-start(s32[1024,4]{0,1:T(4,128)} %param.10) | copy-start | bytes 49156
  2.1 17.4 %collective-permute-start.3 = (bf16[512,512]{1,0:T(8,128)(2,1)S(1)}, bf16[512,512]{1,0:T(8,128)(2,1)S(1)}, u32[]{:S(2)}, u32[]{:S(2)}) collective-permute-start(bf16[512,512]{1,0:T(8,128)(2,1)S(1)} %get-tuple-element.47.near), channel_id=1, source_target_pairs={{0,2},{1,3},{2,0},{3,1},{4,6},{5,7},{6,4},{7,5},{8,10},{9,11},{10,... | collective-permute-start | bytes 1572872 | tf_op jit(solution)/shard_map/ppermute | solution.py:257
  5.2 14.5 %collective-permute-start.4 = (bf16[512,512]{1,0:T(8,128)(2,1)S(1)}, bf16[512,512]{1,0:T(8,128)(2,1)S(1)}, u32[]{:S(2)}, u32[]{:S(2)}) collective-permute-start(bf16[512,512]{1,0:T(8,128)(2,1)S(1)} %get-tuple-element.46.far), channel_id=1, source_target_pairs={{0,12},{1,13},{2,6},{3,7},{4,0},{5,1},{6,10},{7,11},{8,4},{9,5},{1... | collective-permute-start | bytes 1572872 | tf_op jit(solution)/shard_map/ppermute | solution.py:258
  9.2 5.2 %collective-permute-start.1 = (bf16[512,1280]{1,0:T(8,128)(2,1)S(1)}, bf16[512,1280]{1,0:T(8,128)(2,1)S(1)}, u32[]{:S(2)}, u32[]{:S(2)}) collective-permute-start(bf16[512,1280]{1,0:T(8,128)(2,1)S(1)} %get-tuple-element.42), channel_id=1, source_target_pairs={{0,1},{1,0},{2,3},{3,2},{4,5},{5,4},{6,7},{7,6},{8,9},{9,8},{10,11... | collective-permute-start | bytes 3932168 | tf_op jit(solution)/shard_map/ppermute | solution.py:268
  12.2 2.1 %copy-start.1 = (f32[3,2,1024]{2,1,0:T(2,128)S(1)}, f32[3,2,1024]{2,1,0:T(2,128)}, u32[]{:S(2)}) copy-start(f32[3,2,1024]{2,1,0:T(2,128)} %param.15) | copy-start | bytes 73732
  12.2 2.1 %copy-start.4 = (f32[2,1024]{1,0:T(2,128)S(1)}, f32[2,1024]{1,0:T(2,128)}, u32[]{:S(2)}) copy-start(f32[2,1024]{1,0:T(2,128)} %param.13) | copy-start | bytes 24580
  12.3 2.0 %copy-start.5 = (f32[2,1024]{1,0:T(2,128)S(1)}, f32[2,1024]{1,0:T(2,128)}, u32[]{:S(2)}) copy-start(f32[2,1024]{1,0:T(2,128)} %param.14) | copy-start | bytes 24580
  12.3 2.0 %copy-start.6 = (f32[2,1024]{1,0:T(2,128)S(1)}, f32[2,1024]{1,0:T(2,128)}, u32[]{:S(2)}) copy-start(f32[2,1024]{1,0:T(2,128)} %param.12) | copy-start | bytes 24580
  12.5 16.2 %collective-permute-start = (bf16[512,512]{1,0:T(8,128)(2,1)S(1)}, bf16[512,512]{1,0:T(8,128)(2,1)S(1)}, u32[]{:S(2)}, u32[]{:S(2)}) collective-permute-start(bf16[512,512]{1,0:T(8,128)(2,1)S(1)} %get-tuple-element.41), channel_id=1, source_target_pairs={{2,7},{3,6},{4,1},{5,0},{6,11},{7,10},{8,5},{9,4},{10,15},{11,14},... | collective-permute-start | bytes 1572872 | tf_op jit(solution)/shard_map/ppermute | solution.py:276
  13.8 14.1 %collective-permute-start.2 = (bf16[512,512]{1,0:T(8,128)(2,1)S(1)}, bf16[512,512]{1,0:T(8,128)(2,1)S(1)}, u32[]{:S(2)}, u32[]{:S(2)}) collective-permute-start(bf16[512,512]{1,0:T(8,128)(2,1)S(1)} %get-tuple-element.44), channel_id=1, source_target_pairs={{0,3},{1,2},{2,1},{3,0},{4,7},{5,6},{6,5},{7,4},{8,11},{9,10},{10,... | collective-permute-start | bytes 1572872 | tf_op jit(solution)/shard_map/ppermute | solution.py:277
  19.0 2.1 %collective-permute-start.5 = (f32[4,512]{1,0:T(4,128)S(1)}, f32[4,512]{1,0:T(4,128)S(1)}, u32[]{:S(2)}, u32[]{:S(2)}) collective-permute-start(f32[4,512]{1,0:T(4,128)S(1)} %plane.1), channel_id=1, source_target_pairs={{0,1},{1,0},{2,3},{3,2},{4,5},{5,4},{6,7},{7,6},{8,9},{9,8},{10,11... | collective-permute-start | bytes 24584 | tf_op jit(solution)/shard_map/ppermute | solution.py:304
  29.2 3.7 %collective-permute-start.6 = (f32[1,512]{1,0:T(1,128)S(1)}, f32[1,512]{1,0:T(1,128)S(1)}, u32[]{:S(2)}, u32[]{:S(2)}) collective-permute-start(f32[1,512]{1,0:T(1,128)S(1)} %close_b.1), channel_id=1, source_target_pairs={{0,2},{1,3},{2,0},{3,1},{4,6},{5,7},{6,4},{7,5},{8,10},{9,11},{10,... | collective-permute-start | bytes 6152 | tf_op jit(solution)/shard_map/ppermute | solution.py:333
  30.0 3.0 %collective-permute-start.7 = (f32[1,512]{1,0:T(1,128)S(1)}, f32[1,512]{1,0:T(1,128)S(1)}, u32[]{:S(2)}, u32[]{:S(2)}) collective-permute-start(f32[1,512]{1,0:T(1,128)S(1)} %close_b.1), channel_id=1, source_target_pairs={{0,3},{1,2},{2,1},{3,0},{4,7},{5,6},{6,5},{7,4},{8,11},{9,10},{10,... | collective-permute-start | bytes 6152 | tf_op jit(solution)/shard_map/ppermute | solution.py:334
  31.6 1.5 %collective-permute-start.8 = (f32[1,512]{1,0:T(1,128)S(1)}, f32[1,512]{1,0:T(1,128)S(1)}, u32[]{:S(2)}, u32[]{:S(2)}) collective-permute-start(f32[1,512]{1,0:T(1,128)S(1)} %close_a.1.a), channel_id=1, source_target_pairs={{0,1},{1,0},{2,3},{3,2},{4,5},{5,4},{6,7},{7,6},{8,9},{9,8},{10,11... | collective-permute-start | bytes 6152 | tf_op jit(solution)/shard_map/ppermute | solution.py:330

commit v9 on v8

--- a/solution.py
+++ b/solution.py
@@ -62,9 +62,17 @@
                     near[r : r + 64, :], far[r : r + 64, :] = layers[1 - k], layers[k]
 
 
-def give_kernel(potentials, near, far, parcel, rim):
+def give_kernel(potentials, near, far, parcel, rim, raw, sems):
     odd, core, _ = spot()
     rows, half = near.shape
+    size = rows // sems.shape[0]
+    copies = []
+    for i in range(sems.shape[0]):
+        part = pl.ds(i * size, size)
+        copies.append(pltpu.make_async_copy(potentials.at[part], raw.at[part], sems.at[i]))
+        copies[-1].start()
+    for copy in copies:
+        copy.wait()
     for k in range(2):
         low, high = slice(half - LANES, half), slice(half, half + LANES)
         inner, outer = (low, high) if k == 0 else (high, low)
@@ -74,7 +82,7 @@
         def _():
             for r in range(0, rows, 32):
                 at = slice(r, r + 32)
-                near_v, far_v = levels(potentials[at], odd)
+                near_v, far_v = levels(raw[at], odd)
                 near[at, :] = near_v[:, theirs]
                 far[at, :] = far_v[:, theirs]
                 parcel[at, :half] = near_v[:, theirs]
@@ -187,10 +195,10 @@
     for c in range(0, half, wide):
         changes = []
         for r in range(0, rows, 128):
-            above = upper[r : r + 128, start + c : start + c + wide].astype(jnp.float32)
+            above = upper[r : r + 128, start + c : start + c + wide]
             if masked:
-                above = jnp.where(inside, above, 0.0)
-            changes.append((above - lower[r : r + 128, c : c + wide].astype(jnp.float32)).astype(jnp.bfloat16))
+                above = jnp.where(inside, above, jnp.zeros_like(above))
+            changes.append(above - lower[r : r + 128, c : c + wide])
         delta = jnp.concatenate(changes, axis=0)
         mixed = carry[:, c : c + wide] + dot(weights[rows:, rows:], delta)
         total = early[:, c : c + wide] + jnp.sum((delta.astype(jnp.float32) * mixed).reshape(-1, 8, wide), axis=0)
@@ -260,10 +268,11 @@
     near_give, far_give, parcel, rim = call(
         give_kernel,
         (piece, piece, shape((rows, 2 * half + 2 * LANES), bf16), strip),
-        [VMEM],
+        [pl.BlockSpec(memory_space=pl.ANY)],
         "give",
+        scratch=[pltpu.VMEM((rows, layers, 2 * half), bf16), pltpu.SemaphoreType.DMA((4,))],
         moved=rows * cells * 8,
-        limit=4,
+        limit=47,
     )(potentials)
     parcel = lax.ppermute(parcel, "elec", swap)
 

time: 34.1 us -> 34 us (level)
    ppermute x1, waiting for transfers between devices: 0.24 us -> 0.62 us  [local(): far_in_1 = lax.ppermute(far_give, both, joint(inner, 1))]
  transfers between devices with their start and end apart: 9 -> 9, of which waited for: 5 -> 4; matrix products, arithmetic and copies ran while one was open for 9% -> 9% of each run, Pallas kernels for 21% -> 22%
where the time goes in v9:
time: 34 us; the launch traced here: 33.8 us
  starting transfers between devices  11.2 us (33%)
  Pallas kernels  9.88 us (29%)
  waiting for transfers between devices  8.76 us (26%)
  matrix products  2.8 us (8%)
  between operations  0.92 us (3%)
    ppermute x1, waiting for transfers between devices, local(): near_in_1 = lax.ppermute(near_give, both, joint(to_mate, 1))  6.51 us
    pallas_call x1, Pallas kernels, local(): call(plane_kernel, shape((2 * layers, half), f32), [VMEM] * 6, 'plane', s...  4.6 us
    ppermute x1, starting transfers between devices, local(): far_in_0 = lax.ppermute(far, both, joint(ahead, 0))  3.6 us
    ppermute x1, starting transfers between devices, local(): near_in_0 = lax.ppermute(near, both, joint(to_mate, 0))  3.04 us
    dot_general x1, matrix products, dot(): return jnp.dot(left, right, preferred_element_type=jnp.float32)  2.8 us
    pallas_call x1, Pallas kernels, local(): call(keep_kernel, (piece,) * 2, [pl.BlockSpec(memory_space=pl.ANY)], 'kee...  1.44 us
    ppermute x1, waiting for transfers between devices, local(): b_same = lax.ppermute(form_b, both, joint(to_mate, 0))  1.44 us
    pallas_call x1, Pallas kernels, local(): call(early_kernel, (shape((rows, half), f32),) * 2 + (shape((8, half), f3...  1.39 us
  transfers between devices with their start and end apart: 9, of which 4 were waited for; matrix products, arithmetic and copies ran while one was open for 9% of the time, Pallas kernels for 22%

profile of v9, /device:TPU:0, one launch (start us, length us, event | category | flops | bytes accessed | tf_op | source)
XLA Modules:
  0.0 33.8 jit_solution(16691363586402378454)
XLA Ops:
  0.6 0.0 copy-start
  0.6 0.0 copy-start.2
  0.7 0.0 copy-start.7
  0.7 0.0 copy-start.3
  0.7 1.4 %keep.1 = (bf16[512,512]{1,0:T(8,128)(2,1)S(1)}, bf16[512,512]{1,0:T(8,128)(2,1)S(1)}) custom-call(bf16[512,2,1024]{2,1,0:T(2,128)(2,1)} %potentials.1), custom_call_target="tpu_custom_call" | custom-call | bytes 2097152 | tf_op jit(solution)/shard_map/keep/pallas_call | solution.py:256
  2.1 3.0 %collective-permute-start.3 = (bf16[512,512]{1,0:T(8,128)(2,1)S(1)}, bf16[512,512]{1,0:T(8,128)(2,1)S(1)}, u32[]{:S(2)}, u32[]{:S(2)}) collective-permute-start(bf16[512,512]{1,0:T(8,128)(2,1)S(1)} %get-tuple-element.47.near), channel_id=1, source_target_pairs={{0,2},{1,3},{2,0},{3,1},{4,6},{5,7},{6,4},{7,5},{8,10},{9,11},{10,... | collective-permute-start | bytes 1572872 | tf_op jit(solution)/shard_map/ppermute | solution.py:265
  5.2 3.6 %collective-permute-start.4 = (bf16[512,512]{1,0:T(8,128)(2,1)S(1)}, bf16[512,512]{1,0:T(8,128)(2,1)S(1)}, u32[]{:S(2)}, u32[]{:S(2)}) collective-permute-start(bf16[512,512]{1,0:T(8,128)(2,1)S(1)} %get-tuple-element.46.far), channel_id=1, source_target_pairs={{0,12},{1,13},{2,6},{3,7},{4,0},{5,1},{6,10},{7,11},{8,4},{9,5},{1... | collective-permute-start | bytes 1572872 | tf_op jit(solution)/shard_map/ppermute | solution.py:266
  8.8 0.0 copy-done
  8.8 0.6 %give.1 = (bf16[512,512]{1,0:T(8,128)(2,1)S(1)}, bf16[512,512]{1,0:T(8,128)(2,1)S(1)}, bf16[512,1280]{1,0:T(8,128)(2,1)S(1)}, bf16[512,256]{1,0:T(8,128)(2,1)S(1)}) custom-call(bf16[512,2,1024]{2,1,0:T(2,128)(2,1)S(1)} %copy-done), custom_call_target="tpu_custom_call" | custom-call | bytes 4194304 | tf_op jit(solution)/shard_map/give/pallas_call | solution.py:268
  9.4 0.1 collective-permute-start.1
  9.5 0.0 copy-done.2
  9.5 0.0 copy-done.7
  9.6 0.0 copy-done.3
  9.6 2.8 %fusion.10.weights = bf16[1024,1024]{1,0:T(8,128)(2,1)S(1)} fusion(s32[1024]{0:T(1024)S(1)} %add_select_fusion.1, f32[1024]{0:T(1024)S(1)} %convert_element_type.23, s32[1024]{0:T(1024)S(1)} %bitcast.34, s32[1024]{0:T(1024)S(1)} %bitcast.35, s32[1024]{0:T(1024)S(1)} %bitcast.36, s32[1024]{0:T(1024)S(1)} %bitcast.33), kind=kOutput, calls=%fused_computation.12 | convolution fusion | flops 2161115136 | bytes 2121728 | tf_op jit(solution)/shard_map/dot_general | solution.py:29
  12.4 0.0 copy-start.1
  12.4 0.0 copy-start.4
  12.4 0.0 copy-start.5
  12.4 0.0 copy-start.6
  12.5 0.2 cross.1
  12.7 1.3 %collective-permute-start = (bf16[512,512]{1,0:T(8,128)(2,1)S(1)}, bf16[512,512]{1,0:T(8,128)(2,1)S(1)}, u32[]{:S(2)}, u32[]{:S(2)}) collective-permute-start(bf16[512,512]{1,0:T(8,128)(2,1)S(1)} %get-tuple-element.41), channel_id=1, source_target_pairs={{2,7},{3,6},{4,1},{5,0},{6,11},{7,10},{8,5},{9,4},{10,15},{11,14},... | collective-permute-start | bytes 1572872 | tf_op jit(solution)/shard_map/ppermute | solution.py:285
  14.0 0.5 %collective-permute-start.2 = (bf16[512,512]{1,0:T(8,128)(2,1)S(1)}, bf16[512,512]{1,0:T(8,128)(2,1)S(1)}, u32[]{:S(2)}, u32[]{:S(2)}) collective-permute-start(bf16[512,512]{1,0:T(8,128)(2,1)S(1)} %get-tuple-element.44), channel_id=1, source_target_pairs={{0,3},{1,2},{2,1},{3,0},{4,7},{5,6},{6,5},{7,4},{8,11},{9,10},{10,... | collective-permute-start | bytes 1572872 | tf_op jit(solution)/shard_map/ppermute | solution.py:286
  14.5 0.0 copy-done.1
  14.5 0.0 copy-done.4
  14.5 0.0 copy-done.5
  14.5 0.0 copy-done.6
  14.5 0.1 bitcast_multiply_fusion
  14.6 0.0 collective-permute-done.1.parcel.upper
  14.6 4.6 %plane.1 = f32[4,512]{1,0:T(4,128)S(1)} custom-call(bf16[512,512]{1,0:T(8,128)(2,1)S(1)} %get-tuple-element.47.near, bf16[512,512]{1,0:T(8,128)(2,1)S(1)} %get-tuple-element.46.far, bf16[512,256]{1,0:T(8,128)(2,1)S(1)} %get-tuple-element.48.rim, bf16[512,1280]{1,0:T(8,128)(2,1)S(1)} %collective-permute-done.1.parcel.upper, ...), custom_call_target="tpu_custom_call" | custom-call | flops 3221225472 | bytes 8388608 | tf_op jit(solution)/shard_map/plane/pallas_call | solution.py:289
  19.2 0.5 %collective-permute-start.5 = (f32[4,512]{1,0:T(4,128)S(1)}, f32[4,512]{1,0:T(4,128)S(1)}, u32[]{:S(2)}, u32[]{:S(2)}) collective-permute-start(f32[4,512]{1,0:T(4,128)S(1)} %plane.1), channel_id=1, source_target_pairs={{0,1},{1,0},{2,3},{3,2},{4,5},{5,4},{6,7},{7,6},{8,9},{9,8},{10,11... | collective-permute-start | bytes 24584 | tf_op jit(solution)/shard_map/ppermute | solution.py:313
  19.7 0.0 collective-permute-done.3.near_in
  19.7 0.0 collective-permute-done.4.far_in
  19.7 1.4 %early.1 = (f32[512,512]{1,0:T(8,128)S(1)}, f32[512,512]{1,0:T(8,128)S(1)}, f32[8,512]{1,0:T(8,128)S(1)}, f32[8,512]{1,0:T(8,128)S(1)}) custom-call(bf16[512,512]{1,0:T(8,128)(2,1)S(1)} %get-tuple-element.46.far, bf16[512,512]{1,0:T(8,128)(2,1)S(1)} %collective-permute-done.3.near_in, bf16[512,512]{1,0:T(8,128)(2,1)S(1)} %collective-permute-done.4.far_in, ...), custom_call_target="tpu_custom_call" | custom-call | flops 2147483648 | bytes 8388608 | tf_op jit(solution)/shard_map/early/pallas_call | solution.py:320
  21.1 0.0 collective-permute-done.5
  21.2 0.1 fusion.20
  21.3 6.5 %collective-permute-done.2.lower = bf16[512,512]{1,0:T(8,128)(2,1)S(1)} collective-permute-done((bf16[512,512]{1,0:T(8,128)(2,1)S(1)}, bf16[512,512]{1,0:T(8,128)(2,1)S(1)}, u32[]{:S(2)}, u32[]{:S(2)}) %collective-permute-start.2) | collective-permute-done | bytes 524320 | tf_op jit(solution)/shard_map/ppermute | solution.py:286
  27.8 0.5 %close_a.1.a = f32[1,512]{1,0:T(1,128)S(1)} custom-call(bf16[512,1280]{1,0:T(8,128)(2,1)S(1)} %collective-permute-done.1.parcel.upper, bf16[512,512]{1,0:T(8,128)(2,1)S(1)} %collective-permute-done.2.lower, bf16[1024,1024]{1,0:T(8,128)(2,1)S(1)} %fusion.10.weights, f32[512,512]{1,0:T(8,128)S(1)} %get-tuple-element.51.carry, f32[8,512]{1,0:T(8,128)S(1)} %get-tuple-element.55.early), custom_call_target="tpu_custom_call" | custom-call | flops 536870912 | bytes 4194304 | tf_op jit(solution)/shard_map/close_a/pallas_call | solution.py:334
  28.3 0.6 %collective-permute-done.upper = bf16[512,512]{1,0:T(8,128)(2,1)S(1)} collective-permute-done((bf16[512,512]{1,0:T(8,128)(2,1)S(1)}, bf16[512,512]{1,0:T(8,128)(2,1)S(1)}, u32[]{:S(2)}, u32[]{:S(2)}) %collective-permute-start) | collective-permute-done | bytes 524320 | tf_op jit(solution)/shard_map/ppermute | solution.py:285
  28.9 0.5 %close_b.1 = f32[1,512]{1,0:T(1,128)S(1)} custom-call(bf16[512,512]{1,0:T(8,128)(2,1)S(1)} %collective-permute-done.upper, bf16[512,512]{1,0:T(8,128)(2,1)S(1)} %collective-permute-done.2.lower, bf16[1024,1024]{1,0:T(8,128)(2,1)S(1)} %fusion.10.weights, f32[512,512]{1,0:T(8,128)S(1)} %get-tuple-element.57.carry, f32[8,512]{1,0:T(8,128)S(1)} %get-tuple-element.58.early), custom_call_target="tpu_custom_call" | custom-call | flops 536870912 | bytes 4194304 | tf_op jit(solution)/shard_map/close_b/pallas_call | solution.py:334
  29.3 0.8 %collective-permute-start.6 = (f32[1,512]{1,0:T(1,128)S(1)}, f32[1,512]{1,0:T(1,128)S(1)}, u32[]{:S(2)}, u32[]{:S(2)}) collective-permute-start(f32[1,512]{1,0:T(1,128)S(1)} %close_b.1), channel_id=1, source_target_pairs={{0,2},{1,3},{2,0},{3,1},{4,6},{5,7},{6,4},{7,5},{8,10},{9,11},{10,... | collective-permute-start | bytes 6152 | tf_op jit(solution)/shard_map/ppermute | solution.py:342
  30.2 1.3 %collective-permute-start.7 = (f32[1,512]{1,0:T(1,128)S(1)}, f32[1,512]{1,0:T(1,128)S(1)}, u32[]{:S(2)}, u32[]{:S(2)}) collective-permute-start(f32[1,512]{1,0:T(1,128)S(1)} %close_b.1), channel_id=1, source_target_pairs={{0,3},{1,2},{2,1},{3,0},{4,7},{5,6},{6,5},{7,4},{8,11},{9,10},{10,... | collective-permute-start | bytes 6152 | tf_op jit(solution)/shard_map/ppermute | solution.py:343
  31.5 0.1 collective-permute-start.8
  31.6 1.4 %collective-permute-done.6.b = f32[1,512]{1,0:T(1,128)S(1)} collective-permute-done((f32[1,512]{1,0:T(1,128)S(1)}, f32[1,512]{1,0:T(1,128)S(1)}, u32[]{:S(2)}, u32[]{:S(2)}) %collective-permute-start.6) | collective-permute-done | bytes 2080 | tf_op jit(solution)/shard_map/ppermute | solution.py:342
  33.0 0.2 collective-permute-done.7.b_x
  33.2 0.0 collective-permute-done.8.a_x
  33.2 0.6 %finish.1 = (f32[2,1024]{1,0:T(2,128)}, f32[2,1024]{1,0:T(2,128)}) custom-call(f32[1,512]{1,0:T(1,128)S(1)} %collective-permute-done.6.b, f32[1,512]{1,0:T(1,128)S(1)} %collective-permute-done.7.b_x, f32[1,512]{1,0:T(1,128)S(1)} %collective-permute-done.8.a_x, f32[1,512]{1,0:T(1,128)S(1)} %close_a.1.a, f32[2,1024]{1,0:T(2,128)S(1)} %get-tuple-element.60.salt_scale, ...), custom_call_target="tpu_custom_call" | custom-call | bytes 65536 | tf_op jit(solution)/shard_map/finish/pallas_call | solution.py:345
  (10 shorter events, 0.1 us)
Async XLA Ops:
  0.6 8.1 %copy-start = (bf16[512,2,1024]{2,1,0:T(2,128)(2,1)S(1)}, bf16[512,2,1024]{2,1,0:T(2,128)(2,1)}, u32[]{:S(2)}) copy-start(bf16[512,2,1024]{2,1,0:T(2,128)(2,1)} %potentials.1) | copy-start | bytes 6291460
  0.6 8.9 %copy-start.2 = (s32[1024]{0:T(1024)S(1)}, s32[1024]{0:T(1024)}, u32[]{:S(2)}) copy-start(s32[1024]{0:T(1024)} %param.9) | copy-start | bytes 12292
  0.7 8.9 %copy-start.7 = (bf16[1024]{0:T(1024)(128)(2,1)S(1)}, bf16[1024]{0:T(1024)(128)(2,1)}, u32[]{:S(2)}) copy-start(bf16[1024]{0:T(1024)(128)(2,1)} %param.11) | copy-start | bytes 6148
  0.7 8.9 %copy-start.3 = (s32[1024,4]{0,1:T(4,128)S(1)}, s32[1024,4]{0,1:T(4,128)}, u32[]{:S(2)}) copy-start(s32[1024,4]{0,1:T(4,128)} %param.10) | copy-start | bytes 49156
  2.1 17.6 %collective-permute-start.3 = (bf16[512,512]{1,0:T(8,128)(2,1)S(1)}, bf16[512,512]{1,0:T(8,128)(2,1)S(1)}, u32[]{:S(2)}, u32[]{:S(2)}) collective-permute-start(bf16[512,512]{1,0:T(8,128)(2,1)S(1)} %get-tuple-element.47.near), channel_id=1, source_target_pairs={{0,2},{1,3},{2,0},{3,1},{4,6},{5,7},{6,4},{7,5},{8,10},{9,11},{10,... | collective-permute-start | bytes 1572872 | tf_op jit(solution)/shard_map/ppermute | solution.py:265
  5.2 14.5 %collective-permute-start.4 = (bf16[512,512]{1,0:T(8,128)(2,1)S(1)}, bf16[512,512]{1,0:T(8,128)(2,1)S(1)}, u32[]{:S(2)}, u32[]{:S(2)}) collective-permute-start(bf16[512,512]{1,0:T(8,128)(2,1)S(1)} %get-tuple-element.46.far), channel_id=1, source_target_pairs={{0,12},{1,13},{2,6},{3,7},{4,0},{5,1},{6,10},{7,11},{8,4},{9,5},{1... | collective-permute-start | bytes 1572872 | tf_op jit(solution)/shard_map/ppermute | solution.py:266
  9.4 5.1 %collective-permute-start.1 = (bf16[512,1280]{1,0:T(8,128)(2,1)S(1)}, bf16[512,1280]{1,0:T(8,128)(2,1)S(1)}, u32[]{:S(2)}, u32[]{:S(2)}) collective-permute-start(bf16[512,1280]{1,0:T(8,128)(2,1)S(1)} %get-tuple-element.42), channel_id=1, source_target_pairs={{0,1},{1,0},{2,3},{3,2},{4,5},{5,4},{6,7},{7,6},{8,9},{9,8},{10,11... | collective-permute-start | bytes 3932168 | tf_op jit(solution)/shard_map/ppermute | solution.py:277
  12.4 2.1 %copy-start.1 = (f32[3,2,1024]{2,1,0:T(2,128)S(1)}, f32[3,2,1024]{2,1,0:T(2,128)}, u32[]{:S(2)}) copy-start(f32[3,2,1024]{2,1,0:T(2,128)} %param.15) | copy-start | bytes 73732
  12.4 2.1 %copy-start.4 = (f32[2,1024]{1,0:T(2,128)S(1)}, f32[2,1024]{1,0:T(2,128)}, u32[]{:S(2)}) copy-start(f32[2,1024]{1,0:T(2,128)} %param.13) | copy-start | bytes 24580
  12.4 2.0 %copy-start.5 = (f32[2,1024]{1,0:T(2,128)S(1)}, f32[2,1024]{1,0:T(2,128)}, u32[]{:S(2)}) copy-start(f32[2,1024]{1,0:T(2,128)} %param.14) | copy-start | bytes 24580
  12.4 2.0 %copy-start.6 = (f32[2,1024]{1,0:T(2,128)S(1)}, f32[2,1024]{1,0:T(2,128)}, u32[]{:S(2)}) copy-start(f32[2,1024]{1,0:T(2,128)} %param.12) | copy-start | bytes 24580
  12.7 16.2 %collective-permute-start = (bf16[512,512]{1,0:T(8,128)(2,1)S(1)}, bf16[512,512]{1,0:T(8,128)(2,1)S(1)}, u32[]{:S(2)}, u32[]{:S(2)}) collective-permute-start(bf16[512,512]{1,0:T(8,128)(2,1)S(1)} %get-tuple-element.41), channel_id=1, source_target_pairs={{2,7},{3,6},{4,1},{5,0},{6,11},{7,10},{8,5},{9,4},{10,15},{11,14},... | collective-permute-start | bytes 1572872 | tf_op jit(solution)/shard_map/ppermute | solution.py:285
  14.0 13.8 %collective-permute-start.2 = (bf16[512,512]{1,0:T(8,128)(2,1)S(1)}, bf16[512,512]{1,0:T(8,128)(2,1)S(1)}, u32[]{:S(2)}, u32[]{:S(2)}) collective-permute-start(bf16[512,512]{1,0:T(8,128)(2,1)S(1)} %get-tuple-element.44), channel_id=1, source_target_pairs={{0,3},{1,2},{2,1},{3,0},{4,7},{5,6},{6,5},{7,4},{8,11},{9,10},{10,... | collective-permute-start | bytes 1572872 | tf_op jit(solution)/shard_map/ppermute | solution.py:286
  19.2 1.9 %collective-permute-start.5 = (f32[4,512]{1,0:T(4,128)S(1)}, f32[4,512]{1,0:T(4,128)S(1)}, u32[]{:S(2)}, u32[]{:S(2)}) collective-permute-start(f32[4,512]{1,0:T(4,128)S(1)} %plane.1), channel_id=1, source_target_pairs={{0,1},{1,0},{2,3},{3,2},{4,5},{5,4},{6,7},{7,6},{8,9},{9,8},{10,11... | collective-permute-start | bytes 24584 | tf_op jit(solution)/shard_map/ppermute | solution.py:313
  29.3 3.7 %collective-permute-start.6 = (f32[1,512]{1,0:T(1,128)S(1)}, f32[1,512]{1,0:T(1,128)S(1)}, u32[]{:S(2)}, u32[]{:S(2)}) collective-permute-start(f32[1,512]{1,0:T(1,128)S(1)} %close_b.1), channel_id=1, source_target_pairs={{0,2},{1,3},{2,0},{3,1},{4,6},{5,7},{6,4},{7,5},{8,10},{9,11},{10,... | collective-permute-start | bytes 6152 | tf_op jit(solution)/shard_map/ppermute | solution.py:342
  30.2 3.0 %collective-permute-start.7 = (f32[1,512]{1,0:T(1,128)S(1)}, f32[1,512]{1,0:T(1,128)S(1)}, u32[]{:S(2)}, u32[]{:S(2)}) collective-permute-start(f32[1,512]{1,0:T(1,128)S(1)} %close_b.1), channel_id=1, source_target_pairs={{0,3},{1,2},{2,1},{3,0},{4,7},{5,6},{6,5},{7,4},{8,11},{9,10},{10,... | collective-permute-start | bytes 6152 | tf_op jit(solution)/shard_map/ppermute | solution.py:343
  31.5 1.7 %collective-permute-start.8 = (f32[1,512]{1,0:T(1,128)S(1)}, f32[1,512]{1,0:T(1,128)S(1)}, u32[]{:S(2)}, u32[]{:S(2)}) collective-permute-start(f32[1,512]{1,0:T(1,128)S(1)} %close_a.1.a), channel_id=1, source_target_pairs={{0,1},{1,0},{2,3},{3,2},{4,5},{5,4},{6,7},{7,6},{8,9},{9,8},{10,11... | collective-permute-start | bytes 6152 | tf_op jit(solution)/shard_map/ppermute | solution.py:339

commit v10 on v9

--- a/solution.py
+++ b/solution.py
@@ -272,7 +272,7 @@
         "give",
         scratch=[pltpu.VMEM((rows, layers, 2 * half), bf16), pltpu.SemaphoreType.DMA((4,))],
         moved=rows * cells * 8,
-        limit=47,
+        limit=50,
     )(potentials)
     parcel = lax.ppermute(parcel, "elec", swap)
 
@@ -280,8 +280,6 @@
     quadripoles, near_give = lax.optimization_barrier((quadripoles, near_give))
     weights = assemble(quadripoles, weighted_misfit, order)
     cross = call(cross_kernel, shape((rows, rows), bf16), [VMEM], "cross", moved=4 * rows * rows * 2)(weights)
-    near_give, weights = lax.optimization_barrier((near_give, weights))
-    far_give, cross = lax.optimization_barrier((far_give, cross))
     far_in_1 = lax.ppermute(far_give, both, joint(inner, 1))
     near_in_1 = lax.ppermute(near_give, both, joint(to_mate, 1))
 

time: 34 us -> 33.9 us (level)
  waiting for transfers between devices: 8.76 us -> 6.33 us
  Pallas kernels: 9.88 us -> 11.1 us
  local copies, waits for them, and re-layouts: 0.08 us -> 0.51 us
  starting transfers between devices: 11.2 us -> 11.6 us
    ppermute x1, waiting for transfers between devices: 6.51 us -> 4.59 us  [local(): near_in_1 = lax.ppermute(near_give, both, joint(to_mate, 1))]
    pallas_call x1, Pallas kernels: 0.64 us -> 2.01 us  [local(): call(give_kernel, (piece, piece, shape((rows, 2 * half + 2 * LANES), bf16...]
    ppermute x1, waiting for transfers between devices: 1.44 us -> 0.94 us  [local(): b_same = lax.ppermute(form_b, both, joint(to_mate, 0))]
    unnamed x16 -> x14, local copies, waits for them, and re-layouts: 0.04 us -> 0.48 us
    ppermute x1, waiting for transfers between devices: 0.62 us -> 0.27 us  [local(): far_in_1 = lax.ppermute(far_give, both, joint(inner, 1))]
  transfers between devices with their start and end apart: 9 -> 9, of which waited for: 4 -> 4; matrix products, arithmetic and copies ran while one was open for 9% -> 9% of each run, Pallas kernels for 22% -> 26%
where the time goes in v10:
time: 33.9 us; the launch traced here: 33.4 us
  starting transfers between devices  11.6 us (34%)
  Pallas kernels  11.1 us (33%)
  waiting for transfers between devices  6.33 us (19%)
  matrix products  2.8 us (8%)
  between operations  0.88 us (3%)
  local copies, waits for them, and re-layouts  0.51 us (2%)
    ppermute x1, waiting for transfers between devices, local(): near_in_1 = lax.ppermute(near_give, both, joint(to_mate, 1))  4.59 us
    pallas_call x1, Pallas kernels, local(): call(plane_kernel, shape((2 * layers, half), f32), [VMEM] * 6, 'plane', s...  4.59 us
    ppermute x1, starting transfers between devices, local(): far_in_0 = lax.ppermute(far, both, joint(ahead, 0))  3.6 us
    ppermute x1, starting transfers between devices, local(): near_in_0 = lax.ppermute(near, both, joint(to_mate, 0))  3.04 us
    dot_general x1, matrix products, dot(): return jnp.dot(left, right, preferred_element_type=jnp.float32)  2.8 us
    pallas_call x1, Pallas kernels, local(): call(give_kernel, (piece, piece, shape((rows, 2 * half + 2 * LANES), bf16...  2.01 us
    ppermute x1, starting transfers between devices, local(): b_cross = lax.ppermute(form_b, both, joint(to_mate, 1))  1.56 us
    pallas_call x1, Pallas kernels, local(): call(early_kernel, (shape((rows, half), f32),) * 2 + (shape((8, half), f3...  1.39 us
  transfers between devices with their start and end apart: 9, of which 4 were waited for; matrix products, arithmetic and copies ran while one was open for 9% of the time, Pallas kernels for 26%

profile of v10, /device:TPU:0, one launch (start us, length us, event | category | flops | bytes accessed | tf_op | source)
XLA Modules:
  0.0 33.4 jit_solution(16730201852853090759)
XLA Ops:
  0.6 0.0 copy-start.1
  0.6 0.0 copy-start.6
  0.7 0.0 copy-start.2
  0.7 1.3 %keep.1 = (bf16[512,512]{1,0:T(8,128)(2,1)S(1)}, bf16[512,512]{1,0:T(8,128)(2,1)S(1)}) custom-call(bf16[512,2,1024]{2,1,0:T(2,128)(2,1)} %potentials.1), custom_call_target="tpu_custom_call" | custom-call | bytes 2097152 | tf_op jit(solution)/shard_map/keep/pallas_call | solution.py:256
  2.0 3.0 %collective-permute-start.3 = (bf16[512,512]{1,0:T(8,128)(2,1)S(1)}, bf16[512,512]{1,0:T(8,128)(2,1)S(1)}, u32[]{:S(2)}, u32[]{:S(2)}) collective-permute-start(bf16[512,512]{1,0:T(8,128)(2,1)S(1)} %get-tuple-element.40.near), channel_id=1, source_target_pairs={{0,2},{1,3},{2,0},{3,1},{4,6},{5,7},{6,4},{7,5},{8,10},{9,11},{10,... | collective-permute-start | bytes 1572872 | tf_op jit(solution)/shard_map/ppermute | solution.py:265
  5.0 3.6 %collective-permute-start.4 = (bf16[512,512]{1,0:T(8,128)(2,1)S(1)}, bf16[512,512]{1,0:T(8,128)(2,1)S(1)}, u32[]{:S(2)}, u32[]{:S(2)}) collective-permute-start(bf16[512,512]{1,0:T(8,128)(2,1)S(1)} %get-tuple-element.39.far), channel_id=1, source_target_pairs={{0,12},{1,13},{2,6},{3,7},{4,0},{5,1},{6,10},{7,11},{8,4},{9,5},{1... | collective-permute-start | bytes 1572872 | tf_op jit(solution)/shard_map/ppermute | solution.py:266
  8.6 2.0 %give.1 = (bf16[512,512]{1,0:T(8,128)(2,1)S(1)}, bf16[512,512]{1,0:T(8,128)(2,1)S(1)}, bf16[512,1280]{1,0:T(8,128)(2,1)S(1)}, bf16[512,256]{1,0:T(8,128)(2,1)S(1)}) custom-call(bf16[512,2,1024]{2,1,0:T(2,128)(2,1)} %potentials.1), custom_call_target="tpu_custom_call" | custom-call | bytes 4194304 | tf_op jit(solution)/shard_map/give/pallas_call | solution.py:268
  10.6 1.3 %collective-permute-start = (bf16[512,512]{1,0:T(8,128)(2,1)S(1)}, bf16[512,512]{1,0:T(8,128)(2,1)S(1)}, u32[]{:S(2)}, u32[]{:S(2)}) collective-permute-start(bf16[512,512]{1,0:T(8,128)(2,1)S(1)} %get-tuple-element.33), channel_id=1, source_target_pairs={{2,7},{3,6},{4,1},{5,0},{6,11},{7,10},{8,5},{9,4},{10,15},{11,14},... | collective-permute-start | bytes 1572872 | tf_op jit(solution)/shard_map/ppermute | solution.py:283
  11.9 0.1 collective-permute-start.1
  12.0 0.5 %collective-permute-start.2 = (bf16[512,512]{1,0:T(8,128)(2,1)S(1)}, bf16[512,512]{1,0:T(8,128)(2,1)S(1)}, u32[]{:S(2)}, u32[]{:S(2)}) collective-permute-start(bf16[512,512]{1,0:T(8,128)(2,1)S(1)} %get-tuple-element.36), channel_id=1, source_target_pairs={{0,3},{1,2},{2,1},{3,0},{4,7},{5,6},{6,5},{7,4},{8,11},{9,10},{10,... | collective-permute-start | bytes 1572872 | tf_op jit(solution)/shard_map/ppermute | solution.py:284
  12.5 0.0 copy-done.1
  12.5 0.0 copy-done.6
  12.5 0.0 copy-done.2
  12.6 2.8 %fusion.10.weights = bf16[1024,1024]{1,0:T(8,128)(2,1)S(1)} fusion(s32[1024]{0:T(1024)S(1)} %add_select_fusion.1, f32[1024]{0:T(1024)S(1)} %convert_element_type.23, s32[1024]{0:T(1024)S(1)} %bitcast.34, s32[1024]{0:T(1024)S(1)} %bitcast.35, s32[1024]{0:T(1024)S(1)} %bitcast.36, s32[1024]{0:T(1024)S(1)} %bitcast.33), kind=kOutput, calls=%fused_computation.12 | convolution fusion | flops 2161115136 | bytes 2121728 | tf_op jit(solution)/shard_map/dot_general | solution.py:29
  15.4 0.0 copy-start
  15.4 0.0 copy-start.3
  15.4 0.0 copy-start.4
  15.4 0.0 copy-start.5
  15.4 0.2 cross.1
  15.7 0.4 %copy-done = f32[3,2,1024]{2,1,0:T(2,128)S(1)} copy-done((f32[3,2,1024]{2,1,0:T(2,128)S(1)}, f32[3,2,1024]{2,1,0:T(2,128)}, u32[]{:S(2)}) %copy-start) | copy-done | bytes 24600
  16.1 0.0 copy-done.3
  16.1 0.0 copy-done.4
  16.1 0.0 copy-done.5
  16.1 0.1 bitcast_multiply_fusion
  16.2 0.0 collective-permute-done.1.parcel.upper
  16.2 4.6 %plane.1 = f32[4,512]{1,0:T(4,128)S(1)} custom-call(bf16[512,512]{1,0:T(8,128)(2,1)S(1)} %get-tuple-element.40.near, bf16[512,512]{1,0:T(8,128)(2,1)S(1)} %get-tuple-element.39.far, bf16[512,256]{1,0:T(8,128)(2,1)S(1)} %get-tuple-element.41.rim, bf16[512,1280]{1,0:T(8,128)(2,1)S(1)} %collective-permute-done.1.parcel.upper, ...), custom_call_target="tpu_custom_call" | custom-call | flops 3221225472 | bytes 8388608 | tf_op jit(solution)/shard_map/plane/pallas_call | solution.py:287
  20.8 0.5 %collective-permute-start.5 = (f32[4,512]{1,0:T(4,128)S(1)}, f32[4,512]{1,0:T(4,128)S(1)}, u32[]{:S(2)}, u32[]{:S(2)}) collective-permute-start(f32[4,512]{1,0:T(4,128)S(1)} %plane.1), channel_id=1, source_target_pairs={{0,1},{1,0},{2,3},{3,2},{4,5},{5,4},{6,7},{7,6},{8,9},{9,8},{10,11... | collective-permute-start | bytes 24584 | tf_op jit(solution)/shard_map/ppermute | solution.py:311
  21.3 0.0 collective-permute-done.3.near_in
  21.3 0.0 collective-permute-done.4.far_in
  21.3 1.4 %early.1 = (f32[512,512]{1,0:T(8,128)S(1)}, f32[512,512]{1,0:T(8,128)S(1)}, f32[8,512]{1,0:T(8,128)S(1)}, f32[8,512]{1,0:T(8,128)S(1)}) custom-call(bf16[512,512]{1,0:T(8,128)(2,1)S(1)} %get-tuple-element.39.far, bf16[512,512]{1,0:T(8,128)(2,1)S(1)} %collective-permute-done.3.near_in, bf16[512,512]{1,0:T(8,128)(2,1)S(1)} %collective-permute-done.4.far_in, ...), custom_call_target="tpu_custom_call" | custom-call | flops 2147483648 | bytes 8388608 | tf_op jit(solution)/shard_map/early/pallas_call | solution.py:318
  22.7 0.0 collective-permute-done.5
  22.7 0.1 fusion.20
  22.8 4.6 %collective-permute-done.2.lower = bf16[512,512]{1,0:T(8,128)(2,1)S(1)} collective-permute-done((bf16[512,512]{1,0:T(8,128)(2,1)S(1)}, bf16[512,512]{1,0:T(8,128)(2,1)S(1)}, u32[]{:S(2)}, u32[]{:S(2)}) %collective-permute-start.2) | collective-permute-done | bytes 524320 | tf_op jit(solution)/shard_map/ppermute | solution.py:284
  27.4 0.5 %close_a.1.a = f32[1,512]{1,0:T(1,128)S(1)} custom-call(bf16[512,1280]{1,0:T(8,128)(2,1)S(1)} %collective-permute-done.1.parcel.upper, bf16[512,512]{1,0:T(8,128)(2,1)S(1)} %collective-permute-done.2.lower, bf16[1024,1024]{1,0:T(8,128)(2,1)S(1)} %fusion.10.weights, f32[512,512]{1,0:T(8,128)S(1)} %get-tuple-element.43.carry, f32[8,512]{1,0:T(8,128)S(1)} %get-tuple-element.47.early), custom_call_target="tpu_custom_call" | custom-call | flops 536870912 | bytes 4194304 | tf_op jit(solution)/shard_map/close_a/pallas_call | solution.py:332
  27.9 0.3 collective-permute-done.upper
  28.2 0.5 %close_b.1 = f32[1,512]{1,0:T(1,128)S(1)} custom-call(bf16[512,512]{1,0:T(8,128)(2,1)S(1)} %collective-permute-done.upper, bf16[512,512]{1,0:T(8,128)(2,1)S(1)} %collective-permute-done.2.lower, bf16[1024,1024]{1,0:T(8,128)(2,1)S(1)} %fusion.10.weights, f32[512,512]{1,0:T(8,128)S(1)} %get-tuple-element.49.carry, f32[8,512]{1,0:T(8,128)S(1)} %get-tuple-element.50.early), custom_call_target="tpu_custom_call" | custom-call | flops 536870912 | bytes 4194304 | tf_op jit(solution)/shard_map/close_b/pallas_call | solution.py:332
  28.6 1.2 %collective-permute-start.6 = (f32[1,512]{1,0:T(1,128)S(1)}, f32[1,512]{1,0:T(1,128)S(1)}, u32[]{:S(2)}, u32[]{:S(2)}) collective-permute-start(f32[1,512]{1,0:T(1,128)S(1)} %close_b.1), channel_id=1, source_target_pairs={{0,2},{1,3},{2,0},{3,1},{4,6},{5,7},{6,4},{7,5},{8,10},{9,11},{10,... | collective-permute-start | bytes 6152 | tf_op jit(solution)/shard_map/ppermute | solution.py:340
  29.8 1.6 %collective-permute-start.7 = (f32[1,512]{1,0:T(1,128)S(1)}, f32[1,512]{1,0:T(1,128)S(1)}, u32[]{:S(2)}, u32[]{:S(2)}) collective-permute-start(f32[1,512]{1,0:T(1,128)S(1)} %close_b.1), channel_id=1, source_target_pairs={{0,3},{1,2},{2,1},{3,0},{4,7},{5,6},{6,5},{7,4},{8,11},{9,10},{10,... | collective-permute-start | bytes 6152 | tf_op jit(solution)/shard_map/ppermute | solution.py:341
  31.4 0.0 collective-permute-start.8
  31.4 0.9 %collective-permute-done.6.b = f32[1,512]{1,0:T(1,128)S(1)} collective-permute-done((f32[1,512]{1,0:T(1,128)S(1)}, f32[1,512]{1,0:T(1,128)S(1)}, u32[]{:S(2)}, u32[]{:S(2)}) %collective-permute-start.6) | collective-permute-done | bytes 2080 | tf_op jit(solution)/shard_map/ppermute | solution.py:340
  32.3 0.5 %collective-permute-done.7.b_x = f32[1,512]{1,0:T(1,128)S(1)} collective-permute-done((f32[1,512]{1,0:T(1,128)S(1)}, f32[1,512]{1,0:T(1,128)S(1)}, u32[]{:S(2)}, u32[]{:S(2)}) %collective-permute-start.7) | collective-permute-done | bytes 2080 | tf_op jit(solution)/shard_map/ppermute | solution.py:341
  32.8 0.0 collective-permute-done.8.a_x
  32.8 0.6 %finish.1 = (f32[2,1024]{1,0:T(2,128)}, f32[2,1024]{1,0:T(2,128)}) custom-call(f32[1,512]{1,0:T(1,128)S(1)} %collective-permute-done.6.b, f32[1,512]{1,0:T(1,128)S(1)} %collective-permute-done.7.b_x, f32[1,512]{1,0:T(1,128)S(1)} %collective-permute-done.8.a_x, f32[1,512]{1,0:T(1,128)S(1)} %close_a.1.a, f32[2,1024]{1,0:T(2,128)S(1)} %get-tuple-element.52.salt_scale, ...), custom_call_target="tpu_custom_call" | custom-call | bytes 65536 | tf_op jit(solution)/shard_map/finish/pallas_call | solution.py:343
  (10 shorter events, 0.1 us)
Async XLA Ops:
  0.6 11.9 %copy-start.1 = (s32[1024]{0:T(1024)S(1)}, s32[1024]{0:T(1024)}, u32[]{:S(2)}) copy-start(s32[1024]{0:T(1024)} %param.9) | copy-start | bytes 12292
  0.6 11.9 %copy-start.6 = (bf16[1024]{0:T(1024)(128)(2,1)S(1)}, bf16[1024]{0:T(1024)(128)(2,1)}, u32[]{:S(2)}) copy-start(bf16[1024]{0:T(1024)(128)(2,1)} %param.11) | copy-start | bytes 6148
  0.7 11.9 %copy-start.2 = (s32[1024,4]{0,1:T(4,128)S(1)}, s32[1024,4]{0,1:T(4,128)}, u32[]{:S(2)}) copy-start(s32[1024,4]{0,1:T(4,128)} %param.10) | copy-start | bytes 49156
  2.0 19.3 %collective-permute-start.3 = (bf16[512,512]{1,0:T(8,128)(2,1)S(1)}, bf16[512,512]{1,0:T(8,128)(2,1)S(1)}, u32[]{:S(2)}, u32[]{:S(2)}) collective-permute-start(bf16[512,512]{1,0:T(8,128)(2,1)S(1)} %get-tuple-element.40.near), channel_id=1, source_target_pairs={{0,2},{1,3},{2,0},{3,1},{4,6},{5,7},{6,4},{7,5},{8,10},{9,11},{10,... | collective-permute-start | bytes 1572872 | tf_op jit(solution)/shard_map/ppermute | solution.py:265
  5.0 16.3 %collective-permute-start.4 = (bf16[512,512]{1,0:T(8,128)(2,1)S(1)}, bf16[512,512]{1,0:T(8,128)(2,1)S(1)}, u32[]{:S(2)}, u32[]{:S(2)}) collective-permute-start(bf16[512,512]{1,0:T(8,128)(2,1)S(1)} %get-tuple-element.39.far), channel_id=1, source_target_pairs={{0,12},{1,13},{2,6},{3,7},{4,0},{5,1},{6,10},{7,11},{8,4},{9,5},{1... | collective-permute-start | bytes 1572872 | tf_op jit(solution)/shard_map/ppermute | solution.py:266
  10.6 17.5 %collective-permute-start = (bf16[512,512]{1,0:T(8,128)(2,1)S(1)}, bf16[512,512]{1,0:T(8,128)(2,1)S(1)}, u32[]{:S(2)}, u32[]{:S(2)}) collective-permute-start(bf16[512,512]{1,0:T(8,128)(2,1)S(1)} %get-tuple-element.33), channel_id=1, source_target_pairs={{2,7},{3,6},{4,1},{5,0},{6,11},{7,10},{8,5},{9,4},{10,15},{11,14},... | collective-permute-start | bytes 1572872 | tf_op jit(solution)/shard_map/ppermute | solution.py:283
  11.9 4.3 %collective-permute-start.1 = (bf16[512,1280]{1,0:T(8,128)(2,1)S(1)}, bf16[512,1280]{1,0:T(8,128)(2,1)S(1)}, u32[]{:S(2)}, u32[]{:S(2)}) collective-permute-start(bf16[512,1280]{1,0:T(8,128)(2,1)S(1)} %get-tuple-element.34), channel_id=1, source_target_pairs={{0,1},{1,0},{2,3},{3,2},{4,5},{5,4},{6,7},{7,6},{8,9},{9,8},{10,11... | collective-permute-start | bytes 3932168 | tf_op jit(solution)/shard_map/ppermute | solution.py:277
  12.0 15.4 %collective-permute-start.2 = (bf16[512,512]{1,0:T(8,128)(2,1)S(1)}, bf16[512,512]{1,0:T(8,128)(2,1)S(1)}, u32[]{:S(2)}, u32[]{:S(2)}) collective-permute-start(bf16[512,512]{1,0:T(8,128)(2,1)S(1)} %get-tuple-element.36), channel_id=1, source_target_pairs={{0,3},{1,2},{2,1},{3,0},{4,7},{5,6},{6,5},{7,4},{8,11},{9,10},{10,... | collective-permute-start | bytes 1572872 | tf_op jit(solution)/shard_map/ppermute | solution.py:284
  15.4 0.7 %copy-start = (f32[3,2,1024]{2,1,0:T(2,128)S(1)}, f32[3,2,1024]{2,1,0:T(2,128)}, u32[]{:S(2)}) copy-start(f32[3,2,1024]{2,1,0:T(2,128)} %param.15) | copy-start | bytes 73732
  15.4 0.7 %copy-start.3 = (f32[2,1024]{1,0:T(2,128)S(1)}, f32[2,1024]{1,0:T(2,128)}, u32[]{:S(2)}) copy-start(f32[2,1024]{1,0:T(2,128)} %param.13) | copy-start | bytes 24580
  15.4 0.7 %copy-start.4 = (f32[2,1024]{1,0:T(2,128)S(1)}, f32[2,1024]{1,0:T(2,128)}, u32[]{:S(2)}) copy-start(f32[2,1024]{1,0:T(2,128)} %param.14) | copy-start | bytes 24580
  15.4 0.7 %copy-start.5 = (f32[2,1024]{1,0:T(2,128)S(1)}, f32[2,1024]{1,0:T(2,128)}, u32[]{:S(2)}) copy-start(f32[2,1024]{1,0:T(2,128)} %param.12) | copy-start | bytes 24580
  20.8 1.9 %collective-permute-start.5 = (f32[4,512]{1,0:T(4,128)S(1)}, f32[4,512]{1,0:T(4,128)S(1)}, u32[]{:S(2)}, u32[]{:S(2)}) collective-permute-start(f32[4,512]{1,0:T(4,128)S(1)} %plane.1), channel_id=1, source_target_pairs={{0,1},{1,0},{2,3},{3,2},{4,5},{5,4},{6,7},{7,6},{8,9},{9,8},{10,11... | collective-permute-start | bytes 24584 | tf_op jit(solution)/shard_map/ppermute | solution.py:311
  28.6 3.7 %collective-permute-start.6 = (f32[1,512]{1,0:T(1,128)S(1)}, f32[1,512]{1,0:T(1,128)S(1)}, u32[]{:S(2)}, u32[]{:S(2)}) collective-permute-start(f32[1,512]{1,0:T(1,128)S(1)} %close_b.1), channel_id=1, source_target_pairs={{0,2},{1,3},{2,0},{3,1},{4,6},{5,7},{6,4},{7,5},{8,10},{9,11},{10,... | collective-permute-start | bytes 6152 | tf_op jit(solution)/shard_map/ppermute | solution.py:340
  29.8 3.0 %collective-permute-start.7 = (f32[1,512]{1,0:T(1,128)S(1)}, f32[1,512]{1,0:T(1,128)S(1)}, u32[]{:S(2)}, u32[]{:S(2)}) collective-permute-start(f32[1,512]{1,0:T(1,128)S(1)} %close_b.1), channel_id=1, source_target_pairs={{0,3},{1,2},{2,1},{3,0},{4,7},{5,6},{6,5},{7,4},{8,11},{9,10},{10,... | collective-permute-start | bytes 6152 | tf_op jit(solution)/shard_map/ppermute | solution.py:341
  31.4 1.5 %collective-permute-start.8 = (f32[1,512]{1,0:T(1,128)S(1)}, f32[1,512]{1,0:T(1,128)S(1)}, u32[]{:S(2)}, u32[]{:S(2)}) collective-permute-start(f32[1,512]{1,0:T(1,128)S(1)} %close_a.1.a), channel_id=1, source_target_pairs={{0,1},{1,0},{2,3},{3,2},{4,5},{5,4},{6,7},{7,6},{8,9},{9,8},{10,11... | collective-permute-start | bytes 6152 | tf_op jit(solution)/shard_map/ppermute | solution.py:337
